TPU v7x, 128 devices: a whole 4x4x4 slice. The times are simulated.
128 devices in a mesh: seq: 16 (over y_hi, z, core), tp: 8 (over x, y_lo).
Axes of the slice: x: 4, y: 4 (y_hi: 2, y_lo: 2; y = y_hi * 2 + y_lo), z: 4, core: 2. Of those that a mesh axis runs over, the one named last changes fastest.
Arguments:
- cond_hidden: bfloat16 [2048, 10240], P('seq', 'tp'), may hold values from -6 to 6
- cond_down: bfloat16 [10240, 3584], P('tp'), may hold values from -0.0625 to 0.0625
- cond_resid: bfloat16 [2048, 3584], P('seq', 'tp'), may hold values from -6 to 6
- cond_gain: float32 [3584], replicated, may hold values from 0.25 to 1.75
- text_proj: bfloat16 [3584, 3072], P(None, 'tp'), may hold values from -0.09375 to 0.09375
- image_states: bfloat16 [8192, 3072], P('seq', 'tp'), may hold values from -6 to 6
- image_mod: float32 [4, 3072], replicated, may hold values from -6 to 6
- text_mod: float32 [4, 3072], replicated, may hold values from -6 to 6
- query_gain: float32 [128], replicated, may hold values from 1 to 2.2
- key_gain: float32 [128], replicated, may hold values from 1 to 2.2
- image_qkv: bfloat16 [3072, 3, 3072], P('seq', None, 'tp'), may hold values from -0.109375 to 0.109375
- text_qkv: bfloat16 [3072, 3, 3072], P('seq', None, 'tp'), may hold values from -0.109375 to 0.109375
- image_out: bfloat16 [3072, 3072], P('tp', 'seq'), may hold values from -0.109375 to 0.109375
- text_out: bfloat16 [3072, 3072], P('tp', 'seq'), may hold values from -0.109375 to 0.109375
- cond_pos: int32 [2048], P('seq'), may hold values from 0 to 16383
- image_cache: bfloat16 [8192, 3072], P('seq', 'tp'), may hold values from -6 to 6
- text_cache: bfloat16 [2048, 3072], P('seq', 'tp'), may hold values from -6 to 6
Outputs:
- image_next: bfloat16 [8192, 3072], P('seq', 'tp')
- text_next: bfloat16 [2048, 3072], P('seq', 'tp')
All inputs are finite; a program needn't handle non-finite values.
Results may differ from a plain program's by a relative error of at most 0.035.
Values may be sent and summed in bfloat16 or wider, within the bound.
No kernel may reach another device: no remote copies, remote signals or barrier semaphores. Data moves between devices by JAX's collectives and lax.ppermute only.
A program may use at most 256 MiB of HBM per device.

v0:
```python
import functools
import math

import jax
import jax.numpy as jnp
from jax import lax
from jax.experimental import pallas as pl
from jax.experimental.pallas import tpu as pltpu
from jax.sharding import Mesh, PartitionSpec as P

EPS = 1e-06
HD = 128
AXES = ("yh", "z", "c", "x", "yl")
SEQ = ("yh", "z", "c")
TP = ("x", "yl")
BF = jnp.bfloat16
F32 = jnp.float32


def shift(value, axis, step):
    size = lax.axis_size(axis)
    return lax.ppermute(value, axis, [(k, (k + step) % size) for k in range(size)])


def near(value, axis):
    return shift(value, axis, 1), shift(value, axis, -1)


def spread(value, axes):
    count = lax.axis_size(axes)
    copies = jnp.broadcast_to(value[None], (count,) + value.shape)
    return lax.all_to_all(copies, axes, split_axis=0, concat_axis=0, tiled=True)


def table(places):
    return jnp.stack([jnp.asarray(p, jnp.int32) for p in places])


def params(mib=48):
    return pltpu.CompilerParams(vmem_limit_bytes=mib * 1024 * 1024)


ANY = pl.BlockSpec(memory_space=pl.ANY)
VMEM = pl.BlockSpec(memory_space=pltpu.VMEM)
SMEM = pl.BlockSpec(memory_space=pltpu.SMEM)


def text_kernel(state_ref, gain_ref, proj_ref, out_ref):
    parts, rows, share = state_ref.shape
    square = jnp.zeros((rows, 1), F32)
    for t in range(parts):
        block = state_ref[t].astype(F32)
        square += jnp.sum(block * block, axis=-1, keepdims=True)
    factor = lax.rsqrt(square / (parts * share) + EPS)
    total = jnp.zeros(out_ref.shape, F32)
    for t in range(parts):
        normed = (state_ref[t].astype(F32) * factor * gain_ref[t]).astype(BF)
        total += jnp.dot(normed, proj_ref[t], preferred_element_type=F32)
    out_ref[...] = total.astype(BF)


def text_projection(state, gain, proj):
    parts, rows, share = state.shape
    return pl.pallas_call(
        text_kernel,
        out_shape=jax.ShapeDtypeStruct((rows, proj.shape[1]), BF),
        in_specs=[VMEM] * 3,
        out_specs=VMEM,
        compiler_params=params(),
        name="text_projection",
    )(state, gain.reshape(parts, 1, share), proj.reshape(parts, share, proj.shape[1]))


def qkv_kernel(a_index, count, place_ref, mod_ref, cos_ref, sin_ref, gain_ref, text_ref, *refs):
    arrays = a_index[-1][0] + 1
    a_arrays, w_pieces, refs = refs[:arrays], refs[arrays : arrays + count], refs[arrays + count :]
    q_ref, kv_ref, states, modded, weight, sems = refs
    parts, rows, share = states.shape
    width = parts * share
    depth = width // 16
    image_rows = rows // 5 * 4
    a_copies, w_copies = [], ([], [])
    for i, (array, index) in enumerate(a_index):
        dst = states.at[place_ref[i], pl.ds(0, image_rows)]
        a_copies.append(pltpu.make_async_copy(a_arrays[array].at[index], dst, sems.at[i]))
    dst = states.at[:, pl.ds(image_rows, rows - image_rows)]
    a_copies.append(pltpu.make_async_copy(text_ref, dst, sems.at[8]))
    for stream in range(2):
        for i, piece in enumerate(w_pieces):
            start = pl.multiple_of(place_ref[8 + i] * depth, depth)
            src = piece.at[pl.ds(3 * stream, 3)]
            dst = weight.at[pl.ds(3 * stream, 3), pl.ds(start, depth), :]
            sem = sems.at[9 + count * stream + i]
            w_copies[stream].append(pltpu.make_async_copy(src, dst, sem))
    for copy in a_copies + w_copies[0] + w_copies[1]:
        copy.start()
    for copy in a_copies:
        copy.wait()

    tile = 64

    def modulate(first, last, stream):
        @pl.loop(first // tile, last // tile)
        def _(step):
            here = pl.ds(pl.multiple_of(step * tile, tile), tile)
            total = jnp.zeros((tile, share), F32)
            for t in range(parts):
                total += states[t, here, :].astype(F32)
            center = jnp.sum(total, axis=-1, keepdims=True) / width
            total = jnp.zeros((tile, share), F32)
            for t in range(parts):
                shifted = states[t, here, :].astype(F32) - center
                total += shifted * shifted
            factor = lax.rsqrt(jnp.sum(total, axis=-1, keepdims=True) / width + EPS)
            for t in range(parts):
                cols = slice(t * share, (t + 1) * share)
                shifted = states[t, here, :].astype(F32) - center
                gain = 1.0 + mod_ref[stream, 1:2, cols]
                normed = shifted * factor * gain + mod_ref[stream, 0:1, cols]
                modded[here, cols] = normed.astype(BF)

    def prepare(flat, gain, cosine, sine):
        outs = []
        for h in range(share // HD):
            head = flat[:, h * HD : (h + 1) * HD]
            meansq = jnp.mean(head * head, axis=-1, keepdims=True)
            normed = head * lax.rsqrt(meansq + EPS) * gain
            outs.append(normed * cosine + pltpu.roll(normed, HD // 2, 1) * sine)
        return jnp.concatenate(outs, axis=1)

    def project(here, stream):
        def product(j):
            return jnp.dot(modded[here, :], weight[3 * stream + j], preferred_element_type=F32)

        cosine, sine = cos_ref[here, :], sin_ref[here, :]
        q = prepare(product(0), gain_ref[0:1, :], cosine, sine)
        q_ref[here, :] = (q * (math.log2(math.e) / math.sqrt(HD))).astype(BF)
        kv_ref[0, here, :] = prepare(product(1), gain_ref[1:2, :], cosine, sine).astype(BF)
        kv_ref[1, here, :] = product(2).astype(BF)

    modulate(0, image_rows, 0)
    modulate(image_rows, rows, 1)
    for copy in w_copies[0]:
        copy.wait()
    chunk = image_rows // 2

    @pl.loop(0, 2)
    def _(step):
        project(pl.ds(pl.multiple_of(step * chunk, chunk), chunk), 0)

    for copy in w_copies[1]:
        copy.wait()
    project(pl.ds(image_rows, rows - image_rows), 1)


def qkv(a_arrays, a_index, a_places, text_a, w_pieces, w_places, mods, cosine, sine, gains):
    parts, text_rows, share = text_a.shape
    rows = a_arrays[0].shape[-2] + text_rows
    width = parts * share
    arrays, count = len(a_arrays), len(w_pieces)
    return pl.pallas_call(
        functools.partial(qkv_kernel, a_index, count),
        out_shape=(
            jax.ShapeDtypeStruct((rows, share), BF),
            jax.ShapeDtypeStruct((2, rows, share), BF),
        ),
        in_specs=[SMEM, VMEM, VMEM, VMEM, VMEM] + [ANY] * (1 + arrays + count),
        out_specs=(VMEM, VMEM),
        scratch_shapes=[
            pltpu.VMEM((parts, rows, share), BF),
            pltpu.VMEM((rows, width), BF),
            pltpu.VMEM((6, width, share), BF),
            pltpu.SemaphoreType.DMA((9 + 2 * count,)),
        ],
        compiler_params=params(),
        name="qkv",
    )(table(a_places + w_places), mods, cosine, sine, gains, text_a, *a_arrays, *w_pieces)


def attention_kernel(nq, k_sizes, first, *refs):
    nk = len(k_sizes)
    q_refs, refs = refs[:nq], refs[nq:]
    k_refs, v_refs, refs = refs[:nk], refs[nk : 2 * nk], refs[2 * nk :]
    before, refs = ([], refs) if first else (refs[: 2 * nq], refs[2 * nq :])
    out_refs, tot_refs = refs[:nq], refs[nq : 2 * nq]
    keys, values = refs[2 * nq :]
    head = pl.program_id(0)
    at = 0
    for k_ref, v_ref, size in zip(k_refs, v_refs, k_sizes):
        keys[at : at + size, :] = k_ref[0]
        values[at : at + size, 0:HD] = v_ref[0]
        at += size

    @pl.when(head == 0)
    def _():
        values[:, HD:] = jnp.ones((values.shape[0], HD), BF)
        for i in range(nq):
            tot_refs[i][...] = jnp.zeros(tot_refs[i].shape, F32) if first else before[nq + i][...]

    rows = q_refs[0].shape[0]
    lane = lax.broadcasted_iota(jnp.int32, (rows, HD), 1)
    block = 256
    for i in range(nq):
        q = q_refs[i][...]
        total = jnp.zeros((rows, 2 * HD), F32)
        for start in range(0, keys.shape[0], block):
            stop = min(start + block, keys.shape[0])
            scores = lax.dot_general(
                q, keys[start:stop, :], (((1,), (1,)), ((), ())), preferred_element_type=F32
            )
            probs = jnp.exp2(scores).astype(BF)
            total += jnp.dot(probs, values[start:stop, :], preferred_element_type=F32)
        num = total[:, :HD]
        out_refs[i][...] = num if first else before[i][...] + num
        tot_refs[i][...] += jnp.where(lane == head, total[:, HD:], 0.0)


def attention(queries, kvs, before=()):
    rows, width = queries[0].shape
    keys = [(kv[0].reshape(-1, rows, width), 0) for kv in kvs]
    values = [(kv[-1].reshape(-1, rows, width), 2 - len(kv)) for kv in kvs]
    k_sizes = (rows,) * len(kvs)
    nq = len(queries)
    by_head = pl.BlockSpec((rows, HD), lambda h: (0, h))
    fixed = pl.BlockSpec((rows, HD), lambda h: (0, 0))
    sums = [by_head] * nq + [fixed] * nq
    inputs = nq + 2 * len(kvs)
    work = nq * rows * len(kvs) * rows * width
    return pl.pallas_call(
        functools.partial(attention_kernel, nq, k_sizes, not before),
        grid=(width // HD,),
        out_shape=[jax.ShapeDtypeStruct((rows, width), F32)] * nq
        + [jax.ShapeDtypeStruct((rows, HD), F32)] * nq,
        in_specs=[by_head] * nq
        + [
            pl.BlockSpec((1, rows, HD), functools.partial(lambda i, h: (i, 0, h), i))
            for _, i in keys + values
        ]
        + (sums if before else []),
        out_specs=sums,
        input_output_aliases={inputs + i: i for i in range(2 * nq)} if before else {},
        scratch_shapes=[
            pltpu.VMEM((sum(k_sizes), HD), BF),
            pltpu.VMEM((sum(k_sizes), 2 * HD), BF),
        ],
        compiler_params=params(),
        cost_estimate=pl.CostEstimate(
            flops=8 * work, bytes_accessed=8 * nq * rows * width, transcendentals=work // HD
        ),
        name="attention",
    )(*queries, *[k for k, _ in keys + values], *before)


def combine_kernel(num_ref, other_ref, back_ref, tot_ref, other_tot_ref, out_ref):
    share = num_ref.shape[1]
    for h in range(share // HD):
        cols = slice(h * HD, (h + 1) * HD)
        lane, low = slice(share + h, share + h + 1), slice(share + 64 + h, share + 65 + h)
        num = num_ref[:, cols] + other_ref[:, cols] + back_ref[:, cols].astype(F32)
        tot = tot_ref[:, h : h + 1] + other_tot_ref[:, h : h + 1]
        tot += back_ref[:, lane].astype(F32) + back_ref[:, low].astype(F32)
        out_ref[:, cols] = (num / tot).astype(BF)


def combine(num, other, back, tot, other_tot):
    return pl.pallas_call(
        combine_kernel,
        out_shape=jax.ShapeDtypeStruct(num.shape, BF),
        in_specs=[VMEM] * 5,
        out_specs=VMEM,
        compiler_params=params(),
        name="combine",
    )(num, other, back, tot, other_tot)


def out_kernel(place_ref, own_ref, other_ref, weight_ref, out_ref, attended):
    rows, share = own_ref.shape
    image_rows = rows // 5 * 4

    @pl.when(pl.program_id(0) == 0)
    def _():
        first = place_ref[0] == 0
        attended[:, :share] = jnp.where(first, own_ref[...], other_ref[...])
        attended[:, share:] = jnp.where(first, other_ref[...], own_ref[...])

    for stream, here in ((0, slice(0, image_rows)), (1, slice(image_rows, rows))):
        halves = [weight_ref[2 * y : 2 * y + 2, stream].reshape(share, share) for y in range(2)]
        out_ref[0, here, :] = lax.dot_general(
            attended[here, :],
            jnp.concatenate(halves, axis=1),
            (((1,), (1,)), ((), ())),
            preferred_element_type=F32,
        ).astype(BF)


def out_projection(own, other, weight, yl):
    rows, share = own.shape
    whole = pl.BlockSpec((rows, share), lambda x: (0, 0))
    return pl.pallas_call(
        out_kernel,
        grid=(4,),
        out_shape=jax.ShapeDtypeStruct((4, rows, share), BF),
        in_specs=[SMEM, whole, whole]
        + [pl.BlockSpec((4,) + weight.shape[1:], lambda x: (x, 0, 0, 0))],
        out_specs=pl.BlockSpec((1, rows, share), lambda x: (x, 0, 0)),
        scratch_shapes=[pltpu.VMEM((rows, 2 * share), BF)],
        compiler_params=params(),
        name="out_projection",
    )(table([yl]), own, other, weight)


def angles_of(positions):
    freqs = 10000.0 ** (-(jnp.arange(HD // 2, dtype=F32) * 2.0) / HD)
    angles = positions[:, None] * freqs[None, :]
    cosine, sine = jnp.cos(angles), jnp.sin(angles)
    return jnp.concatenate([cosine, cosine], axis=1), jnp.concatenate([-sine, sine], axis=1)


def shards(
    cond_hidden,
    cond_down,
    cond_resid,
    cond_gain,
    text_proj,
    image_states,
    image_mod,
    text_mod,
    query_gain,
    key_gain,
    image_qkv,
    text_qkv,
    image_out,
    text_out,
    cond_pos,
    image_cache,
    text_cache,
):
    seq_index = lax.axis_index(SEQ)
    tp_index = lax.axis_index(TP)
    image_rows, share = image_states.shape
    text_rows = cond_hidden.shape[0]

    yh, z, c, x, yl = (lax.axis_index(a) for a in AXES)
    together = lax.optimization_barrier
    outs = jnp.stack([jnp.transpose(image_out), jnp.transpose(text_out)])
    weight = jnp.transpose(jnp.concatenate([image_qkv, text_qkv], axis=1), (1, 0, 2))

    turned = [
        (4 * zh + 2 * zl + y, 4 * zh + 2 * y + zl)
        for zh in range(2)
        for zl in range(2)
        for y in range(2)
    ]
    outs = lax.ppermute(outs, ("z", "yl"), turned)
    w_near = near(weight, "z")
    w_pair = shift(weight, "yh", 1)
    a_own = jnp.stack([image_states, shift(image_states, "yl", 1)])
    cond_hidden, a_own, outs = together((cond_hidden, a_own, outs))

    a_near = near(a_own, "x")
    out_w = lax.all_gather(outs, SEQ)
    partial_value = jnp.dot(cond_hidden, cond_down, preferred_element_type=F32).astype(BF)
    enc_share = cond_down.shape[1] // 8
    sent = jnp.transpose(partial_value.reshape(text_rows, 8, enc_share), (1, 0, 2))
    got = lax.all_to_all(sent, TP, split_axis=0, concat_axis=0, tiled=True)

    got, w_near, w_pair = together((got, w_near, w_pair))
    w_next = near(w_pair, "z")
    cond_state = (jnp.sum(got.astype(F32), axis=0) + cond_resid.astype(F32)).astype(BF)
    state = spread(cond_state, TP)
    state, a_near, w_near, w_next = together((state, a_near, w_near, w_next))

    text_states = text_projection(state, cond_gain, text_proj)
    text_a = spread(text_states, TP)
    a_far = (shift(a_near[0][0], "x", 1), shift(a_near[1][1], "x", -1))
    w_far = (shift(w_near[0], "z", 1), shift(w_next[1], "z", -1))
    text_a, a_far, w_far = together((text_a, a_far, w_far))

    a_arrays = [a_own, *a_near, *a_far]
    a_index = tuple((i, (p,)) for i in range(3) for p in range(2)) + ((3, ()), (4, ()))
    a_places = [
        (x + d) % 4 * 2 + (yl + p) % 2 for d, p in [(d, p) for d in (0, 3, 1, 2) for p in range(2)]
    ]
    w_arrays = [weight, *w_near, w_far[0], w_pair, *w_next, w_far[1]]
    w_arrays += [shift(w, "c", 1) for w in w_arrays]
    blocks = [(p, d) for p in range(2) for d in (0, 3, 1, 2)]

    gains = jnp.stack([query_gain, key_gain])
    image_pos = (seq_index * image_rows + jnp.arange(image_rows)).astype(F32)
    w_places = [
        (yh + p) % 2 * 8 + (z + d) % 4 * 2 + (c + k) % 2 for k in range(2) for p, d in blocks
    ]
    query, kv = qkv(
        a_arrays,
        a_index,
        a_places,
        text_a,
        w_arrays,
        w_places,
        jnp.stack([image_mod, text_mod]),
        *angles_of(jnp.concatenate([image_pos, cond_pos.astype(F32)])),
        gains,
    )
    pair_query = shift(query, "yh", 1)
    kv_left, kv_right = near(kv, "z")
    core_query = shift(query, "c", 1)
    own_queries = [query, core_query]
    own = attention(own_queries, [(kv,)])
    pair_query, own = together((pair_query, own))
    pair_queries = [pair_query, shift(pair_query, "c", 1)]
    pair = attention(pair_queries, [(kv,)])
    pair, kv_left, kv_right = together((pair, kv_left, kv_right))
    kv_far = (shift(kv_left[0], "z", 1), shift(kv_right[1], "z", -1))
    pair = attention(pair_queries, [(kv_left,), (kv_right,)], pair)
    pair, kv_far = together((pair, kv_far))
    pair = attention(pair_queries, [kv_far], pair)

    sent_num = pair[0] + shift(pair[1], "c", 1)
    sent_tot = pair[2] + shift(pair[3], "c", 1)
    high = sent_tot.astype(BF)
    low = (sent_tot - high.astype(F32)).astype(BF)
    mixed = jnp.concatenate([sent_num.astype(BF), high[:, :64], low[:, :64]], axis=1)
    mixed, own = together((mixed, own))
    back = shift(mixed, "yh", 1)
    own = attention(own_queries, [(kv_left,), (kv_right,), kv_far], own)
    back, own = together((back, own))
    attended = combine(own[0], shift(own[1], "c", 1), back, own[2], shift(own[3], "c", 1))

    parts = out_projection(attended, shift(attended, "yl", 1), out_w, yl)
    got = lax.all_to_all(parts, "x", split_axis=0, concat_axis=0, tiled=True)
    branch = jnp.sum(got.astype(F32), axis=0)

    def finish(states, mod, rows, cache):
        gates = lax.dynamic_slice_in_dim(mod, tp_index * share, share, 1)
        return (
            states.astype(F32) + gates[2] * branch[rows] + gates[3] * cache.astype(F32)
        ).astype(BF)

    return (
        finish(image_states, image_mod, slice(0, image_rows), image_cache),
        finish(text_states, text_mod, slice(image_rows, None), text_cache),
    )


def solution(mesh):
    fine = Mesh(mesh.devices.reshape(2, 4, 2, 4, 2), AXES)
    return jax.shard_map(
        shards,
        mesh=fine,
        in_specs=(
            P(SEQ, TP),
            P(TP, None),
            P(SEQ, TP),
            P(),
            P(None, TP),
            P(SEQ, TP),
            P(),
            P(),
            P(),
            P(),
            P(SEQ, None, TP),
            P(SEQ, None, TP),
            P(TP, SEQ),
            P(TP, SEQ),
            P(SEQ),
            P(SEQ, TP),
            P(SEQ, TP),
        ),
        out_specs=(P(SEQ, TP), P(SEQ, TP)),
        check_vma=False,
    )
```

profile of v0, /device:TPU:0, one launch (start us, length us, event | category | flops | bytes accessed | tf_op | source)
XLA Modules:
  0.0 276.9 jit_solution(9449274811390017460)
XLA Ops:
  7.2 1.7 collective-permute-start
  8.9 1.0 pad_maximum_fusion.4
  10.0 0.7 collective-permute-start.1
  10.6 1.3 maximum_bitcast_fusion.refs_5_
  11.9 3.2 %collective-permute-start.2 = (bf16[6,192,384]{2,1,0:T(8,128)(2,1)S(1)}, bf16[6,192,384]{2,1,0:T(8,128)(2,1)}, u32[]{:S(2)}, u32[]{:S(2)}) collective-permute-start(bf16[6,192,384]{2,1,0:T(8,128)(2,1)S(1)} %maximum_bitcast_fusion.refs_5_), channel_id=1, source_target_pairs={{0,16},{16,32},{32,48},{48,0},{1,17},{17,33},{33,49},{49,1},{2,18}... | collective-permute-start | bytes 2654216 | tf_op jit(solution)/shard_map/ppermute | solution.py:22
  15.1 2.5 collective-permute-start.3
  17.6 3.2 %collective-permute-start.4 = (bf16[6,192,384]{2,1,0:T(8,128)(2,1)S(1)}, bf16[6,192,384]{2,1,0:T(8,128)(2,1)}, u32[]{:S(2)}, u32[]{:S(2)}) collective-permute-start(bf16[6,192,384]{2,1,0:T(8,128)(2,1)S(1)} %maximum_bitcast_fusion.refs_5_), channel_id=1, source_target_pairs={{0,64},{64,0},{1,65},{65,1},{2,66},{66,2},{3,67},{67,3},{4,68},{68... | collective-permute-start | bytes 2654216 | tf_op jit(solution)/shard_map/ppermute | solution.py:22
  20.9 6.0 %convolution_convert_fusion = bf16[128,3584]{1,0:T(8,128)(2,1)} fusion(bf16[128,1280]{1,0:T(8,128)(2,1)S(1)} %copy-done, bf16[1280,3584]{1,0:T(8,128)(2,1)} %param.18), kind=kOutput, calls=%fused_computation | convolution fusion | flops 1174863872 | bytes 10420224 | tf_op jit(solution)/shard_map/dot_general | solution.py:362
  27.0 2.3 copy.34
  29.2 11.7 %all-to-all-start = ((bf16[8,128,448]{1,2,0:T(8,128)(2,1)}), bf16[8,128,448]{1,2,0:T(8,128)(2,1)S(1)}, u32[]{:S(2)}, u32[]{:S(2)}) async-start(bf16[8,128,448]{1,2,0:T(8,128)(2,1)} %bitcast.36), calls=%async_computation | async-start | bytes 1835008 | tf_op jit(solution)/shard_map/all_to_all | solution.py:365
  40.9 12.5 %all-to-all-done = bf16[8,128,448]{1,2,0:T(8,128)(2,1)S(1)} async-done(((bf16[8,128,448]{1,2,0:T(8,128)(2,1)}), bf16[8,128,448]{1,2,0:T(8,128)(2,1)S(1)}, u32[]{:S(2)}, u32[]{:S(2)}) %all-to-all-start) | async-done | bytes 917536 | tf_op jit(solution)/shard_map/all_to_all | solution.py:365
  53.4 3.3 %collective-permute-start.7 = (bf16[6,192,384]{2,1,0:T(8,128)(2,1)}, bf16[6,192,384]{2,1,0:T(8,128)(2,1)}, u32[]{:S(2)}, u32[]{:S(2)}) collective-permute-start(bf16[6,192,384]{2,1,0:T(8,128)(2,1)} %collective-permute-done.4.refs_9_), channel_id=1, source_target_pairs={{0,16},{16,32},{32,48},{48,0},{1,17},{17,33},{33,49},{49,1},{2,18}... | collective-permute-start | bytes 2654216 | tf_op jit(solution)/shard_map/ppermute | solution.py:22
  56.7 2.1 collective-permute-start.8
  59.0 1.1 broadcast_in_dim.4
  60.1 4.4 %all-to-all-start.1 = ((bf16[8,128,448]{1,2,0:T(8,128)(2,1)}), bf16[8,128,448]{1,2,0:T(8,128)(2,1)}, u32[]{:S(2)}, u32[]{:S(2)}) async-start(bf16[8,128,448]{1,2,0:T(8,128)(2,1)} %broadcast_in_dim.4), calls=%async_computation.1 | async-start | bytes 1835008 | tf_op jit(solution)/shard_map/all_to_all | solution.py:32
  64.6 2.0 collective-permute-start.5
  66.6 1.3 collective-permute-start.6
  67.9 25.5 %collective-permute-done.5.refs_1_ = bf16[2,512,384]{2,1,0:T(8,128)(2,1)S(1)} collective-permute-done((bf16[2,512,384]{2,1,0:T(8,128)(2,1)S(1)}, bf16[2,512,384]{2,1,0:T(8,128)(2,1)S(1)}, u32[]{:S(2)}, u32[]{:S(2)}) %collective-permute-start.5) | collective-permute-done | bytes 786464 | tf_op jit(solution)/shard_map/ppermute | solution.py:22
  93.5 1.2 collective-permute-start.10
  94.8 0.9 collective-permute-start.9
  95.7 3.2 %collective-permute-start.12 = (bf16[6,192,384]{2,1,0:T(8,128)(2,1)}, bf16[6,192,384]{2,1,0:T(8,128)(2,1)}, u32[]{:S(2)}, u32[]{:S(2)}) collective-permute-start(bf16[6,192,384]{2,1,0:T(8,128)(2,1)} %collective-permute-done.8.refs_11_), channel_id=1, source_target_pairs={{0,48},{16,0},{32,16},{48,32},{1,49},{17,1},{33,17},{49,33},{2,50}... | collective-permute-start | bytes 2654216 | tf_op jit(solution)/shard_map/ppermute | solution.py:22
  99.0 3.0 %collective-permute-done.10.refs_4_ = bf16[512,384]{1,0:T(8,128)(2,1)S(1)} collective-permute-done((bf16[512,384]{1,0:T(8,128)(2,1)S(1)}, bf16[512,384]{1,0:T(8,128)(2,1)S(1)}, u32[]{:S(2)}, u32[]{:S(2)}) %collective-permute-start.10) | collective-permute-done | bytes 393248 | tf_op jit(solution)/shard_map/ppermute | solution.py:22
  101.9 0.7 copy-done.7
  102.7 1.7 collective-permute-done.9.refs_3_
  104.4 0.7 copy-done.9
  105.3 1.5 copy.35.state_ref
  106.8 1.8 copy-done.2
  108.5 1.0 text_projection.1
  109.5 0.6 copy-done.5
  110.2 1.0 broadcast_in_dim.5
  111.1 4.0 %all-to-all-start.2 = ((bf16[8,128,384]{2,1,0:T(8,128)(2,1)}), bf16[8,128,384]{2,1,0:T(8,128)(2,1)S(1)}, u32[]{:S(2)}, u32[]{:S(2)}) async-start(bf16[8,128,384]{2,1,0:T(8,128)(2,1)} %broadcast_in_dim.5), calls=%async_computation.2 | async-start | bytes 1572864 | tf_op jit(solution)/shard_map/all_to_all | solution.py:32
  115.2 8.0 %collective-permute-done.11.refs_8_ = bf16[6,192,384]{2,1,0:T(8,128)(2,1)} collective-permute-done((bf16[6,192,384]{2,1,0:T(8,128)(2,1)}, bf16[6,192,384]{2,1,0:T(8,128)(2,1)}, u32[]{:S(2)}, u32[]{:S(2)}) %collective-permute-start.11) | collective-permute-done | bytes 884768 | tf_op jit(solution)/shard_map/ppermute | solution.py:22
  123.2 1.1 collective-permute-done.12.refs_12_
  124.3 3.9 %all-to-all-done.2.text_ref = bf16[8,128,384]{2,1,0:T(8,128)(2,1)S(1)} async-done(((bf16[8,128,384]{2,1,0:T(8,128)(2,1)}), bf16[8,128,384]{2,1,0:T(8,128)(2,1)S(1)}, u32[]{:S(2)}, u32[]{:S(2)}) %all-to-all-start.2) | async-done | bytes 786464 | tf_op jit(solution)/shard_map/all_to_all | solution.py:32
  129.2 1.2 fusion.7
  131.0 1.3 collective-permute-done.16.refs_16_
  132.2 1.3 collective-permute-done.20.refs_20_
  133.5 14.2 %qkv.1 = (bf16[640,384]{1,0:T(8,128)(2,1)S(1)}, bf16[2,640,384]{2,1,0:T(8,128)(2,1)}) custom-call(s32[24]{0:T(128)S(1)} %stack.139.place_ref, f32[2,4,3072]{2,1,0:T(4,128)S(1)} %pad_maximum_fusion.5.mod_ref, f32[640,128]{1,0:T(8,128)S(1)} %get-tuple-element.147.cos_ref, f32[640,128]{1,0:T(8,128)S(1)} %get-tuple-element.148.sin_ref, ...), custom_call_target="tpu_custom_call" | custom-call | tf_op jit(solution)/shard_map/qkv/pallas_call | solution.py:161
  147.9 3.3 %collective-permute-start.21 = (bf16[640,384]{1,0:T(8,128)(2,1)S(1)}, bf16[640,384]{1,0:T(8,128)(2,1)S(1)}, u32[]{:S(2)}, u32[]{:S(2)}) collective-permute-start(bf16[640,384]{1,0:T(8,128)(2,1)S(1)} %get-tuple-element.88.refs_0_), channel_id=1, source_target_pairs={{0,64},{64,0},{1,65},{65,1},{2,66},{66,2},{3,67},{67,3},{4,68},{68... | collective-permute-start | bytes 1474568 | tf_op jit(solution)/shard_map/ppermute | solution.py:22
  151.3 3.2 %collective-permute-start.25 = (bf16[2,640,384]{2,1,0:T(8,128)(2,1)}, bf16[2,640,384]{2,1,0:T(8,128)(2,1)S(1)}, u32[]{:S(2)}, u32[]{:S(2)}) collective-permute-start(bf16[2,640,384]{2,1,0:T(8,128)(2,1)} %get-tuple-element.89.refs_2_.refs_3_), channel_id=1, source_target_pairs={{0,48},{16,0},{32,16},{48,32},{1,49},{17,1},{33,17},{49,33},{2,50}... | collective-permute-start | bytes 2949128 | tf_op jit(solution)/shard_map/ppermute | solution.py:22
  154.5 1.2 copy-done.12
  155.7 4.7 %attention.5 = (f32[640,384]{1,0:T(8,128)S(1)}, f32[640,384]{1,0:T(8,128)S(1)}, f32[640,128]{1,0:T(8,128)S(1)}, f32[640,128]{1,0:T(8,128)S(1)}) custom-call(bf16[640,384]{1,0:T(8,128)(2,1)S(1)} %get-tuple-element.88.refs_0_, bf16[640,384]{1,0:T(8,128)(2,1)S(1)} %collective-permute-done.22.refs_1_, bf16[2,640,384]{2,1,0:T(8,128)(2,1)S(1)} %copy-done.12, ...), custom_call_target="tpu_custom_call" | custom-call | flops 2516582400 | bytes 3932160 | tf_op jit(solution)/shard_map/attention/pallas_call | solution.py:229
  160.4 2.6 collective-permute-done.21.refs_0_
  163.1 1.9 collective-permute-done.23.refs_1_
  164.9 4.7 %attention.6 = (f32[640,384]{1,0:T(8,128)S(1)}, f32[640,384]{1,0:T(8,128)S(1)}, f32[640,128]{1,0:T(8,128)S(1)}, f32[640,128]{1,0:T(8,128)S(1)}) custom-call(bf16[640,384]{1,0:T(8,128)(2,1)S(1)} %collective-permute-done.21.refs_0_, bf16[640,384]{1,0:T(8,128)(2,1)S(1)} %collective-permute-done.23.refs_1_, bf16[2,640,384]{2,1,0:T(8,128)(2,1)S(1)} %copy-done.13, ...), custom_call_target="tpu_custom_call" | custom-call | flops 2516582400 | bytes 3932160 | tf_op jit(solution)/shard_map/attention/pallas_call | solution.py:229
  169.6 6.9 %collective-permute-done.24.refs_2_.refs_4_.refs_5_ = bf16[2,640,384]{2,1,0:T(8,128)(2,1)S(1)} collective-permute-done((bf16[2,640,384]{2,1,0:T(8,128)(2,1)}, bf16[2,640,384]{2,1,0:T(8,128)(2,1)S(1)}, u32[]{:S(2)}, u32[]{:S(2)}) %collective-permute-start.24) | collective-permute-done | bytes 983072 | tf_op jit(solution)/shard_map/ppermute | solution.py:22
  176.7 3.5 %collective-permute-start.27 = (bf16[640,384]{1,0:T(8,128)(2,1)S(1)}, bf16[640,384]{1,0:T(8,128)(2,1)S(1)}, u32[]{:S(2)}, u32[]{:S(2)}) collective-permute-start(bf16[640,384]{1,0:T(8,128)(2,1)S(1)} %slice_bitcast_fusion), channel_id=1, source_target_pairs={{0,48},{16,0},{32,16},{48,32},{1,49},{17,1},{33,17},{49,33},{2,50}... | collective-permute-start | bytes 1474568 | tf_op jit(solution)/shard_map/ppermute | solution.py:22
  180.2 7.7 %attention.7 = (f32[640,384]{1,0:T(8,128)S(1)}, f32[640,384]{1,0:T(8,128)S(1)}, f32[640,128]{1,0:T(8,128)S(1)}, f32[640,128]{1,0:T(8,128)S(1)}) custom-call(bf16[640,384]{1,0:T(8,128)(2,1)S(1)} %collective-permute-done.21.refs_0_, ...), custom_call_target="tpu_custom_call", output_to_operand_aliasing={{0}: (6, {}), {1}: (7, {}), {2}: (8, {}), {3}: (9, {})} | custom-call | flops 5033164800 | bytes 3932160 | tf_op jit(solution)/shard_map/attention/pallas_call | solution.py:229
  187.9 2.4 collective-permute-done.26
  190.3 4.9 %attention.8 = (f32[640,384]{1,0:T(8,128)S(1)}, f32[640,384]{1,0:T(8,128)S(1)}, f32[640,128]{1,0:T(8,128)S(1)}, f32[640,128]{1,0:T(8,128)S(1)}) custom-call(bf16[640,384]{1,0:T(8,128)(2,1)S(1)} %collective-permute-done.21.refs_0_, ...), custom_call_target="tpu_custom_call", output_to_operand_aliasing={{0}: (4, {}), {1}: (5, {}), {2}: (6, {}), {3}: (7, {})} | custom-call | flops 2516582400 | bytes 3932160 | tf_op jit(solution)/shard_map/attention/pallas_call | solution.py:229
  195.8 2.5 collective-permute-done.29
  199.1 11.0 %attention.9 = (f32[640,384]{1,0:T(8,128)S(1)}, f32[640,384]{1,0:T(8,128)S(1)}, f32[640,128]{1,0:T(8,128)S(1)}, f32[640,128]{1,0:T(8,128)S(1)}) custom-call(bf16[640,384]{1,0:T(8,128)(2,1)S(1)} %get-tuple-element.88.refs_0_, ...), custom_call_target="tpu_custom_call", output_to_operand_aliasing={{0}: (8, {}), {1}: (9, {}), {2}: (10, {}), {3}: (11, {})} | custom-call | flops 7549747200 | bytes 3932160 | tf_op jit(solution)/shard_map/attention/pallas_call | solution.py:229
  210.1 6.9 %collective-permute-done.30.back_ref = bf16[640,512]{1,0:T(8,128)(2,1)S(1)} collective-permute-done((bf16[640,512]{1,0:T(8,128)(2,1)S(1)}, bf16[640,512]{1,0:T(8,128)(2,1)S(1)}, u32[]{:S(2)}, u32[]{:S(2)}) %collective-permute-start.30) | collective-permute-done | bytes 655392 | tf_op jit(solution)/shard_map/ppermute | solution.py:22
  217.0 0.5 collective-permute-start.32
  217.5 2.5 collective-permute-done.32.other_tot_ref
  220.1 0.5 combine.1.own_ref
  220.6 1.3 collective-permute-start.33
  221.9 12.1 %collective-permute-done.33.other_ref = bf16[640,384]{1,0:T(8,128)(2,1)S(1)} collective-permute-done((bf16[640,384]{1,0:T(8,128)(2,1)S(1)}, bf16[640,384]{1,0:T(8,128)(2,1)S(1)}, u32[]{:S(2)}, u32[]{:S(2)}) %collective-permute-start.33) | collective-permute-done | bytes 491552 | tf_op jit(solution)/shard_map/ppermute | solution.py:22
  234.0 6.0 %out_projection.1 = bf16[4,640,384]{2,1,0:T(8,128)(2,1)} custom-call(s32[1]{0:T(128)} %bitcast.place_ref, bf16[640,384]{1,0:T(8,128)(2,1)S(1)} %combine.1.own_ref, bf16[640,384]{1,0:T(8,128)(2,1)S(1)} %collective-permute-done.33.other_ref, bf16[16,2,192,384]{3,2,1,0:T(8,128)(2,1)} %bitcast.62), custom_call_target="tpu_custom_call" | custom-call | tf_op jit(solution)/shard_map/out_projection/pallas_call | solution.py:299
  239.9 3.6 %all-to-all-start.3 = ((bf16[4,640,384]{2,1,0:T(8,128)(2,1)}), bf16[4,640,384]{2,1,0:T(8,128)(2,1)S(1)}, u32[]{:S(2)}, u32[]{:S(2)}) async-start(bf16[4,640,384]{2,1,0:T(8,128)(2,1)} %out_projection.1), calls=%async_computation.3 | async-start | bytes 3932160 | tf_op jit(solution)/shard_map/all_to_all | solution.py:430
  243.6 0.9 dynamic-slice_reduce_fusion.1
  244.5 23.7 %all-to-all-done.3 = bf16[4,640,384]{2,1,0:T(8,128)(2,1)S(1)} async-done(((bf16[4,640,384]{2,1,0:T(8,128)(2,1)}), bf16[4,640,384]{2,1,0:T(8,128)(2,1)S(1)}, u32[]{:S(2)}, u32[]{:S(2)}) %all-to-all-start.3) | async-done | bytes 1966112 | tf_op jit(solution)/shard_map/all_to_all | solution.py:430
  268.4 0.7 fusion.6
  269.1 0.9 fusion.2
  (108 shorter events, 4.0 us)
Async XLA Ops:
  7.2 13.8 %copy-start = (bf16[128,1280]{1,0:T(8,128)(2,1)S(1)}, bf16[128,1280]{1,0:T(8,128)(2,1)}, u32[]{:S(2)}) copy-start(bf16[128,1280]{1,0:T(8,128)(2,1)} %param.17) | copy-start | bytes 983044
  7.2 13.6 %copy-start.14 = (bf16[512,384]{1,0:T(8,128)(2,1)S(1)}, bf16[512,384]{1,0:T(8,128)(2,1)}, u32[]{:S(2)}) copy-start(bf16[512,384]{1,0:T(8,128)(2,1)} %param.22) | copy-start | bytes 1179652
  7.2 13.6 %collective-permute-start = (bf16[512,384]{1,0:T(8,128)(2,1)}, bf16[512,384]{1,0:T(8,128)(2,1)S(1)}, u32[]{:S(2)}, u32[]{:S(2)}) collective-permute-start(bf16[512,384]{1,0:T(8,128)(2,1)} %param.22), channel_id=1, source_target_pairs={{0,1},{1,0},{2,3},{3,2},{4,5},{5,4},{6,7},{7,6},{8,9},{9,8},{10,11... | collective-permute-start | bytes 1179656 | tf_op jit(solution)/shard_map/ppermute | solution.py:22
  10.0 10.9 %collective-permute-start.1 = (bf16[2,192,384]{2,1,0:T(8,128)(2,1)S(1)}, bf16[2,192,384]{2,1,0:T(8,128)(2,1)S(1)}, u32[]{:S(2)}, u32[]{:S(2)}) collective-permute-start(bf16[2,192,384]{2,1,0:T(8,128)(2,1)S(1)} %pad_maximum_fusion.4), channel_id=1, source_target_pairs={{0,0},{1,16},{16,1},{17,17},{32,32},{33,48},{48,33},{49,49},{2,2},... | collective-permute-start | bytes 884744 | tf_op jit(solution)/shard_map/ppermute | solution.py:354
  11.9 29.0 %collective-permute-start.2 = (bf16[6,192,384]{2,1,0:T(8,128)(2,1)S(1)}, bf16[6,192,384]{2,1,0:T(8,128)(2,1)}, u32[]{:S(2)}, u32[]{:S(2)}) collective-permute-start(bf16[6,192,384]{2,1,0:T(8,128)(2,1)S(1)} %maximum_bitcast_fusion.refs_5_), channel_id=1, source_target_pairs={{0,16},{16,32},{32,48},{48,0},{1,17},{17,33},{33,49},{49,1},{2,18}... | collective-permute-start | bytes 2654216 | tf_op jit(solution)/shard_map/ppermute | solution.py:22
  15.1 25.8 %collective-permute-start.3 = (bf16[6,192,384]{2,1,0:T(8,128)(2,1)S(1)}, bf16[6,192,384]{2,1,0:T(8,128)(2,1)}, u32[]{:S(2)}, u32[]{:S(2)}) collective-permute-start(bf16[6,192,384]{2,1,0:T(8,128)(2,1)S(1)} %maximum_bitcast_fusion.refs_5_), channel_id=1, source_target_pairs={{0,48},{16,0},{32,16},{48,32},{1,49},{17,1},{33,17},{49,33},{2,50}... | collective-permute-start | bytes 2654216 | tf_op jit(solution)/shard_map/ppermute | solution.py:22
  17.6 23.3 %collective-permute-start.4 = (bf16[6,192,384]{2,1,0:T(8,128)(2,1)S(1)}, bf16[6,192,384]{2,1,0:T(8,128)(2,1)}, u32[]{:S(2)}, u32[]{:S(2)}) collective-permute-start(bf16[6,192,384]{2,1,0:T(8,128)(2,1)S(1)} %maximum_bitcast_fusion.refs_5_), channel_id=1, source_target_pairs={{0,64},{64,0},{1,65},{65,1},{2,66},{66,2},{3,67},{67,3},{4,68},{68... | collective-permute-start | bytes 2654216 | tf_op jit(solution)/shard_map/ppermute | solution.py:22
  20.9 6.1 %copy-start.17 = (bf16[2,192,384]{2,1,0:T(8,128)(2,1)}, bf16[2,192,384]{2,1,0:T(8,128)(2,1)S(1)}, u32[]{:S(2)}) copy-start(bf16[2,192,384]{2,1,0:T(8,128)(2,1)S(1)} %collective-permute-done.1) | copy-start | bytes 884740
  27.0 32.0 %copy-start.18 = (bf16[128,448]{0,1:T(8,128)(2,1)S(1)}, bf16[128,448]{0,1:T(8,128)(2,1)}, u32[]{:S(2)}) copy-start(bf16[128,448]{0,1:T(8,128)(2,1)} %param.19) | copy-start | bytes 344068
  29.2 24.2 %all-to-all-start = ((bf16[8,128,448]{1,2,0:T(8,128)(2,1)}), bf16[8,128,448]{1,2,0:T(8,128)(2,1)S(1)}, u32[]{:S(2)}, u32[]{:S(2)}) async-start(bf16[8,128,448]{1,2,0:T(8,128)(2,1)} %bitcast.36), calls=%async_computation | async-start | bytes 1835008 | tf_op jit(solution)/shard_map/all_to_all | solution.py:365
  53.4 40.0 %collective-permute-start.7 = (bf16[6,192,384]{2,1,0:T(8,128)(2,1)}, bf16[6,192,384]{2,1,0:T(8,128)(2,1)}, u32[]{:S(2)}, u32[]{:S(2)}) collective-permute-start(bf16[6,192,384]{2,1,0:T(8,128)(2,1)} %collective-permute-done.4.refs_9_), channel_id=1, source_target_pairs={{0,16},{16,32},{32,48},{48,0},{1,17},{17,33},{33,49},{49,1},{2,18}... | collective-permute-start | bytes 2654216 | tf_op jit(solution)/shard_map/ppermute | solution.py:22
  56.7 36.7 %collective-permute-start.8 = (bf16[6,192,384]{2,1,0:T(8,128)(2,1)}, bf16[6,192,384]{2,1,0:T(8,128)(2,1)}, u32[]{:S(2)}, u32[]{:S(2)}) collective-permute-start(bf16[6,192,384]{2,1,0:T(8,128)(2,1)} %collective-permute-done.4.refs_9_), channel_id=1, source_target_pairs={{0,48},{16,0},{32,16},{48,32},{1,49},{17,1},{33,17},{49,33},{2,50}... | collective-permute-start | bytes 2654216 | tf_op jit(solution)/shard_map/ppermute | solution.py:22
  60.1 45.1 %copy-start.22 = (f32[3584]{0:T(1024)S(1)}, f32[3584]{0:T(1024)}, u32[]{:S(2)}) copy-start(f32[3584]{0:T(1024)} %param.20) | copy-start | bytes 43012
  60.1 33.3 %all-to-all-start.1 = ((bf16[8,128,448]{1,2,0:T(8,128)(2,1)}), bf16[8,128,448]{1,2,0:T(8,128)(2,1)}, u32[]{:S(2)}, u32[]{:S(2)}) async-start(bf16[8,128,448]{1,2,0:T(8,128)(2,1)} %broadcast_in_dim.4), calls=%async_computation.1 | async-start | bytes 1835008 | tf_op jit(solution)/shard_map/all_to_all | solution.py:32
  64.6 169.4 %all-gather.3.cloned.1.call-start = ((), (), s32[]{:S(2)}) async-start(), calls=%async_computation.4 | async-start | bytes 5013504 | tf_op jit(solution)/shard_map/all_gather | solution.py:361
  64.6 28.8 %collective-permute-start.5 = (bf16[2,512,384]{2,1,0:T(8,128)(2,1)S(1)}, bf16[2,512,384]{2,1,0:T(8,128)(2,1)S(1)}, u32[]{:S(2)}, u32[]{:S(2)}) collective-permute-start(bf16[2,512,384]{2,1,0:T(8,128)(2,1)S(1)} %pad_maximum_fusion.refs_0_), channel_id=1, source_target_pairs={{0,2},{2,4},{4,6},{6,0},{1,3},{3,5},{5,7},{7,1},{8,10},{10,12},{12... | collective-permute-start | bytes 2359304 | tf_op jit(solution)/shard_map/ppermute | solution.py:22
  66.6 26.8 %collective-permute-start.6 = (bf16[2,512,384]{2,1,0:T(8,128)(2,1)S(1)}, bf16[2,512,384]{2,1,0:T(8,128)(2,1)S(1)}, u32[]{:S(2)}, u32[]{:S(2)}) collective-permute-start(bf16[2,512,384]{2,1,0:T(8,128)(2,1)S(1)} %pad_maximum_fusion.refs_0_), channel_id=1, source_target_pairs={{0,6},{2,0},{4,2},{6,4},{1,7},{3,1},{5,3},{7,5},{8,14},{10,8},{12,... | collective-permute-start | bytes 2359304 | tf_op jit(solution)/shard_map/ppermute | solution.py:22
  93.4 11.8 %copy-start.3 = (bf16[2,512,384]{2,1,0:T(8,128)(2,1)}, bf16[2,512,384]{2,1,0:T(8,128)(2,1)S(1)}, u32[]{:S(2)}) copy-start(bf16[2,512,384]{2,1,0:T(8,128)(2,1)S(1)} %collective-permute-done.6.refs_2_) | copy-start | bytes 2359300
  93.5 8.4 %collective-permute-start.10 = (bf16[512,384]{1,0:T(8,128)(2,1)S(1)}, bf16[512,384]{1,0:T(8,128)(2,1)S(1)}, u32[]{:S(2)}, u32[]{:S(2)}) collective-permute-start(bf16[512,384]{1,0:T(8,128)(2,1)S(1)} %slice_bitcast_fusion.2), channel_id=1, source_target_pairs={{0,6},{2,0},{4,2},{6,4},{1,7},{3,1},{5,3},{7,5},{8,14},{10,8},{12,... | collective-permute-start | bytes 1179656 | tf_op jit(solution)/shard_map/ppermute | solution.py:22
  94.8 9.7 %collective-permute-start.9 = (bf16[512,384]{1,0:T(8,128)(2,1)S(1)}, bf16[512,384]{1,0:T(8,128)(2,1)S(1)}, u32[]{:S(2)}, u32[]{:S(2)}) collective-permute-start(bf16[512,384]{1,0:T(8,128)(2,1)S(1)} %slice_bitcast_fusion.3), channel_id=1, source_target_pairs={{0,2},{2,4},{4,6},{6,0},{1,3},{3,5},{5,7},{7,1},{8,10},{10,12},{12... | collective-permute-start | bytes 1179656 | tf_op jit(solution)/shard_map/ppermute | solution.py:22
  95.7 27.5 %collective-permute-start.11 = (bf16[6,192,384]{2,1,0:T(8,128)(2,1)}, bf16[6,192,384]{2,1,0:T(8,128)(2,1)}, u32[]{:S(2)}, u32[]{:S(2)}) collective-permute-start(bf16[6,192,384]{2,1,0:T(8,128)(2,1)} %collective-permute-done.2.refs_6_), channel_id=1, source_target_pairs={{0,16},{16,32},{32,48},{48,0},{1,17},{17,33},{33,49},{49,1},{2,18}... | collective-permute-start | bytes 2654216 | tf_op jit(solution)/shard_map/ppermute | solution.py:22
  95.7 28.6 %collective-permute-start.12 = (bf16[6,192,384]{2,1,0:T(8,128)(2,1)}, bf16[6,192,384]{2,1,0:T(8,128)(2,1)}, u32[]{:S(2)}, u32[]{:S(2)}) collective-permute-start(bf16[6,192,384]{2,1,0:T(8,128)(2,1)} %collective-permute-done.8.refs_11_), channel_id=1, source_target_pairs={{0,48},{16,0},{32,16},{48,32},{1,49},{17,1},{33,17},{49,33},{2,50}... | collective-permute-start | bytes 2654216 | tf_op jit(solution)/shard_map/ppermute | solution.py:22
  98.9 29.2 %collective-permute-start.13 = (bf16[6,192,384]{2,1,0:T(8,128)(2,1)S(1)}, bf16[6,192,384]{2,1,0:T(8,128)(2,1)}, u32[]{:S(2)}, u32[]{:S(2)}) collective-permute-start(bf16[6,192,384]{2,1,0:T(8,128)(2,1)S(1)} %maximum_bitcast_fusion.refs_5_), channel_id=1, source_target_pairs={{0,8},{8,0},{1,9},{9,1},{2,10},{10,2},{3,11},{11,3},{4,12},{12,4},... | collective-permute-start | bytes 2654216 | tf_op jit(solution)/shard_map/ppermute | solution.py:22
  101.9 0.8 copy-start.7
  102.7 25.5 %collective-permute-start.17 = (bf16[6,192,384]{2,1,0:T(8,128)(2,1)}, bf16[6,192,384]{2,1,0:T(8,128)(2,1)}, u32[]{:S(2)}, u32[]{:S(2)}) collective-permute-start(bf16[6,192,384]{2,1,0:T(8,128)(2,1)} %collective-permute-done.4.refs_9_), channel_id=1, source_target_pairs={{0,8},{8,0},{1,9},{9,1},{2,10},{10,2},{3,11},{11,3},{4,12},{12,4},... | collective-permute-start | bytes 2654216 | tf_op jit(solution)/shard_map/ppermute | solution.py:22
  104.4 0.7 copy-start.9
  105.2 23.5 %collective-permute-start.14 = (bf16[6,192,384]{2,1,0:T(8,128)(2,1)}, bf16[6,192,384]{2,1,0:T(8,128)(2,1)}, u32[]{:S(2)}, u32[]{:S(2)}) collective-permute-start(bf16[6,192,384]{2,1,0:T(8,128)(2,1)} %collective-permute-done.2.refs_6_), channel_id=1, source_target_pairs={{0,8},{8,0},{1,9},{9,1},{2,10},{10,2},{3,11},{11,3},{4,12},{12,4},... | collective-permute-start | bytes 2654216 | tf_op jit(solution)/shard_map/ppermute | solution.py:22
  106.8 1.8 copy-start.2
  110.2 5.0 %copy-start.23 = (f32[128]{0:T(128)S(1)}, f32[128]{0:T(128)}, u32[]{:S(2)}) copy-start(f32[128]{0:T(128)} %param.26) | copy-start | bytes 1540
  110.2 5.0 %copy-start.24 = (f32[128]{0:T(128)S(1)}, f32[128]{0:T(128)}, u32[]{:S(2)}) copy-start(f32[128]{0:T(128)} %param.25) | copy-start | bytes 1540
  110.2 18.8 %copy-start.25 = (s32[128]{0:T(128)S(1)}, s32[128]{0:T(128)}, u32[]{:S(2)}) copy-start(s32[128]{0:T(128)} %param.31) | copy-start | bytes 1540
  111.1 17.1 %all-to-all-start.2 = ((bf16[8,128,384]{2,1,0:T(8,128)(2,1)}), bf16[8,128,384]{2,1,0:T(8,128)(2,1)S(1)}, u32[]{:S(2)}, u32[]{:S(2)}) async-start(bf16[8,128,384]{2,1,0:T(8,128)(2,1)} %broadcast_in_dim.5), calls=%async_computation.2 | async-start | bytes 1572864 | tf_op jit(solution)/shard_map/all_to_all | solution.py:32
  115.1 15.5 %copy-start.20 = (f32[4,3072]{1,0:T(4,128)S(1)}, f32[4,3072]{1,0:T(4,128)}, u32[]{:S(2)}) copy-start(f32[4,3072]{1,0:T(4,128)} %param.24) | copy-start | bytes 147460
  115.1 15.5 %copy-start.21 = (f32[4,3072]{1,0:T(4,128)S(1)}, f32[4,3072]{1,0:T(4,128)}, u32[]{:S(2)}) copy-start(f32[4,3072]{1,0:T(4,128)} %param.23) | copy-start | bytes 147460
  123.2 7.5 %collective-permute-start.19 = (bf16[6,192,384]{2,1,0:T(8,128)(2,1)}, bf16[6,192,384]{2,1,0:T(8,128)(2,1)}, u32[]{:S(2)}, u32[]{:S(2)}) collective-permute-start(bf16[6,192,384]{2,1,0:T(8,128)(2,1)} %collective-permute-done.8.refs_11_), channel_id=1, source_target_pairs={{0,8},{8,0},{1,9},{9,1},{2,10},{10,2},{3,11},{11,3},{4,12},{12,4},... | collective-permute-start | bytes 2654216 | tf_op jit(solution)/shard_map/ppermute | solution.py:22
  124.3 6.4 %collective-permute-start.15 = (bf16[6,192,384]{2,1,0:T(8,128)(2,1)}, bf16[6,192,384]{2,1,0:T(8,128)(2,1)}, u32[]{:S(2)}, u32[]{:S(2)}) collective-permute-start(bf16[6,192,384]{2,1,0:T(8,128)(2,1)} %collective-permute-done.3.refs_7_), channel_id=1, source_target_pairs={{0,8},{8,0},{1,9},{9,1},{2,10},{10,2},{3,11},{11,3},{4,12},{12,4},... | collective-permute-start | bytes 2654216 | tf_op jit(solution)/shard_map/ppermute | solution.py:22
  128.2 2.8 %collective-permute-start.18 = (bf16[6,192,384]{2,1,0:T(8,128)(2,1)}, bf16[6,192,384]{2,1,0:T(8,128)(2,1)}, u32[]{:S(2)}, u32[]{:S(2)}) collective-permute-start(bf16[6,192,384]{2,1,0:T(8,128)(2,1)} %collective-permute-done.7.refs_10_), channel_id=1, source_target_pairs={{0,8},{8,0},{1,9},{9,1},{2,10},{10,2},{3,11},{11,3},{4,12},{12,4},... | collective-permute-start | bytes 2654216 | tf_op jit(solution)/shard_map/ppermute | solution.py:22
  128.2 4.0 %collective-permute-start.16 = (bf16[6,192,384]{2,1,0:T(8,128)(2,1)}, bf16[6,192,384]{2,1,0:T(8,128)(2,1)}, u32[]{:S(2)}, u32[]{:S(2)}) collective-permute-start(bf16[6,192,384]{2,1,0:T(8,128)(2,1)} %collective-permute-done.11.refs_8_), channel_id=1, source_target_pairs={{0,8},{8,0},{1,9},{9,1},{2,10},{10,2},{3,11},{11,3},{4,12},{12,4},... | collective-permute-start | bytes 2654216 | tf_op jit(solution)/shard_map/ppermute | solution.py:22
  128.7 4.8 %collective-permute-start.20 = (bf16[6,192,384]{2,1,0:T(8,128)(2,1)}, bf16[6,192,384]{2,1,0:T(8,128)(2,1)}, u32[]{:S(2)}, u32[]{:S(2)}) collective-permute-start(bf16[6,192,384]{2,1,0:T(8,128)(2,1)} %collective-permute-done.12.refs_12_), channel_id=1, source_target_pairs={{0,8},{8,0},{1,9},{9,1},{2,10},{10,2},{3,11},{11,3},{4,12},{12,4},... | collective-permute-start | bytes 2654216 | tf_op jit(solution)/shard_map/ppermute | solution.py:22
  129.1 4.4 %copy-start.4 = (bf16[2,512,384]{2,1,0:T(8,128)(2,1)S(1)}, bf16[2,512,384]{2,1,0:T(8,128)(2,1)}, u32[]{:S(2)}) copy-start(bf16[2,512,384]{2,1,0:T(8,128)(2,1)} %copy-done.3) | copy-start | bytes 2359300
  129.1 4.4 %copy-start.8 = (bf16[512,384]{1,0:T(8,128)(2,1)S(1)}, bf16[512,384]{1,0:T(8,128)(2,1)}, u32[]{:S(2)}) copy-start(bf16[512,384]{1,0:T(8,128)(2,1)} %copy-done.7) | copy-start | bytes 1179652
  129.1 4.4 %copy-start.10 = (bf16[512,384]{1,0:T(8,128)(2,1)S(1)}, bf16[512,384]{1,0:T(8,128)(2,1)}, u32[]{:S(2)}) copy-start(bf16[512,384]{1,0:T(8,128)(2,1)} %copy-done.9) | copy-start | bytes 1179652
  147.7 6.8 %collective-permute-start.22 = (bf16[640,384]{1,0:T(8,128)(2,1)S(1)}, bf16[640,384]{1,0:T(8,128)(2,1)S(1)}, u32[]{:S(2)}, u32[]{:S(2)}) collective-permute-start(bf16[640,384]{1,0:T(8,128)(2,1)S(1)} %get-tuple-element.88.refs_0_), channel_id=1, source_target_pairs={{0,8},{8,0},{1,9},{9,1},{2,10},{10,2},{3,11},{11,3},{4,12},{12,4},... | collective-permute-start | bytes 1474568 | tf_op jit(solution)/shard_map/ppermute | solution.py:22
  147.9 15.1 %collective-permute-start.21 = (bf16[640,384]{1,0:T(8,128)(2,1)S(1)}, bf16[640,384]{1,0:T(8,128)(2,1)S(1)}, u32[]{:S(2)}, u32[]{:S(2)}) collective-permute-start(bf16[640,384]{1,0:T(8,128)(2,1)S(1)} %get-tuple-element.88.refs_0_), channel_id=1, source_target_pairs={{0,64},{64,0},{1,65},{65,1},{2,66},{66,2},{3,67},{67,3},{4,68},{68... | collective-permute-start | bytes 1474568 | tf_op jit(solution)/shard_map/ppermute | solution.py:22
  151.3 25.2 %collective-permute-start.24 = (bf16[2,640,384]{2,1,0:T(8,128)(2,1)}, bf16[2,640,384]{2,1,0:T(8,128)(2,1)S(1)}, u32[]{:S(2)}, u32[]{:S(2)}) collective-permute-start(bf16[2,640,384]{2,1,0:T(8,128)(2,1)} %get-tuple-element.89.refs_2_.refs_3_), channel_id=1, source_target_pairs={{0,16},{16,32},{32,48},{48,0},{1,17},{17,33},{33,49},{49,1},{2,18}... | collective-permute-start | bytes 2949128 | tf_op jit(solution)/shard_map/ppermute | solution.py:22
  151.3 25.2 %collective-permute-start.25 = (bf16[2,640,384]{2,1,0:T(8,128)(2,1)}, bf16[2,640,384]{2,1,0:T(8,128)(2,1)S(1)}, u32[]{:S(2)}, u32[]{:S(2)}) collective-permute-start(bf16[2,640,384]{2,1,0:T(8,128)(2,1)} %get-tuple-element.89.refs_2_.refs_3_), channel_id=1, source_target_pairs={{0,48},{16,0},{32,16},{48,32},{1,49},{17,1},{33,17},{49,33},{2,50}... | collective-permute-start | bytes 2949128 | tf_op jit(solution)/shard_map/ppermute | solution.py:22
  154.5 1.2 copy-start.12
  155.7 9.2 %copy-start.13 = (bf16[2,640,384]{2,1,0:T(8,128)(2,1)S(1)}, bf16[2,640,384]{2,1,0:T(8,128)(2,1)}, u32[]{:S(2)}) copy-start(bf16[2,640,384]{2,1,0:T(8,128)(2,1)} %get-tuple-element.89.refs_2_.refs_3_) | copy-start | bytes 2949124
  163.0 1.9 collective-permute-start.23
  176.5 11.4 %copy-start.11 = (bf16[2,640,384]{2,1,0:T(8,128)(2,1)}, bf16[2,640,384]{2,1,0:T(8,128)(2,1)S(1)}, u32[]{:S(2)}) copy-start(bf16[2,640,384]{2,1,0:T(8,128)(2,1)S(1)} %collective-permute-done.25.refs_3_.refs_5_.refs_6_) | copy-start | bytes 2949124
  176.6 13.7 %collective-permute-start.26 = (bf16[640,384]{1,0:T(8,128)(2,1)S(1)}, bf16[640,384]{1,0:T(8,128)(2,1)S(1)}, u32[]{:S(2)}, u32[]{:S(2)}) collective-permute-start(bf16[640,384]{1,0:T(8,128)(2,1)S(1)} %slice_bitcast_fusion.1), channel_id=1, source_target_pairs={{0,16},{16,32},{32,48},{48,0},{1,17},{17,33},{33,49},{49,1},{2,18}... | collective-permute-start | bytes 1474568 | tf_op jit(solution)/shard_map/ppermute | solution.py:22
  176.7 13.6 %collective-permute-start.27 = (bf16[640,384]{1,0:T(8,128)(2,1)S(1)}, bf16[640,384]{1,0:T(8,128)(2,1)S(1)}, u32[]{:S(2)}, u32[]{:S(2)}) collective-permute-start(bf16[640,384]{1,0:T(8,128)(2,1)S(1)} %slice_bitcast_fusion), channel_id=1, source_target_pairs={{0,48},{16,0},{32,16},{48,32},{1,49},{17,1},{33,17},{49,33},{2,50}... | collective-permute-start | bytes 1474568 | tf_op jit(solution)/shard_map/ppermute | solution.py:22
  195.2 3.2 %collective-permute-start.28 = (f32[640,384]{1,0:T(8,128)S(1)}, f32[640,384]{1,0:T(8,128)S(1)}, u32[]{:S(2)}, u32[]{:S(2)}) collective-permute-start(f32[640,384]{1,0:T(8,128)S(1)} %get-tuple-element.116), channel_id=1, source_target_pairs={{0,8},{8,0},{1,9},{9,1},{2,10},{10,2},{3,11},{11,3},{4,12},{12,4},... | collective-permute-start | bytes 2949128 | tf_op jit(solution)/shard_map/ppermute | solution.py:22
  195.3 3.0 %collective-permute-start.29 = (f32[640,128]{1,0:T(8,128)S(1)}, f32[640,128]{1,0:T(8,128)S(1)}, u32[]{:S(2)}, u32[]{:S(2)}) collective-permute-start(f32[640,128]{1,0:T(8,128)S(1)} %get-tuple-element.118), channel_id=1, source_target_pairs={{0,8},{8,0},{1,9},{9,1},{2,10},{10,2},{3,11},{11,3},{4,12},{12,4},... | collective-permute-start | bytes 983048 | tf_op jit(solution)/shard_map/ppermute | solution.py:22
  198.7 18.4 %collective-permute-start.30 = (bf16[640,512]{1,0:T(8,128)(2,1)S(1)}, bf16[640,512]{1,0:T(8,128)(2,1)S(1)}, u32[]{:S(2)}, u32[]{:S(2)}) collective-permute-start(bf16[640,512]{1,0:T(8,128)(2,1)S(1)} %pad_maximum_fusion.1), channel_id=1, source_target_pairs={{0,64},{64,0},{1,65},{65,1},{2,66},{66,2},{3,67},{67,3},{4,68},{68... | collective-permute-start | bytes 1966088 | tf_op jit(solution)/shard_map/ppermute | solution.py:22
  217.0 3.0 %collective-permute-start.31 = (f32[640,384]{1,0:T(8,128)S(1)}, f32[640,384]{1,0:T(8,128)S(1)}, u32[]{:S(2)}, u32[]{:S(2)}) collective-permute-start(f32[640,384]{1,0:T(8,128)S(1)} %get-tuple-element.133), channel_id=1, source_target_pairs={{0,8},{8,0},{1,9},{9,1},{2,10},{10,2},{3,11},{11,3},{4,12},{12,4},... | collective-permute-start | bytes 2949128 | tf_op jit(solution)/shard_map/ppermute | solution.py:22
  217.0 3.0 %collective-permute-start.32 = (f32[640,128]{1,0:T(8,128)S(1)}, f32[640,128]{1,0:T(8,128)S(1)}, u32[]{:S(2)}, u32[]{:S(2)}) collective-permute-start(f32[640,128]{1,0:T(8,128)S(1)} %get-tuple-element.136), channel_id=1, source_target_pairs={{0,8},{8,0},{1,9},{9,1},{2,10},{10,2},{3,11},{11,3},{4,12},{12,4},... | collective-permute-start | bytes 983048 | tf_op jit(solution)/shard_map/ppermute | solution.py:22
  220.6 13.3 %collective-permute-start.33 = (bf16[640,384]{1,0:T(8,128)(2,1)S(1)}, bf16[640,384]{1,0:T(8,128)(2,1)S(1)}, u32[]{:S(2)}, u32[]{:S(2)}) collective-permute-start(bf16[640,384]{1,0:T(8,128)(2,1)S(1)} %combine.1.own_ref), channel_id=1, source_target_pairs={{0,1},{1,0},{2,3},{3,2},{4,5},{5,4},{6,7},{7,6},{8,9},{9,8},{10,11... | collective-permute-start | bytes 1474568 | tf_op jit(solution)/shard_map/ppermute | solution.py:22
  239.9 28.2 %all-to-all-start.3 = ((bf16[4,640,384]{2,1,0:T(8,128)(2,1)}), bf16[4,640,384]{2,1,0:T(8,128)(2,1)S(1)}, u32[]{:S(2)}, u32[]{:S(2)}) async-start(bf16[4,640,384]{2,1,0:T(8,128)(2,1)} %out_projection.1), calls=%async_computation.3 | async-start | bytes 3932160 | tf_op jit(solution)/shard_map/all_to_all | solution.py:430
  243.5 24.9 %copy-start.6 = (bf16[128,384]{1,0:T(8,128)(2,1)S(1)}, bf16[128,384]{1,0:T(8,128)(2,1)}, u32[]{:S(2)}) copy-start(bf16[128,384]{1,0:T(8,128)(2,1)} %copy-done.5) | copy-start | bytes 294916
  243.5 24.9 %copy-start.19 = (bf16[128,384]{1,0:T(8,128)(2,1)S(1)}, bf16[128,384]{1,0:T(8,128)(2,1)}, u32[]{:S(2)}) copy-start(bf16[128,384]{1,0:T(8,128)(2,1)} %param.33) | copy-start | bytes 294916
  243.5 25.6 %copy-start.15 = (bf16[512,384]{1,0:T(8,128)(2,1)S(1)}, bf16[512,384]{1,0:T(8,128)(2,1)}, u32[]{:S(2)}) copy-start(bf16[512,384]{1,0:T(8,128)(2,1)} %param.22) | copy-start | bytes 1179652
  243.6 25.6 %copy-start.16 = (bf16[512,384]{1,0:T(8,128)(2,1)S(1)}, bf16[512,384]{1,0:T(8,128)(2,1)}, u32[]{:S(2)}) copy-start(bf16[512,384]{1,0:T(8,128)(2,1)} %param.32) | copy-start | bytes 1179652
  268.2 1.9 copy-start.1
  (1 other events, 0.6 us)
Sparse Core Ops, SparseCore 0:
  68.1 59.4 all-gather.2
where the time goes:
time: 278 us; the launch traced here: 277 us
  waiting for transfers between devices  120 us (43%)
  starting transfers between devices  63.1 us (23%)
  Pallas kernels  54.7 us (20%)
  between operations  14.6 us (5%)
  local copies, waits for them, and re-layouts  12.3 us (4%)
  other arithmetic  6.24 us (2%)
  matrix products  6.04 us (2%)
    ppermute x33, waiting for transfers between devices, shift(): lax.ppermute(value, axis, [(k, (k + step) % size) for k in range(size)])  80 us
    ppermute x33, starting transfers between devices, shift(): lax.ppermute(value, axis, [(k, (k + step) % size) for k in range(size)])  38.7 us
    pallas_call x5, Pallas kernels, attention(): pl.pallas_call(functools.partial(attention_kernel, nq, k_sizes, not befor...  33 us
    all_to_all x1, waiting for transfers between devices, shards(): got = lax.all_to_all(parts, 'x', split_axis=0, concat_axis=0, tiled=True)  23.7 us
    pallas_call x1, Pallas kernels, qkv(): pl.pallas_call(functools.partial(qkv_kernel, a_index, count), out_shape=(...  14.2 us
    all_to_all x1, waiting for transfers between devices, shards(): got = lax.all_to_all(sent, TP, split_axis=0, concat_axis=0, tiled=True)  12.5 us
    all_to_all x1, starting transfers between devices, shards(): got = lax.all_to_all(sent, TP, split_axis=0, concat_axis=0, tiled=True)  11.7 us
    all_to_all x2, starting transfers between devices, spread(): return lax.all_to_all(copies, axes, split_axis=0, concat_axis=0, tiled=True)  8.4 us
  transfers between devices with their start and end apart: 39, of which 19 were waited for; matrix products, arithmetic and copies ran while one was open for 6% of the time, Pallas kernels for 18%

commit v1 on v0

--- a/solution.py
+++ b/solution.py
@@ -345,6 +345,23 @@
     outs = jnp.stack([jnp.transpose(image_out), jnp.transpose(text_out)])
     weight = jnp.transpose(jnp.concatenate([image_qkv, text_qkv], axis=1), (1, 0, 2))
 
+    a_pair = shift(image_states, "yl", 1)
+    a_near = near(image_states, "x")
+    w_pair = shift(weight, "yh", 1)
+    cond_hidden, a_pair, a_near = together((cond_hidden, a_pair, a_near))
+
+    w_near = near(weight, "z")
+    a_next = near(a_pair, "x")
+    partial_value = jnp.dot(cond_hidden, cond_down, preferred_element_type=F32).astype(BF)
+    enc_share = cond_down.shape[1] // 8
+    sent = jnp.transpose(partial_value.reshape(text_rows, 8, enc_share), (1, 0, 2))
+    got = lax.all_to_all(sent, TP, split_axis=0, concat_axis=0, tiled=True)
+    got, a_near, a_next, w_near, w_pair, outs = together(
+        (got, a_near, a_next, w_near, w_pair, outs)
+    )
+
+    a_far = (shift(a_near[0], "x", 1), shift(a_next[1], "x", -1))
+    w_next = near(w_pair, "z")
     turned = [
         (4 * zh + 2 * zl + y, 4 * zh + 2 * y + zl)
         for zh in range(2)
@@ -352,38 +369,22 @@
         for y in range(2)
     ]
     outs = lax.ppermute(outs, ("z", "yl"), turned)
-    w_near = near(weight, "z")
-    w_pair = shift(weight, "yh", 1)
-    a_own = jnp.stack([image_states, shift(image_states, "yl", 1)])
-    cond_hidden, a_own, outs = together((cond_hidden, a_own, outs))
-
-    a_near = near(a_own, "x")
-    out_w = lax.all_gather(outs, SEQ)
-    partial_value = jnp.dot(cond_hidden, cond_down, preferred_element_type=F32).astype(BF)
-    enc_share = cond_down.shape[1] // 8
-    sent = jnp.transpose(partial_value.reshape(text_rows, 8, enc_share), (1, 0, 2))
-    got = lax.all_to_all(sent, TP, split_axis=0, concat_axis=0, tiled=True)
-
-    got, w_near, w_pair = together((got, w_near, w_pair))
-    w_next = near(w_pair, "z")
     cond_state = (jnp.sum(got.astype(F32), axis=0) + cond_resid.astype(F32)).astype(BF)
     state = spread(cond_state, TP)
-    state, a_near, w_near, w_next = together((state, a_near, w_near, w_next))
+    state, a_far, w_near, w_next, outs = together((state, a_far, w_near, w_next, outs))
+    out_w = lax.all_gather(outs, SEQ)
 
     text_states = text_projection(state, cond_gain, text_proj)
     text_a = spread(text_states, TP)
-    a_far = (shift(a_near[0][0], "x", 1), shift(a_near[1][1], "x", -1))
     w_far = (shift(w_near[0], "z", 1), shift(w_next[1], "z", -1))
-    text_a, a_far, w_far = together((text_a, a_far, w_far))
-
-    a_arrays = [a_own, *a_near, *a_far]
-    a_index = tuple((i, (p,)) for i in range(3) for p in range(2)) + ((3, ()), (4, ()))
-    a_places = [
-        (x + d) % 4 * 2 + (yl + p) % 2 for d, p in [(d, p) for d in (0, 3, 1, 2) for p in range(2)]
-    ]
+    text_a, w_far = together((text_a, w_far))
+
+    blocks = [(p, d) for p in range(2) for d in (0, 3, 1, 2)]
+    a_arrays = [image_states, *a_near, a_far[0], a_pair, *a_next, a_far[1]]
+    a_index = tuple((i, ()) for i in range(8))
+    a_places = [(x + d) % 4 * 2 + (yl + p) % 2 for p, d in blocks]
     w_arrays = [weight, *w_near, w_far[0], w_pair, *w_next, w_far[1]]
     w_arrays += [shift(w, "c", 1) for w in w_arrays]
-    blocks = [(p, d) for p in range(2) for d in (0, 3, 1, 2)]
 
     gains = jnp.stack([query_gain, key_gain])
     image_pos = (seq_index * image_rows + jnp.arange(image_rows)).astype(F32)

time: 278 us -> 273 us (0.982)
  waiting for transfers between devices: 120 us -> 114 us
  starting transfers between devices: 63.1 us -> 58.4 us
  local copies, waits for them, and re-layouts: 12.3 us -> 15.1 us
    all_to_all x1, waiting for transfers between devices: 12.5 us -> 0.01 us  [shards(): got = lax.all_to_all(sent, TP, split_axis=0, concat_axis=0, tiled=True)]
    all_to_all x1, starting transfers between devices: 11.7 us -> 4.54 us  [shards(): got = lax.all_to_all(sent, TP, split_axis=0, concat_axis=0, tiled=True)]
    ppermute x33 -> x35, waiting for transfers between devices: 80 us -> 86.6 us  [shift(): lax.ppermute(value, axis, [(k, (k + step) % size) for k in range(size)])]
    unnamed x52 -> x58, local copies, waits for them, and re-layouts: 5.24 us -> 8.92 us
    ppermute x33 -> x35, starting transfers between devices: 38.7 us -> 39.8 us  [shift(): lax.ppermute(value, axis, [(k, (k + step) % size) for k in range(size)])]
  transfers between devices with their start and end apart: 39 -> 41, of which waited for: 19 -> 18; matrix products, arithmetic and copies ran while one was open for 6% -> 6% of each run, Pallas kernels for 18% -> 18%
where the time goes in v1:
time: 273 us; the launch traced here: 272 us
  waiting for transfers between devices  114 us (42%)
  starting transfers between devices  58.4 us (21%)
  Pallas kernels  54.6 us (20%)
  local copies, waits for them, and re-layouts  15.1 us (6%)
  between operations  14.5 us (5%)
  other arithmetic  8.75 us (3%)
  matrix products  6.05 us (2%)
    ppermute x35, waiting for transfers between devices, shift(): lax.ppermute(value, axis, [(k, (k + step) % size) for k in range(size)])  86.6 us
    ppermute x35, starting transfers between devices, shift(): lax.ppermute(value, axis, [(k, (k + step) % size) for k in range(size)])  39.8 us
    pallas_call x5, Pallas kernels, attention(): pl.pallas_call(functools.partial(attention_kernel, nq, k_sizes, not befor...  33 us
    all_to_all x1, waiting for transfers between devices, shards(): got = lax.all_to_all(parts, 'x', split_axis=0, concat_axis=0, tiled=True)  24.6 us
    pallas_call x1, Pallas kernels, qkv(): pl.pallas_call(functools.partial(qkv_kernel, a_index, count), out_shape=(...  14.1 us
    unnamed x58, local copies, waits for them, and re-layouts  8.92 us
    all_to_all x2, starting transfers between devices, spread(): return lax.all_to_all(copies, axes, split_axis=0, concat_axis=0, tiled=True)  8.02 us
    dot_general x1, matrix products, shards(): jnp.dot(cond_hidden, cond_down, preferred_element_type=F32).astype(BF)  6.05 us
  transfers between devices with their start and end apart: 41, of which 18 were waited for; matrix products, arithmetic and copies ran while one was open for 6% of the time, Pallas kernels for 18%

profile of v1, /device:TPU:0, one launch (start us, length us, event | category | flops | bytes accessed | tf_op | source)
XLA Modules:
  0.0 271.7 jit_solution(14912063822071699444)
XLA Ops:
  7.2 1.7 collective-permute-start
  8.9 1.5 collective-permute-start.1
  10.4 1.7 collective-permute-start.2
  12.2 1.2 maximum_bitcast_fusion.refs_8_
  13.4 2.0 collective-permute-start.5
  15.4 2.2 collective-permute-start.6
  18.2 3.4 %collective-permute-start.7 = (bf16[6,192,384]{2,1,0:T(8,128)(2,1)S(1)}, bf16[6,192,384]{2,1,0:T(8,128)(2,1)}, u32[]{:S(2)}, u32[]{:S(2)}) collective-permute-start(bf16[6,192,384]{2,1,0:T(8,128)(2,1)S(1)} %maximum_bitcast_fusion.refs_8_), channel_id=1, source_target_pairs={{0,64},{64,0},{1,65},{65,1},{2,66},{66,2},{3,67},{67,3},{4,68},{68... | collective-permute-start | bytes 2654216 | tf_op jit(solution)/shard_map/ppermute | solution.py:22
  21.6 6.0 %convolution_convert_fusion = bf16[128,3584]{1,0:T(8,128)(2,1)} fusion(bf16[128,1280]{1,0:T(8,128)(2,1)S(1)} %copy-done, bf16[1280,3584]{1,0:T(8,128)(2,1)} %param.18), kind=kOutput, calls=%fused_computation | convolution fusion | flops 1174863872 | bytes 10420224 | tf_op jit(solution)/shard_map/dot_general | solution.py:355
  27.7 2.3 copy.34
  30.0 4.5 %all-to-all-start = ((bf16[8,128,448]{1,2,0:T(8,128)(2,1)}), bf16[8,128,448]{1,2,0:T(8,128)(2,1)}, u32[]{:S(2)}, u32[]{:S(2)}) async-start(bf16[8,128,448]{1,2,0:T(8,128)(2,1)} %bitcast.30), calls=%async_computation | async-start | bytes 1835008 | tf_op jit(solution)/shard_map/all_to_all | solution.py:358
  34.5 2.0 collective-permute-start.3
  36.5 1.2 collective-permute-start.4
  37.8 0.8 pad_maximum_fusion.3
  38.5 16.8 %collective-permute-done.3.refs_5_ = bf16[512,384]{1,0:T(8,128)(2,1)S(1)} collective-permute-done((bf16[512,384]{1,0:T(8,128)(2,1)S(1)}, bf16[512,384]{1,0:T(8,128)(2,1)S(1)}, u32[]{:S(2)}, u32[]{:S(2)}) %collective-permute-start.3) | collective-permute-done | bytes 393248 | tf_op jit(solution)/shard_map/ppermute | solution.py:22
  55.3 2.0 collective-permute-start.10
  57.4 2.2 collective-permute-start.11
  59.6 1.3 convert_reduce_fusion.1
  60.9 1.1 broadcast_in_dim.4
  62.0 4.2 %all-to-all-start.1 = ((bf16[8,128,448]{1,2,0:T(8,128)(2,1)}), bf16[8,128,448]{1,2,0:T(8,128)(2,1)}, u32[]{:S(2)}, u32[]{:S(2)}) async-start(bf16[8,128,448]{1,2,0:T(8,128)(2,1)} %broadcast_in_dim.4), calls=%async_computation.1 | async-start | bytes 1835008 | tf_op jit(solution)/shard_map/all_to_all | solution.py:32
  66.3 1.9 collective-permute-start.8
  68.1 1.4 collective-permute-start.9
  69.6 1.6 collective-permute-start.12
  71.2 14.5 %collective-permute-done.8.refs_3_ = bf16[512,384]{1,0:T(8,128)(2,1)S(1)} collective-permute-done((bf16[512,384]{1,0:T(8,128)(2,1)S(1)}, bf16[512,384]{1,0:T(8,128)(2,1)S(1)}, u32[]{:S(2)}, u32[]{:S(2)}) %collective-permute-start.8) | collective-permute-done | bytes 393248 | tf_op jit(solution)/shard_map/ppermute | solution.py:22
  85.7 0.8 copy-done.12
  86.7 3.2 %collective-permute-start.14 = (bf16[6,192,384]{2,1,0:T(8,128)(2,1)}, bf16[6,192,384]{2,1,0:T(8,128)(2,1)}, u32[]{:S(2)}, u32[]{:S(2)}) collective-permute-start(bf16[6,192,384]{2,1,0:T(8,128)(2,1)} %collective-permute-done.11.refs_14_), channel_id=1, source_target_pairs={{0,48},{16,0},{32,16},{48,32},{1,49},{17,1},{33,17},{49,33},{2,50}... | collective-permute-start | bytes 2654216 | tf_op jit(solution)/shard_map/ppermute | solution.py:22
  90.5 1.5 copy.35.state_ref
  92.0 1.8 copy-done.2
  93.8 1.0 text_projection.1
  94.8 1.0 broadcast_in_dim.5
  95.8 3.8 %all-to-all-start.2 = ((bf16[8,128,384]{2,1,0:T(8,128)(2,1)}), bf16[8,128,384]{2,1,0:T(8,128)(2,1)S(1)}, u32[]{:S(2)}, u32[]{:S(2)}) async-start(bf16[8,128,384]{2,1,0:T(8,128)(2,1)} %broadcast_in_dim.5), calls=%async_computation.2 | async-start | bytes 1572864 | tf_op jit(solution)/shard_map/all_to_all | solution.py:32
  99.6 9.8 %collective-permute-done.13.refs_11_ = bf16[6,192,384]{2,1,0:T(8,128)(2,1)} collective-permute-done((bf16[6,192,384]{2,1,0:T(8,128)(2,1)}, bf16[6,192,384]{2,1,0:T(8,128)(2,1)}, u32[]{:S(2)}, u32[]{:S(2)}) %collective-permute-start.13) | collective-permute-done | bytes 884768 | tf_op jit(solution)/shard_map/ppermute | solution.py:22
  110.1 3.1 %all-to-all-done.2.text_ref = bf16[8,128,384]{2,1,0:T(8,128)(2,1)S(1)} async-done(((bf16[8,128,384]{2,1,0:T(8,128)(2,1)}), bf16[8,128,384]{2,1,0:T(8,128)(2,1)S(1)}, u32[]{:S(2)}, u32[]{:S(2)}) %all-to-all-start.2) | async-done | bytes 786464 | tf_op jit(solution)/shard_map/all_to_all | solution.py:32
  114.1 1.2 fusion.7
  115.9 1.3 collective-permute-done.18.refs_19_
  117.2 1.3 collective-permute-done.22.refs_23_
  118.5 1.0 copy-done.5
  119.5 1.0 copy-done.7
  120.5 1.0 copy-done.9
  121.5 1.0 copy-done.11
  122.5 1.0 copy-done.13
  123.5 14.1 %qkv.1 = (bf16[640,384]{1,0:T(8,128)(2,1)S(1)}, bf16[2,640,384]{2,1,0:T(8,128)(2,1)}) custom-call(s32[24]{0:T(128)S(1)} %stack.130.place_ref, f32[2,4,3072]{2,1,0:T(4,128)S(1)} %pad_maximum_fusion.4.mod_ref, f32[640,128]{1,0:T(8,128)S(1)} %get-tuple-element.157.cos_ref, f32[640,128]{1,0:T(8,128)S(1)} %get-tuple-element.158.sin_ref, ...), custom_call_target="tpu_custom_call" | custom-call | tf_op jit(solution)/shard_map/qkv/pallas_call | solution.py:161
  137.8 2.7 collective-permute-start.23
  141.0 2.7 %collective-permute-start.27 = (bf16[2,640,384]{2,1,0:T(8,128)(2,1)}, bf16[2,640,384]{2,1,0:T(8,128)(2,1)S(1)}, u32[]{:S(2)}, u32[]{:S(2)}) collective-permute-start(bf16[2,640,384]{2,1,0:T(8,128)(2,1)} %get-tuple-element.99.refs_2_.refs_3_), channel_id=1, source_target_pairs={{0,48},{16,0},{32,16},{48,32},{1,49},{17,1},{33,17},{49,33},{2,50}... | collective-permute-start | bytes 2949128 | tf_op jit(solution)/shard_map/ppermute | solution.py:22
  143.7 1.2 copy-done.15
  144.9 4.7 %attention.5 = (f32[640,384]{1,0:T(8,128)S(1)}, f32[640,384]{1,0:T(8,128)S(1)}, f32[640,128]{1,0:T(8,128)S(1)}, f32[640,128]{1,0:T(8,128)S(1)}) custom-call(bf16[640,384]{1,0:T(8,128)(2,1)S(1)} %get-tuple-element.98.refs_0_, bf16[640,384]{1,0:T(8,128)(2,1)S(1)} %collective-permute-done.24.refs_1_, bf16[2,640,384]{2,1,0:T(8,128)(2,1)S(1)} %copy-done.15, ...), custom_call_target="tpu_custom_call" | custom-call | flops 2516582400 | bytes 3932160 | tf_op jit(solution)/shard_map/attention/pallas_call | solution.py:229
  149.6 3.1 %collective-permute-done.23.refs_0_ = bf16[640,384]{1,0:T(8,128)(2,1)S(1)} collective-permute-done((bf16[640,384]{1,0:T(8,128)(2,1)S(1)}, bf16[640,384]{1,0:T(8,128)(2,1)S(1)}, u32[]{:S(2)}, u32[]{:S(2)}) %collective-permute-start.23) | collective-permute-done | bytes 491552 | tf_op jit(solution)/shard_map/ppermute | solution.py:22
  152.8 1.9 collective-permute-done.25.refs_1_
  154.6 4.7 %attention.6 = (f32[640,384]{1,0:T(8,128)S(1)}, f32[640,384]{1,0:T(8,128)S(1)}, f32[640,128]{1,0:T(8,128)S(1)}, f32[640,128]{1,0:T(8,128)S(1)}) custom-call(bf16[640,384]{1,0:T(8,128)(2,1)S(1)} %collective-permute-done.23.refs_0_, bf16[640,384]{1,0:T(8,128)(2,1)S(1)} %collective-permute-done.25.refs_1_, bf16[2,640,384]{2,1,0:T(8,128)(2,1)S(1)} %copy-done.16, ...), custom_call_target="tpu_custom_call" | custom-call | flops 2516582400 | bytes 3932160 | tf_op jit(solution)/shard_map/attention/pallas_call | solution.py:229
  159.3 8.8 %collective-permute-done.26.refs_2_.refs_4_.refs_5_ = bf16[2,640,384]{2,1,0:T(8,128)(2,1)S(1)} collective-permute-done((bf16[2,640,384]{2,1,0:T(8,128)(2,1)}, bf16[2,640,384]{2,1,0:T(8,128)(2,1)S(1)}, u32[]{:S(2)}, u32[]{:S(2)}) %collective-permute-start.26) | collective-permute-done | bytes 983072 | tf_op jit(solution)/shard_map/ppermute | solution.py:22
  168.6 3.3 %collective-permute-start.29 = (bf16[640,384]{1,0:T(8,128)(2,1)S(1)}, bf16[640,384]{1,0:T(8,128)(2,1)S(1)}, u32[]{:S(2)}, u32[]{:S(2)}) collective-permute-start(bf16[640,384]{1,0:T(8,128)(2,1)S(1)} %slice_bitcast_fusion), channel_id=1, source_target_pairs={{0,48},{16,0},{32,16},{48,32},{1,49},{17,1},{33,17},{49,33},{2,50}... | collective-permute-start | bytes 1474568 | tf_op jit(solution)/shard_map/ppermute | solution.py:22
  171.8 7.7 %attention.7 = (f32[640,384]{1,0:T(8,128)S(1)}, f32[640,384]{1,0:T(8,128)S(1)}, f32[640,128]{1,0:T(8,128)S(1)}, f32[640,128]{1,0:T(8,128)S(1)}) custom-call(bf16[640,384]{1,0:T(8,128)(2,1)S(1)} %collective-permute-done.23.refs_0_, ...), custom_call_target="tpu_custom_call", output_to_operand_aliasing={{0}: (6, {}), {1}: (7, {}), {2}: (8, {}), {3}: (9, {})} | custom-call | flops 5033164800 | bytes 3932160 | tf_op jit(solution)/shard_map/attention/pallas_call | solution.py:229
  179.5 3.0 %collective-permute-done.28 = bf16[640,384]{1,0:T(8,128)(2,1)S(1)} collective-permute-done((bf16[640,384]{1,0:T(8,128)(2,1)S(1)}, bf16[640,384]{1,0:T(8,128)(2,1)S(1)}, u32[]{:S(2)}, u32[]{:S(2)}) %collective-permute-start.28) | collective-permute-done | bytes 491552 | tf_op jit(solution)/shard_map/ppermute | solution.py:22
  182.5 4.9 %attention.8 = (f32[640,384]{1,0:T(8,128)S(1)}, f32[640,384]{1,0:T(8,128)S(1)}, f32[640,128]{1,0:T(8,128)S(1)}, f32[640,128]{1,0:T(8,128)S(1)}) custom-call(bf16[640,384]{1,0:T(8,128)(2,1)S(1)} %collective-permute-done.23.refs_0_, ...), custom_call_target="tpu_custom_call", output_to_operand_aliasing={{0}: (4, {}), {1}: (5, {}), {2}: (6, {}), {3}: (7, {})} | custom-call | flops 2516582400 | bytes 3932160 | tf_op jit(solution)/shard_map/attention/pallas_call | solution.py:229
  188.0 2.5 collective-permute-done.31
  191.3 11.0 %attention.9 = (f32[640,384]{1,0:T(8,128)S(1)}, f32[640,384]{1,0:T(8,128)S(1)}, f32[640,128]{1,0:T(8,128)S(1)}, f32[640,128]{1,0:T(8,128)S(1)}) custom-call(bf16[640,384]{1,0:T(8,128)(2,1)S(1)} %get-tuple-element.98.refs_0_, ...), custom_call_target="tpu_custom_call", output_to_operand_aliasing={{0}: (8, {}), {1}: (9, {}), {2}: (10, {}), {3}: (11, {})} | custom-call | flops 7549747200 | bytes 3932160 | tf_op jit(solution)/shard_map/attention/pallas_call | solution.py:229
  202.4 6.8 %collective-permute-done.32.back_ref = bf16[640,512]{1,0:T(8,128)(2,1)S(1)} collective-permute-done((bf16[640,512]{1,0:T(8,128)(2,1)S(1)}, bf16[640,512]{1,0:T(8,128)(2,1)S(1)}, u32[]{:S(2)}, u32[]{:S(2)}) %collective-permute-start.32) | collective-permute-done | bytes 655392 | tf_op jit(solution)/shard_map/ppermute | solution.py:22
  209.7 2.5 collective-permute-done.34.other_tot_ref
  213.4 12.8 %collective-permute-done.35.other_ref = bf16[640,384]{1,0:T(8,128)(2,1)S(1)} collective-permute-done((bf16[640,384]{1,0:T(8,128)(2,1)S(1)}, bf16[640,384]{1,0:T(8,128)(2,1)S(1)}, u32[]{:S(2)}, u32[]{:S(2)}) %collective-permute-start.35) | collective-permute-done | bytes 491552 | tf_op jit(solution)/shard_map/ppermute | solution.py:22
  226.1 6.0 %out_projection.1 = bf16[4,640,384]{2,1,0:T(8,128)(2,1)} custom-call(s32[1]{0:T(128)} %bitcast.place_ref, bf16[640,384]{1,0:T(8,128)(2,1)S(1)} %combine.1.own_ref, bf16[640,384]{1,0:T(8,128)(2,1)S(1)} %collective-permute-done.35.other_ref, bf16[16,2,192,384]{3,2,1,0:T(8,128)(2,1)} %bitcast.56), custom_call_target="tpu_custom_call" | custom-call | tf_op jit(solution)/shard_map/out_projection/pallas_call | solution.py:299
  232.1 4.4 %all-to-all-start.3 = ((bf16[4,640,384]{2,1,0:T(8,128)(2,1)}), bf16[4,640,384]{2,1,0:T(8,128)(2,1)}, u32[]{:S(2)}, u32[]{:S(2)}) async-start(bf16[4,640,384]{2,1,0:T(8,128)(2,1)} %out_projection.1), calls=%async_computation.3 | async-start | bytes 3932160 | tf_op jit(solution)/shard_map/all_to_all | solution.py:431
  236.7 24.6 %all-to-all-done.3 = bf16[4,640,384]{2,1,0:T(8,128)(2,1)} async-done(((bf16[4,640,384]{2,1,0:T(8,128)(2,1)}), bf16[4,640,384]{2,1,0:T(8,128)(2,1)}, u32[]{:S(2)}, u32[]{:S(2)}) %all-to-all-start.3) | async-done | bytes 1966112 | tf_op jit(solution)/shard_map/all_to_all | solution.py:431
  261.3 2.0 convert_reduce_fusion
  263.3 0.7 fusion.6
  264.0 0.9 fusion.2
  (115 shorter events, 8.0 us)
Async XLA Ops:
  7.2 14.4 %copy-start = (bf16[128,1280]{1,0:T(8,128)(2,1)S(1)}, bf16[128,1280]{1,0:T(8,128)(2,1)}, u32[]{:S(2)}) copy-start(bf16[128,1280]{1,0:T(8,128)(2,1)} %param.17) | copy-start | bytes 983044
  7.2 11.1 %collective-permute-start = (bf16[512,384]{1,0:T(8,128)(2,1)}, bf16[512,384]{1,0:T(8,128)(2,1)S(1)}, u32[]{:S(2)}, u32[]{:S(2)}) collective-permute-start(bf16[512,384]{1,0:T(8,128)(2,1)} %refs_0_.1), channel_id=1, source_target_pairs={{0,1},{1,0},{2,3},{3,2},{4,5},{5,4},{6,7},{7,6},{8,9},{9,8},{10,11... | collective-permute-start | bytes 1179656 | tf_op jit(solution)/shard_map/ppermute | solution.py:22
  8.9 12.7 %collective-permute-start.1 = (bf16[512,384]{1,0:T(8,128)(2,1)}, bf16[512,384]{1,0:T(8,128)(2,1)S(1)}, u32[]{:S(2)}, u32[]{:S(2)}) collective-permute-start(bf16[512,384]{1,0:T(8,128)(2,1)} %refs_0_.1), channel_id=1, source_target_pairs={{0,2},{2,4},{4,6},{6,0},{1,3},{3,5},{5,7},{7,1},{8,10},{10,12},{12... | collective-permute-start | bytes 1179656 | tf_op jit(solution)/shard_map/ppermute | solution.py:22
  10.4 11.2 %collective-permute-start.2 = (bf16[512,384]{1,0:T(8,128)(2,1)}, bf16[512,384]{1,0:T(8,128)(2,1)S(1)}, u32[]{:S(2)}, u32[]{:S(2)}) collective-permute-start(bf16[512,384]{1,0:T(8,128)(2,1)} %refs_0_.1), channel_id=1, source_target_pairs={{0,6},{2,0},{4,2},{6,4},{1,7},{3,1},{5,3},{7,5},{8,14},{10,8},{12,... | collective-permute-start | bytes 1179656 | tf_op jit(solution)/shard_map/ppermute | solution.py:22
  13.4 41.9 %collective-permute-start.5 = (bf16[6,192,384]{2,1,0:T(8,128)(2,1)S(1)}, bf16[6,192,384]{2,1,0:T(8,128)(2,1)}, u32[]{:S(2)}, u32[]{:S(2)}) collective-permute-start(bf16[6,192,384]{2,1,0:T(8,128)(2,1)S(1)} %maximum_bitcast_fusion.refs_8_), channel_id=1, source_target_pairs={{0,16},{16,32},{32,48},{48,0},{1,17},{17,33},{33,49},{49,1},{2,18}... | collective-permute-start | bytes 2654216 | tf_op jit(solution)/shard_map/ppermute | solution.py:22
  15.4 39.9 %collective-permute-start.6 = (bf16[6,192,384]{2,1,0:T(8,128)(2,1)S(1)}, bf16[6,192,384]{2,1,0:T(8,128)(2,1)}, u32[]{:S(2)}, u32[]{:S(2)}) collective-permute-start(bf16[6,192,384]{2,1,0:T(8,128)(2,1)S(1)} %maximum_bitcast_fusion.refs_8_), channel_id=1, source_target_pairs={{0,48},{16,0},{32,16},{48,32},{1,49},{17,1},{33,17},{49,33},{2,50}... | collective-permute-start | bytes 2654216 | tf_op jit(solution)/shard_map/ppermute | solution.py:22
  18.2 37.1 %collective-permute-start.7 = (bf16[6,192,384]{2,1,0:T(8,128)(2,1)S(1)}, bf16[6,192,384]{2,1,0:T(8,128)(2,1)}, u32[]{:S(2)}, u32[]{:S(2)}) collective-permute-start(bf16[6,192,384]{2,1,0:T(8,128)(2,1)S(1)} %maximum_bitcast_fusion.refs_8_), channel_id=1, source_target_pairs={{0,64},{64,0},{1,65},{65,1},{2,66},{66,2},{3,67},{67,3},{4,68},{68... | collective-permute-start | bytes 2654216 | tf_op jit(solution)/shard_map/ppermute | solution.py:22
  21.6 6.1 %copy-start.4 = (bf16[512,384]{1,0:T(8,128)(2,1)}, bf16[512,384]{1,0:T(8,128)(2,1)S(1)}, u32[]{:S(2)}) copy-start(bf16[512,384]{1,0:T(8,128)(2,1)S(1)} %collective-permute-done.2.refs_2_) | copy-start | bytes 1179652
  27.7 10.1 %copy-start.19 = (bf16[384,192]{0,1:T(8,128)(2,1)S(1)}, bf16[384,192]{0,1:T(8,128)(2,1)}, u32[]{:S(2)}) copy-start(bf16[384,192]{0,1:T(8,128)(2,1)} %param.30) | copy-start | bytes 442372
  27.7 10.1 %copy-start.20 = (bf16[384,192]{0,1:T(8,128)(2,1)S(1)}, bf16[384,192]{0,1:T(8,128)(2,1)}, u32[]{:S(2)}) copy-start(bf16[384,192]{0,1:T(8,128)(2,1)} %param.29) | copy-start | bytes 442372
  30.0 30.9 %copy-start.21 = (bf16[128,448]{0,1:T(8,128)(2,1)S(1)}, bf16[128,448]{0,1:T(8,128)(2,1)}, u32[]{:S(2)}) copy-start(bf16[128,448]{0,1:T(8,128)(2,1)} %param.19) | copy-start | bytes 344068
  30.0 25.4 %all-to-all-start = ((bf16[8,128,448]{1,2,0:T(8,128)(2,1)}), bf16[8,128,448]{1,2,0:T(8,128)(2,1)}, u32[]{:S(2)}, u32[]{:S(2)}) async-start(bf16[8,128,448]{1,2,0:T(8,128)(2,1)} %bitcast.30), calls=%async_computation | async-start | bytes 1835008 | tf_op jit(solution)/shard_map/all_to_all | solution.py:358
  34.5 20.8 %collective-permute-start.3 = (bf16[512,384]{1,0:T(8,128)(2,1)S(1)}, bf16[512,384]{1,0:T(8,128)(2,1)S(1)}, u32[]{:S(2)}, u32[]{:S(2)}) collective-permute-start(bf16[512,384]{1,0:T(8,128)(2,1)S(1)} %collective-permute-done.refs_4_), channel_id=1, source_target_pairs={{0,2},{2,4},{4,6},{6,0},{1,3},{3,5},{5,7},{7,1},{8,10},{10,12},{12... | collective-permute-start | bytes 1179656 | tf_op jit(solution)/shard_map/ppermute | solution.py:22
  36.5 18.8 %collective-permute-start.4 = (bf16[512,384]{1,0:T(8,128)(2,1)S(1)}, bf16[512,384]{1,0:T(8,128)(2,1)S(1)}, u32[]{:S(2)}, u32[]{:S(2)}) collective-permute-start(bf16[512,384]{1,0:T(8,128)(2,1)S(1)} %collective-permute-done.refs_4_), channel_id=1, source_target_pairs={{0,6},{2,0},{4,2},{6,4},{1,7},{3,1},{5,3},{7,5},{8,14},{10,8},{12,... | collective-permute-start | bytes 1179656 | tf_op jit(solution)/shard_map/ppermute | solution.py:22
  55.3 6.7 %copy-start.6 = (bf16[512,384]{1,0:T(8,128)(2,1)}, bf16[512,384]{1,0:T(8,128)(2,1)S(1)}, u32[]{:S(2)}) copy-start(bf16[512,384]{1,0:T(8,128)(2,1)S(1)} %collective-permute-done.3.refs_5_) | copy-start | bytes 1179652
  55.3 12.8 %copy-start.8 = (bf16[512,384]{1,0:T(8,128)(2,1)}, bf16[512,384]{1,0:T(8,128)(2,1)S(1)}, u32[]{:S(2)}) copy-start(bf16[512,384]{1,0:T(8,128)(2,1)S(1)} %collective-permute-done.4.refs_6_) | copy-start | bytes 1179652
  55.3 31.2 %collective-permute-start.10 = (bf16[6,192,384]{2,1,0:T(8,128)(2,1)}, bf16[6,192,384]{2,1,0:T(8,128)(2,1)}, u32[]{:S(2)}, u32[]{:S(2)}) collective-permute-start(bf16[6,192,384]{2,1,0:T(8,128)(2,1)} %collective-permute-done.7.refs_12_), channel_id=1, source_target_pairs={{0,16},{16,32},{32,48},{48,0},{1,17},{17,33},{33,49},{49,1},{2,18}... | collective-permute-start | bytes 2654216 | tf_op jit(solution)/shard_map/ppermute | solution.py:22
  57.4 29.2 %collective-permute-start.11 = (bf16[6,192,384]{2,1,0:T(8,128)(2,1)}, bf16[6,192,384]{2,1,0:T(8,128)(2,1)}, u32[]{:S(2)}, u32[]{:S(2)}) collective-permute-start(bf16[6,192,384]{2,1,0:T(8,128)(2,1)} %collective-permute-done.7.refs_12_), channel_id=1, source_target_pairs={{0,48},{16,0},{32,16},{48,32},{1,49},{17,1},{33,17},{49,33},{2,50}... | collective-permute-start | bytes 2654216 | tf_op jit(solution)/shard_map/ppermute | solution.py:22
  60.9 29.5 %copy-start.25 = (f32[3584]{0:T(1024)S(1)}, f32[3584]{0:T(1024)}, u32[]{:S(2)}) copy-start(f32[3584]{0:T(1024)} %param.20) | copy-start | bytes 43012
  62.0 24.5 %all-to-all-start.1 = ((bf16[8,128,448]{1,2,0:T(8,128)(2,1)}), bf16[8,128,448]{1,2,0:T(8,128)(2,1)}, u32[]{:S(2)}, u32[]{:S(2)}) async-start(bf16[8,128,448]{1,2,0:T(8,128)(2,1)} %broadcast_in_dim.4), calls=%async_computation.1 | async-start | bytes 1835008 | tf_op jit(solution)/shard_map/all_to_all | solution.py:32
  66.2 159.9 %all-gather.3.cloned.1.call-start = ((), (), s32[]{:S(2)}) async-start(), calls=%async_computation.4 | async-start | bytes 5013504 | tf_op jit(solution)/shard_map/all_gather | solution.py:375
  66.3 19.4 %collective-permute-start.8 = (bf16[512,384]{1,0:T(8,128)(2,1)S(1)}, bf16[512,384]{1,0:T(8,128)(2,1)S(1)}, u32[]{:S(2)}, u32[]{:S(2)}) collective-permute-start(bf16[512,384]{1,0:T(8,128)(2,1)S(1)} %collective-permute-done.1.refs_1_), channel_id=1, source_target_pairs={{0,2},{2,4},{4,6},{6,0},{1,3},{3,5},{5,7},{7,1},{8,10},{10,12},{12... | collective-permute-start | bytes 1179656 | tf_op jit(solution)/shard_map/ppermute | solution.py:22
  68.1 17.6 %collective-permute-start.9 = (bf16[512,384]{1,0:T(8,128)(2,1)S(1)}, bf16[512,384]{1,0:T(8,128)(2,1)S(1)}, u32[]{:S(2)}, u32[]{:S(2)}) collective-permute-start(bf16[512,384]{1,0:T(8,128)(2,1)S(1)} %collective-permute-done.4.refs_6_), channel_id=1, source_target_pairs={{0,6},{2,0},{4,2},{6,4},{1,7},{3,1},{5,3},{7,5},{8,14},{10,8},{12,... | collective-permute-start | bytes 1179656 | tf_op jit(solution)/shard_map/ppermute | solution.py:22
  69.6 1.6 collective-permute-start.12
  71.2 15.4 %copy-start.18 = (bf16[2,192,384]{2,1,0:T(8,128)(2,1)}, bf16[2,192,384]{2,1,0:T(8,128)(2,1)S(1)}, u32[]{:S(2)}) copy-start(bf16[2,192,384]{2,1,0:T(8,128)(2,1)S(1)} %collective-permute-done.12) | copy-start | bytes 884740
  85.7 9.0 %copy-start.10 = (bf16[512,384]{1,0:T(8,128)(2,1)}, bf16[512,384]{1,0:T(8,128)(2,1)S(1)}, u32[]{:S(2)}) copy-start(bf16[512,384]{1,0:T(8,128)(2,1)S(1)} %collective-permute-done.8.refs_3_) | copy-start | bytes 1179652
  86.6 22.8 %collective-permute-start.13 = (bf16[6,192,384]{2,1,0:T(8,128)(2,1)}, bf16[6,192,384]{2,1,0:T(8,128)(2,1)}, u32[]{:S(2)}, u32[]{:S(2)}) collective-permute-start(bf16[6,192,384]{2,1,0:T(8,128)(2,1)} %collective-permute-done.5.refs_9_), channel_id=1, source_target_pairs={{0,16},{16,32},{32,48},{48,0},{1,17},{17,33},{33,49},{49,1},{2,18}... | collective-permute-start | bytes 2654216 | tf_op jit(solution)/shard_map/ppermute | solution.py:22
  86.7 23.4 %collective-permute-start.14 = (bf16[6,192,384]{2,1,0:T(8,128)(2,1)}, bf16[6,192,384]{2,1,0:T(8,128)(2,1)}, u32[]{:S(2)}, u32[]{:S(2)}) collective-permute-start(bf16[6,192,384]{2,1,0:T(8,128)(2,1)} %collective-permute-done.11.refs_14_), channel_id=1, source_target_pairs={{0,48},{16,0},{32,16},{48,32},{1,49},{17,1},{33,17},{49,33},{2,50}... | collective-permute-start | bytes 2654216 | tf_op jit(solution)/shard_map/ppermute | solution.py:22
  89.9 23.3 %collective-permute-start.15 = (bf16[6,192,384]{2,1,0:T(8,128)(2,1)S(1)}, bf16[6,192,384]{2,1,0:T(8,128)(2,1)}, u32[]{:S(2)}, u32[]{:S(2)}) collective-permute-start(bf16[6,192,384]{2,1,0:T(8,128)(2,1)S(1)} %maximum_bitcast_fusion.refs_8_), channel_id=1, source_target_pairs={{0,8},{8,0},{1,9},{9,1},{2,10},{10,2},{3,11},{11,3},{4,12},{12,4},... | collective-permute-start | bytes 2654216 | tf_op jit(solution)/shard_map/ppermute | solution.py:22
  89.9 23.3 %collective-permute-start.19 = (bf16[6,192,384]{2,1,0:T(8,128)(2,1)}, bf16[6,192,384]{2,1,0:T(8,128)(2,1)}, u32[]{:S(2)}, u32[]{:S(2)}) collective-permute-start(bf16[6,192,384]{2,1,0:T(8,128)(2,1)} %collective-permute-done.7.refs_12_), channel_id=1, source_target_pairs={{0,8},{8,0},{1,9},{9,1},{2,10},{10,2},{3,11},{11,3},{4,12},{12,4},... | collective-permute-start | bytes 2654216 | tf_op jit(solution)/shard_map/ppermute | solution.py:22
  90.4 23.3 %collective-permute-start.16 = (bf16[6,192,384]{2,1,0:T(8,128)(2,1)}, bf16[6,192,384]{2,1,0:T(8,128)(2,1)}, u32[]{:S(2)}, u32[]{:S(2)}) collective-permute-start(bf16[6,192,384]{2,1,0:T(8,128)(2,1)} %collective-permute-done.5.refs_9_), channel_id=1, source_target_pairs={{0,8},{8,0},{1,9},{9,1},{2,10},{10,2},{3,11},{11,3},{4,12},{12,4},... | collective-permute-start | bytes 2654216 | tf_op jit(solution)/shard_map/ppermute | solution.py:22
  92.0 1.8 copy-start.2
  94.8 4.8 %copy-start.26 = (f32[128]{0:T(128)S(1)}, f32[128]{0:T(128)}, u32[]{:S(2)}) copy-start(f32[128]{0:T(128)} %param.26) | copy-start | bytes 1540
  94.8 4.8 %copy-start.27 = (f32[128]{0:T(128)S(1)}, f32[128]{0:T(128)}, u32[]{:S(2)}) copy-start(f32[128]{0:T(128)} %param.25) | copy-start | bytes 1540
  94.8 19.2 %copy-start.28 = (s32[128]{0:T(128)S(1)}, s32[128]{0:T(128)}, u32[]{:S(2)}) copy-start(s32[128]{0:T(128)} %param.31) | copy-start | bytes 1540
  95.8 17.4 %all-to-all-start.2 = ((bf16[8,128,384]{2,1,0:T(8,128)(2,1)}), bf16[8,128,384]{2,1,0:T(8,128)(2,1)S(1)}, u32[]{:S(2)}, u32[]{:S(2)}) async-start(bf16[8,128,384]{2,1,0:T(8,128)(2,1)} %broadcast_in_dim.5), calls=%async_computation.2 | async-start | bytes 1572864 | tf_op jit(solution)/shard_map/all_to_all | solution.py:32
  99.5 16.0 %copy-start.23 = (f32[4,3072]{1,0:T(4,128)S(1)}, f32[4,3072]{1,0:T(4,128)}, u32[]{:S(2)}) copy-start(f32[4,3072]{1,0:T(4,128)} %param.24) | copy-start | bytes 147460
  99.6 16.0 %copy-start.24 = (f32[4,3072]{1,0:T(4,128)S(1)}, f32[4,3072]{1,0:T(4,128)}, u32[]{:S(2)}) copy-start(f32[4,3072]{1,0:T(4,128)} %param.23) | copy-start | bytes 147460
  99.6 18.9 %copy-start.3 = (bf16[512,384]{1,0:T(8,128)(2,1)S(1)}, bf16[512,384]{1,0:T(8,128)(2,1)}, u32[]{:S(2)}) copy-start(bf16[512,384]{1,0:T(8,128)(2,1)} %refs_0_.1) | copy-start | bytes 1179652
  109.4 6.2 %collective-permute-start.21 = (bf16[6,192,384]{2,1,0:T(8,128)(2,1)}, bf16[6,192,384]{2,1,0:T(8,128)(2,1)}, u32[]{:S(2)}, u32[]{:S(2)}) collective-permute-start(bf16[6,192,384]{2,1,0:T(8,128)(2,1)} %collective-permute-done.11.refs_14_), channel_id=1, source_target_pairs={{0,8},{8,0},{1,9},{9,1},{2,10},{10,2},{3,11},{11,3},{4,12},{12,4},... | collective-permute-start | bytes 2654216 | tf_op jit(solution)/shard_map/ppermute | solution.py:22
  110.1 5.6 %collective-permute-start.17 = (bf16[6,192,384]{2,1,0:T(8,128)(2,1)}, bf16[6,192,384]{2,1,0:T(8,128)(2,1)}, u32[]{:S(2)}, u32[]{:S(2)}) collective-permute-start(bf16[6,192,384]{2,1,0:T(8,128)(2,1)} %collective-permute-done.6.refs_10_), channel_id=1, source_target_pairs={{0,8},{8,0},{1,9},{9,1},{2,10},{10,2},{3,11},{11,3},{4,12},{12,4},... | collective-permute-start | bytes 2654216 | tf_op jit(solution)/shard_map/ppermute | solution.py:22
  113.2 2.8 %collective-permute-start.20 = (bf16[6,192,384]{2,1,0:T(8,128)(2,1)}, bf16[6,192,384]{2,1,0:T(8,128)(2,1)}, u32[]{:S(2)}, u32[]{:S(2)}) collective-permute-start(bf16[6,192,384]{2,1,0:T(8,128)(2,1)} %collective-permute-done.10.refs_13_), channel_id=1, source_target_pairs={{0,8},{8,0},{1,9},{9,1},{2,10},{10,2},{3,11},{11,3},{4,12},{12,4},... | collective-permute-start | bytes 2654216 | tf_op jit(solution)/shard_map/ppermute | solution.py:22
  113.2 4.0 %collective-permute-start.18 = (bf16[6,192,384]{2,1,0:T(8,128)(2,1)}, bf16[6,192,384]{2,1,0:T(8,128)(2,1)}, u32[]{:S(2)}, u32[]{:S(2)}) collective-permute-start(bf16[6,192,384]{2,1,0:T(8,128)(2,1)} %collective-permute-done.13.refs_11_), channel_id=1, source_target_pairs={{0,8},{8,0},{1,9},{9,1},{2,10},{10,2},{3,11},{11,3},{4,12},{12,4},... | collective-permute-start | bytes 2654216 | tf_op jit(solution)/shard_map/ppermute | solution.py:22
  113.7 4.8 %collective-permute-start.22 = (bf16[6,192,384]{2,1,0:T(8,128)(2,1)}, bf16[6,192,384]{2,1,0:T(8,128)(2,1)}, u32[]{:S(2)}, u32[]{:S(2)}) collective-permute-start(bf16[6,192,384]{2,1,0:T(8,128)(2,1)} %collective-permute-done.14.refs_15_), channel_id=1, source_target_pairs={{0,8},{8,0},{1,9},{9,1},{2,10},{10,2},{3,11},{11,3},{4,12},{12,4},... | collective-permute-start | bytes 2654216 | tf_op jit(solution)/shard_map/ppermute | solution.py:22
  137.5 6.2 %collective-permute-start.24 = (bf16[640,384]{1,0:T(8,128)(2,1)S(1)}, bf16[640,384]{1,0:T(8,128)(2,1)S(1)}, u32[]{:S(2)}, u32[]{:S(2)}) collective-permute-start(bf16[640,384]{1,0:T(8,128)(2,1)S(1)} %get-tuple-element.98.refs_0_), channel_id=1, source_target_pairs={{0,8},{8,0},{1,9},{9,1},{2,10},{10,2},{3,11},{11,3},{4,12},{12,4},... | collective-permute-start | bytes 1474568 | tf_op jit(solution)/shard_map/ppermute | solution.py:22
  137.8 15.0 %collective-permute-start.23 = (bf16[640,384]{1,0:T(8,128)(2,1)S(1)}, bf16[640,384]{1,0:T(8,128)(2,1)S(1)}, u32[]{:S(2)}, u32[]{:S(2)}) collective-permute-start(bf16[640,384]{1,0:T(8,128)(2,1)S(1)} %get-tuple-element.98.refs_0_), channel_id=1, source_target_pairs={{0,64},{64,0},{1,65},{65,1},{2,66},{66,2},{3,67},{67,3},{4,68},{68... | collective-permute-start | bytes 1474568 | tf_op jit(solution)/shard_map/ppermute | solution.py:22
  140.5 27.6 %collective-permute-start.26 = (bf16[2,640,384]{2,1,0:T(8,128)(2,1)}, bf16[2,640,384]{2,1,0:T(8,128)(2,1)S(1)}, u32[]{:S(2)}, u32[]{:S(2)}) collective-permute-start(bf16[2,640,384]{2,1,0:T(8,128)(2,1)} %get-tuple-element.99.refs_2_.refs_3_), channel_id=1, source_target_pairs={{0,16},{16,32},{32,48},{48,0},{1,17},{17,33},{33,49},{49,1},{2,18}... | collective-permute-start | bytes 2949128 | tf_op jit(solution)/shard_map/ppermute | solution.py:22
  141.0 27.1 %collective-permute-start.27 = (bf16[2,640,384]{2,1,0:T(8,128)(2,1)}, bf16[2,640,384]{2,1,0:T(8,128)(2,1)S(1)}, u32[]{:S(2)}, u32[]{:S(2)}) collective-permute-start(bf16[2,640,384]{2,1,0:T(8,128)(2,1)} %get-tuple-element.99.refs_2_.refs_3_), channel_id=1, source_target_pairs={{0,48},{16,0},{32,16},{48,32},{1,49},{17,1},{33,17},{49,33},{2,50}... | collective-permute-start | bytes 2949128 | tf_op jit(solution)/shard_map/ppermute | solution.py:22
  143.7 1.2 copy-start.15
  144.9 9.7 %copy-start.16 = (bf16[2,640,384]{2,1,0:T(8,128)(2,1)S(1)}, bf16[2,640,384]{2,1,0:T(8,128)(2,1)}, u32[]{:S(2)}) copy-start(bf16[2,640,384]{2,1,0:T(8,128)(2,1)} %get-tuple-element.99.refs_2_.refs_3_) | copy-start | bytes 2949124
  152.8 1.9 collective-permute-start.25
  168.1 11.4 %copy-start.14 = (bf16[2,640,384]{2,1,0:T(8,128)(2,1)}, bf16[2,640,384]{2,1,0:T(8,128)(2,1)S(1)}, u32[]{:S(2)}) copy-start(bf16[2,640,384]{2,1,0:T(8,128)(2,1)S(1)} %collective-permute-done.27.refs_3_.refs_5_.refs_6_) | copy-start | bytes 2949124
  168.2 14.3 %collective-permute-start.28 = (bf16[640,384]{1,0:T(8,128)(2,1)S(1)}, bf16[640,384]{1,0:T(8,128)(2,1)S(1)}, u32[]{:S(2)}, u32[]{:S(2)}) collective-permute-start(bf16[640,384]{1,0:T(8,128)(2,1)S(1)} %slice_bitcast_fusion.1), channel_id=1, source_target_pairs={{0,16},{16,32},{32,48},{48,0},{1,17},{17,33},{33,49},{49,1},{2,18}... | collective-permute-start | bytes 1474568 | tf_op jit(solution)/shard_map/ppermute | solution.py:22
  168.6 13.9 %collective-permute-start.29 = (bf16[640,384]{1,0:T(8,128)(2,1)S(1)}, bf16[640,384]{1,0:T(8,128)(2,1)S(1)}, u32[]{:S(2)}, u32[]{:S(2)}) collective-permute-start(bf16[640,384]{1,0:T(8,128)(2,1)S(1)} %slice_bitcast_fusion), channel_id=1, source_target_pairs={{0,48},{16,0},{32,16},{48,32},{1,49},{17,1},{33,17},{49,33},{2,50}... | collective-permute-start | bytes 1474568 | tf_op jit(solution)/shard_map/ppermute | solution.py:22
  187.4 3.2 %collective-permute-start.30 = (f32[640,384]{1,0:T(8,128)S(1)}, f32[640,384]{1,0:T(8,128)S(1)}, u32[]{:S(2)}, u32[]{:S(2)}) collective-permute-start(f32[640,384]{1,0:T(8,128)S(1)} %get-tuple-element.126), channel_id=1, source_target_pairs={{0,8},{8,0},{1,9},{9,1},{2,10},{10,2},{3,11},{11,3},{4,12},{12,4},... | collective-permute-start | bytes 2949128 | tf_op jit(solution)/shard_map/ppermute | solution.py:22
  187.5 3.0 %collective-permute-start.31 = (f32[640,128]{1,0:T(8,128)S(1)}, f32[640,128]{1,0:T(8,128)S(1)}, u32[]{:S(2)}, u32[]{:S(2)}) collective-permute-start(f32[640,128]{1,0:T(8,128)S(1)} %get-tuple-element.128), channel_id=1, source_target_pairs={{0,8},{8,0},{1,9},{9,1},{2,10},{10,2},{3,11},{11,3},{4,12},{12,4},... | collective-permute-start | bytes 983048 | tf_op jit(solution)/shard_map/ppermute | solution.py:22
  190.9 18.4 %collective-permute-start.32 = (bf16[640,512]{1,0:T(8,128)(2,1)S(1)}, bf16[640,512]{1,0:T(8,128)(2,1)S(1)}, u32[]{:S(2)}, u32[]{:S(2)}) collective-permute-start(bf16[640,512]{1,0:T(8,128)(2,1)S(1)} %pad_maximum_fusion), channel_id=1, source_target_pairs={{0,64},{64,0},{1,65},{65,1},{2,66},{66,2},{3,67},{67,3},{4,68},{68... | collective-permute-start | bytes 1966088 | tf_op jit(solution)/shard_map/ppermute | solution.py:22
  209.2 3.0 %collective-permute-start.33 = (f32[640,384]{1,0:T(8,128)S(1)}, f32[640,384]{1,0:T(8,128)S(1)}, u32[]{:S(2)}, u32[]{:S(2)}) collective-permute-start(f32[640,384]{1,0:T(8,128)S(1)} %get-tuple-element.143), channel_id=1, source_target_pairs={{0,8},{8,0},{1,9},{9,1},{2,10},{10,2},{3,11},{11,3},{4,12},{12,4},... | collective-permute-start | bytes 2949128 | tf_op jit(solution)/shard_map/ppermute | solution.py:22
  209.2 3.0 %collective-permute-start.34 = (f32[640,128]{1,0:T(8,128)S(1)}, f32[640,128]{1,0:T(8,128)S(1)}, u32[]{:S(2)}, u32[]{:S(2)}) collective-permute-start(f32[640,128]{1,0:T(8,128)S(1)} %get-tuple-element.146), channel_id=1, source_target_pairs={{0,8},{8,0},{1,9},{9,1},{2,10},{10,2},{3,11},{11,3},{4,12},{12,4},... | collective-permute-start | bytes 983048 | tf_op jit(solution)/shard_map/ppermute | solution.py:22
  212.8 13.3 %collective-permute-start.35 = (bf16[640,384]{1,0:T(8,128)(2,1)S(1)}, bf16[640,384]{1,0:T(8,128)(2,1)S(1)}, u32[]{:S(2)}, u32[]{:S(2)}) collective-permute-start(bf16[640,384]{1,0:T(8,128)(2,1)S(1)} %combine.1.own_ref), channel_id=1, source_target_pairs={{0,1},{1,0},{2,3},{3,2},{4,5},{5,4},{6,7},{7,6},{8,9},{9,8},{10,11... | collective-permute-start | bytes 1474568 | tf_op jit(solution)/shard_map/ppermute | solution.py:22
  232.1 29.2 %all-to-all-start.3 = ((bf16[4,640,384]{2,1,0:T(8,128)(2,1)}), bf16[4,640,384]{2,1,0:T(8,128)(2,1)}, u32[]{:S(2)}, u32[]{:S(2)}) async-start(bf16[4,640,384]{2,1,0:T(8,128)(2,1)} %out_projection.1), calls=%async_computation.3 | async-start | bytes 3932160 | tf_op jit(solution)/shard_map/all_to_all | solution.py:431
  236.6 26.7 %copy-start.22 = (bf16[128,384]{1,0:T(8,128)(2,1)S(1)}, bf16[128,384]{1,0:T(8,128)(2,1)}, u32[]{:S(2)}) copy-start(bf16[128,384]{1,0:T(8,128)(2,1)} %param.33) | copy-start | bytes 294916
  236.6 27.4 %copy-start.17 = (bf16[512,384]{1,0:T(8,128)(2,1)S(1)}, bf16[512,384]{1,0:T(8,128)(2,1)}, u32[]{:S(2)}) copy-start(bf16[512,384]{1,0:T(8,128)(2,1)} %param.32) | copy-start | bytes 1179652
  261.3 3.6 %copy-start.1 = (bf16[128,1280]{1,0:T(8,128)(2,1)S(1)}, bf16[128,1280]{1,0:T(8,128)(2,1)}, u32[]{:S(2)}) copy-start(bf16[128,1280]{1,0:T(8,128)(2,1)} %param.17) | copy-start | bytes 983044
  (6 other events, 5.8 us)
Sparse Core Ops, SparseCore 0:
  86.7 65.0 all-gather.2

commit v2 on v1

--- a/solution.py
+++ b/solution.py
@@ -71,53 +71,84 @@
     )(state, gain.reshape(parts, 1, share), proj.reshape(parts, share, proj.shape[1]))
 
 
-def qkv_kernel(a_index, count, place_ref, mod_ref, cos_ref, sin_ref, gain_ref, text_ref, *refs):
-    arrays = a_index[-1][0] + 1
-    a_arrays, w_pieces, refs = refs[:arrays], refs[arrays : arrays + count], refs[arrays + count :]
-    q_ref, kv_ref, states, modded, weight, sems = refs
+def normalise(states, mod_ref, out_ref, first):
     parts, rows, share = states.shape
     width = parts * share
+    tile = 64
+
+    @pl.loop(0, rows // tile)
+    def _(step):
+        here = pl.ds(pl.multiple_of(step * tile, tile), tile)
+        there = pl.ds(pl.multiple_of(first + step * tile, tile), tile)
+        total = jnp.zeros((tile, share), F32)
+        for t in range(parts):
+            total += states[t, here, :].astype(F32)
+        center = jnp.sum(total, axis=-1, keepdims=True) / width
+        total = jnp.zeros((tile, share), F32)
+        for t in range(parts):
+            shifted = states[t, here, :].astype(F32) - center
+            total += shifted * shifted
+        factor = lax.rsqrt(jnp.sum(total, axis=-1, keepdims=True) / width + EPS)
+        for t in range(parts):
+            cols = slice(t * share, (t + 1) * share)
+            shifted = states[t, here, :].astype(F32) - center
+            normed = shifted * factor * (1.0 + mod_ref[1:2, cols]) + mod_ref[0:1, cols]
+            out_ref[there, cols] = normed.astype(BF)
+
+
+def modulate_kernel(count, place_ref, mod_ref, *refs):
+    pieces, (out_ref, states, sems) = refs[:count], refs[count:]
+    copies = [
+        pltpu.make_async_copy(piece, states.at[place_ref[i]], sems.at[i])
+        for i, piece in enumerate(pieces)
+    ]
+    for copy in copies:
+        copy.start()
+    for copy in copies:
+        copy.wait()
+    normalise(states, mod_ref, out_ref, 0)
+
+
+def modulate(pieces, places, mod):
+    rows, share = pieces[0].shape
+    count = len(pieces)
+    return pl.pallas_call(
+        functools.partial(modulate_kernel, count),
+        out_shape=jax.ShapeDtypeStruct((rows, count * share), BF),
+        in_specs=[SMEM, VMEM] + [ANY] * count,
+        out_specs=VMEM,
+        scratch_shapes=[
+            pltpu.VMEM((count, rows, share), BF),
+            pltpu.SemaphoreType.DMA((count,)),
+        ],
+        compiler_params=params(),
+        name="modulate",
+    )(table(places), mod, *pieces)
+
+
+def qkv_kernel(count, place_ref, mod_ref, cos_ref, sin_ref, gain_ref, image_ref, *refs):
+    text_ref, w_pieces, refs = refs[0], refs[1 : 1 + count], refs[1 + count :]
+    q_ref, kv_ref, states, modded, weight, sems = refs
+    share = states.shape[2]
+    rows, width = modded.shape
     depth = width // 16
-    image_rows = rows // 5 * 4
-    a_copies, w_copies = [], ([], [])
-    for i, (array, index) in enumerate(a_index):
-        dst = states.at[place_ref[i], pl.ds(0, image_rows)]
-        a_copies.append(pltpu.make_async_copy(a_arrays[array].at[index], dst, sems.at[i]))
-    dst = states.at[:, pl.ds(image_rows, rows - image_rows)]
-    a_copies.append(pltpu.make_async_copy(text_ref, dst, sems.at[8]))
+    image_rows = image_ref.shape[0]
+    image_copy = pltpu.make_async_copy(
+        image_ref, modded.at[pl.ds(0, image_rows)], sems.at[2 * count]
+    )
+    text_copy = pltpu.make_async_copy(text_ref, states, sems.at[2 * count + 1])
+    w_copies = ([], [])
     for stream in range(2):
         for i, piece in enumerate(w_pieces):
-            start = pl.multiple_of(place_ref[8 + i] * depth, depth)
+            start = pl.multiple_of(place_ref[i] * depth, depth)
             src = piece.at[pl.ds(3 * stream, 3)]
             dst = weight.at[pl.ds(3 * stream, 3), pl.ds(start, depth), :]
-            sem = sems.at[9 + count * stream + i]
+            sem = sems.at[count * stream + i]
             w_copies[stream].append(pltpu.make_async_copy(src, dst, sem))
-    for copy in a_copies + w_copies[0] + w_copies[1]:
+    for copy in [text_copy, image_copy] + w_copies[0] + w_copies[1]:
         copy.start()
-    for copy in a_copies:
-        copy.wait()
-
-    tile = 64
-
-    def modulate(first, last, stream):
-        @pl.loop(first // tile, last // tile)
-        def _(step):
-            here = pl.ds(pl.multiple_of(step * tile, tile), tile)
-            total = jnp.zeros((tile, share), F32)
-            for t in range(parts):
-                total += states[t, here, :].astype(F32)
-            center = jnp.sum(total, axis=-1, keepdims=True) / width
-            total = jnp.zeros((tile, share), F32)
-            for t in range(parts):
-                shifted = states[t, here, :].astype(F32) - center
-                total += shifted * shifted
-            factor = lax.rsqrt(jnp.sum(total, axis=-1, keepdims=True) / width + EPS)
-            for t in range(parts):
-                cols = slice(t * share, (t + 1) * share)
-                shifted = states[t, here, :].astype(F32) - center
-                gain = 1.0 + mod_ref[stream, 1:2, cols]
-                normed = shifted * factor * gain + mod_ref[stream, 0:1, cols]
-                modded[here, cols] = normed.astype(BF)
+    text_copy.wait()
+    normalise(states, mod_ref, modded, image_rows)
 
     def prepare(flat, gain, cosine, sine):
         outs = []
@@ -138,8 +169,7 @@
         kv_ref[0, here, :] = prepare(product(1), gain_ref[1:2, :], cosine, sine).astype(BF)
         kv_ref[1, here, :] = product(2).astype(BF)
 
-    modulate(0, image_rows, 0)
-    modulate(image_rows, rows, 1)
+    image_copy.wait()
     for copy in w_copies[0]:
         copy.wait()
     chunk = image_rows // 2
@@ -153,28 +183,28 @@
     project(pl.ds(image_rows, rows - image_rows), 1)
 
 
-def qkv(a_arrays, a_index, a_places, text_a, w_pieces, w_places, mods, cosine, sine, gains):
+def qkv(image, text_a, w_pieces, w_places, mod, cosine, sine, gains):
     parts, text_rows, share = text_a.shape
-    rows = a_arrays[0].shape[-2] + text_rows
-    width = parts * share
-    arrays, count = len(a_arrays), len(w_pieces)
+    image_rows, width = image.shape
+    rows = image_rows + text_rows
+    count = len(w_pieces)
     return pl.pallas_call(
-        functools.partial(qkv_kernel, a_index, count),
+        functools.partial(qkv_kernel, count),
         out_shape=(
             jax.ShapeDtypeStruct((rows, share), BF),
             jax.ShapeDtypeStruct((2, rows, share), BF),
         ),
-        in_specs=[SMEM, VMEM, VMEM, VMEM, VMEM] + [ANY] * (1 + arrays + count),
+        in_specs=[SMEM, VMEM, VMEM, VMEM, VMEM] + [ANY] * (2 + count),
         out_specs=(VMEM, VMEM),
         scratch_shapes=[
-            pltpu.VMEM((parts, rows, share), BF),
+            pltpu.VMEM((parts, text_rows, share), BF),
             pltpu.VMEM((rows, width), BF),
             pltpu.VMEM((6, width, share), BF),
-            pltpu.SemaphoreType.DMA((9 + 2 * count,)),
+            pltpu.SemaphoreType.DMA((2 * count + 2,)),
         ],
         compiler_params=params(),
         name="qkv",
-    )(table(a_places + w_places), mods, cosine, sine, gains, text_a, *a_arrays, *w_pieces)
+    )(table(w_places), mod, cosine, sine, gains, image, text_a, *w_pieces)
 
 
 def attention_kernel(nq, k_sizes, first, *refs):
@@ -345,10 +375,17 @@
     outs = jnp.stack([jnp.transpose(image_out), jnp.transpose(text_out)])
     weight = jnp.transpose(jnp.concatenate([image_qkv, text_qkv], axis=1), (1, 0, 2))
 
+    turned = [
+        (4 * zh + 2 * zl + y, 4 * zh + 2 * y + zl)
+        for zh in range(2)
+        for zl in range(2)
+        for y in range(2)
+    ]
+    outs = lax.ppermute(outs, ("z", "yl"), turned)
     a_pair = shift(image_states, "yl", 1)
     a_near = near(image_states, "x")
     w_pair = shift(weight, "yh", 1)
-    cond_hidden, a_pair, a_near = together((cond_hidden, a_pair, a_near))
+    cond_hidden, a_pair, a_near, outs = together((cond_hidden, a_pair, a_near, outs))
 
     w_near = near(weight, "z")
     a_next = near(a_pair, "x")
@@ -360,29 +397,23 @@
         (got, a_near, a_next, w_near, w_pair, outs)
     )
 
+    out_w = lax.all_gather(outs, SEQ)
     a_far = (shift(a_near[0], "x", 1), shift(a_next[1], "x", -1))
     w_next = near(w_pair, "z")
-    turned = [
-        (4 * zh + 2 * zl + y, 4 * zh + 2 * y + zl)
-        for zh in range(2)
-        for zl in range(2)
-        for y in range(2)
-    ]
-    outs = lax.ppermute(outs, ("z", "yl"), turned)
     cond_state = (jnp.sum(got.astype(F32), axis=0) + cond_resid.astype(F32)).astype(BF)
     state = spread(cond_state, TP)
-    state, a_far, w_near, w_next, outs = together((state, a_far, w_near, w_next, outs))
-    out_w = lax.all_gather(outs, SEQ)
+    state, a_far, w_near, w_next = together((state, a_far, w_near, w_next))
 
     text_states = text_projection(state, cond_gain, text_proj)
     text_a = spread(text_states, TP)
     w_far = (shift(w_near[0], "z", 1), shift(w_next[1], "z", -1))
-    text_a, w_far = together((text_a, w_far))
 
     blocks = [(p, d) for p in range(2) for d in (0, 3, 1, 2)]
     a_arrays = [image_states, *a_near, a_far[0], a_pair, *a_next, a_far[1]]
-    a_index = tuple((i, ()) for i in range(8))
     a_places = [(x + d) % 4 * 2 + (yl + p) % 2 for p, d in blocks]
+    image_modded = modulate(a_arrays, a_places, image_mod)
+    text_a, w_far, image_modded = together((text_a, w_far, image_modded))
+
     w_arrays = [weight, *w_near, w_far[0], w_pair, *w_next, w_far[1]]
     w_arrays += [shift(w, "c", 1) for w in w_arrays]
 
@@ -392,13 +423,11 @@
         (yh + p) % 2 * 8 + (z + d) % 4 * 2 + (c + k) % 2 for k in range(2) for p, d in blocks
     ]
     query, kv = qkv(
-        a_arrays,
-        a_index,
-        a_places,
+        image_modded,
         text_a,
         w_arrays,
         w_places,
-        jnp.stack([image_mod, text_mod]),
+        text_mod,
         *angles_of(jnp.concatenate([image_pos, cond_pos.astype(F32)])),
         gains,
     )

time: 273 us -> 275 us (level)
  waiting for transfers between devices: 114 us -> 96.4 us
  starting transfers between devices: 58.4 us -> 69.6 us
  Pallas kernels: 54.6 us -> 59.3 us
  local copies, waits for them, and re-layouts: 15.1 us -> 18.4 us
    ppermute x35, waiting for transfers between devices: 86.6 us -> 70.7 us  [shift(): lax.ppermute(value, axis, [(k, (k + step) % size) for k in range(size)])]
    ppermute x35, starting transfers between devices: 39.8 us -> 51.1 us  [shift(): lax.ppermute(value, axis, [(k, (k + step) % size) for k in range(size)])]
    pallas_call x1 -> x2, Pallas kernels: 14.1 us -> 18.8 us  [the longest x1 12.4 us: qkv(): pl.pallas_call(functools.partial(qkv_kernel, count), out_shape=(jax.Shape...]
    unnamed x58 -> x60, local copies, waits for them, and re-layouts: 8.92 us -> 12.2 us
  transfers between devices with their start and end apart: 41 -> 41, of which waited for: 18 -> 17; matrix products, arithmetic and copies ran while one was open for 6% -> 7% of each run, Pallas kernels for 18% -> 20%
where the time goes in v2:
time: 275 us; the launch traced here: 273 us
  waiting for transfers between devices  96.4 us (35%)
  starting transfers between devices  69.6 us (25%)
  Pallas kernels  59.3 us (22%)
  local copies, waits for them, and re-layouts  18.4 us (7%)
  between operations  14.5 us (5%)
  other arithmetic  8.99 us (3%)
  matrix products  6.13 us (2%)
    ppermute x35, waiting for transfers between devices, shift(): lax.ppermute(value, axis, [(k, (k + step) % size) for k in range(size)])  70.7 us
    ppermute x35, starting transfers between devices, shift(): lax.ppermute(value, axis, [(k, (k + step) % size) for k in range(size)])  51.1 us
    pallas_call x5, Pallas kernels, attention(): pl.pallas_call(functools.partial(attention_kernel, nq, k_sizes, not befor...  33 us
    all_to_all x1, waiting for transfers between devices, shards(): got = lax.all_to_all(parts, 'x', split_axis=0, concat_axis=0, tiled=True)  24.8 us
    pallas_call x1, Pallas kernels, qkv(): pl.pallas_call(functools.partial(qkv_kernel, count), out_shape=(jax.Shape...  12.4 us
    unnamed x60, local copies, waits for them, and re-layouts  12.2 us
    all_to_all x2, starting transfers between devices, spread(): return lax.all_to_all(copies, axes, split_axis=0, concat_axis=0, tiled=True)  8.96 us
    pallas_call x1, Pallas kernels, modulate(): pl.pallas_call(functools.partial(modulate_kernel, count), out_shape=jax.S...  6.44 us
  transfers between devices with their start and end apart: 41, of which 17 were waited for; matrix products, arithmetic and copies ran while one was open for 7% of the time, Pallas kernels for 20%

profile of v2, /device:TPU:0, one launch (start us, length us, event | category | flops | bytes accessed | tf_op | source)
XLA Modules:
  0.0 273.3 jit_solution(4327137486873779427)
XLA Ops:
  7.2 1.7 collective-permute-start
  8.9 1.5 collective-permute-start.1
  10.4 1.7 collective-permute-start.2
  12.2 1.0 pad_maximum_fusion.3
  13.9 1.3 maximum_bitcast_fusion.refs_1_
  15.1 3.2 %collective-permute-start.6 = (bf16[6,192,384]{2,1,0:T(8,128)(2,1)S(1)}, bf16[6,192,384]{2,1,0:T(8,128)(2,1)S(1)}, u32[]{:S(2)}, u32[]{:S(2)}) collective-permute-start(bf16[6,192,384]{2,1,0:T(8,128)(2,1)S(1)} %maximum_bitcast_fusion.refs_1_), channel_id=1, source_target_pairs={{0,16},{16,32},{32,48},{48,0},{1,17},{17,33},{33,49},{49,1},{2,18}... | collective-permute-start | bytes 2654216 | tf_op jit(solution)/shard_map/ppermute | solution.py:22
  18.4 10.4 %collective-permute-start.7 = (bf16[6,192,384]{2,1,0:T(8,128)(2,1)S(1)}, bf16[6,192,384]{2,1,0:T(8,128)(2,1)}, u32[]{:S(2)}, u32[]{:S(2)}) collective-permute-start(bf16[6,192,384]{2,1,0:T(8,128)(2,1)S(1)} %maximum_bitcast_fusion.refs_1_), channel_id=1, source_target_pairs={{0,48},{16,0},{32,16},{48,32},{1,49},{17,1},{33,17},{49,33},{2,50}... | collective-permute-start | bytes 2654216 | tf_op jit(solution)/shard_map/ppermute | solution.py:22
  28.7 3.2 %collective-permute-start.8 = (bf16[6,192,384]{2,1,0:T(8,128)(2,1)S(1)}, bf16[6,192,384]{2,1,0:T(8,128)(2,1)}, u32[]{:S(2)}, u32[]{:S(2)}) collective-permute-start(bf16[6,192,384]{2,1,0:T(8,128)(2,1)S(1)} %maximum_bitcast_fusion.refs_1_), channel_id=1, source_target_pairs={{0,64},{64,0},{1,65},{65,1},{2,66},{66,2},{3,67},{67,3},{4,68},{68... | collective-permute-start | bytes 2654216 | tf_op jit(solution)/shard_map/ppermute | solution.py:22
  31.9 6.1 %convolution_convert_fusion = bf16[128,3584]{1,0:T(8,128)(2,1)} fusion(bf16[128,1280]{1,0:T(8,128)(2,1)S(1)} %copy-done, bf16[1280,3584]{1,0:T(8,128)(2,1)} %param.18), kind=kOutput, calls=%fused_computation | convolution fusion | flops 1174863872 | bytes 10420224 | tf_op jit(solution)/shard_map/dot_general | solution.py:392
  38.1 2.2 copy.34
  40.3 4.4 %all-to-all-start = ((bf16[8,128,448]{1,2,0:T(8,128)(2,1)}), bf16[8,128,448]{1,2,0:T(8,128)(2,1)}, u32[]{:S(2)}, u32[]{:S(2)}) async-start(bf16[8,128,448]{1,2,0:T(8,128)(2,1)} %bitcast.55), calls=%async_computation | async-start | bytes 1835008 | tf_op jit(solution)/shard_map/all_to_all | solution.py:395
  44.7 2.0 collective-permute-start.4
  46.7 1.3 collective-permute-start.5
  48.1 17.2 %collective-permute-done.4.refs_5_ = bf16[512,384]{1,0:T(8,128)(2,1)S(1)} collective-permute-done((bf16[512,384]{1,0:T(8,128)(2,1)S(1)}, bf16[512,384]{1,0:T(8,128)(2,1)S(1)}, u32[]{:S(2)}, u32[]{:S(2)}) %collective-permute-start.4) | collective-permute-done | bytes 393248 | tf_op jit(solution)/shard_map/ppermute | solution.py:22
  65.2 0.8 copy-done.8
  66.1 0.8 copy-done.10
  66.9 3.2 %collective-permute-start.12 = (bf16[6,192,384]{2,1,0:T(8,128)(2,1)}, bf16[6,192,384]{2,1,0:T(8,128)(2,1)}, u32[]{:S(2)}, u32[]{:S(2)}) collective-permute-start(bf16[6,192,384]{2,1,0:T(8,128)(2,1)} %collective-permute-done.8.refs_5_), channel_id=1, source_target_pairs={{0,48},{16,0},{32,16},{48,32},{1,49},{17,1},{33,17},{49,33},{2,50}... | collective-permute-start | bytes 2654216 | tf_op jit(solution)/shard_map/ppermute | solution.py:22
  70.1 1.3 convert_reduce_fusion.1
  71.5 1.1 broadcast_in_dim.4
  72.5 4.2 %all-to-all-start.1 = ((bf16[8,128,448]{1,2,0:T(8,128)(2,1)}), bf16[8,128,448]{1,2,0:T(8,128)(2,1)}, u32[]{:S(2)}, u32[]{:S(2)}) async-start(bf16[8,128,448]{1,2,0:T(8,128)(2,1)} %broadcast_in_dim.4), calls=%async_computation.1 | async-start | bytes 1835008 | tf_op jit(solution)/shard_map/all_to_all | solution.py:32
  76.8 3.1 %collective-permute-start.10 = (bf16[512,384]{1,0:T(8,128)(2,1)S(1)}, bf16[512,384]{1,0:T(8,128)(2,1)S(1)}, u32[]{:S(2)}, u32[]{:S(2)}) collective-permute-start(bf16[512,384]{1,0:T(8,128)(2,1)S(1)} %copy-done.11), channel_id=1, source_target_pairs={{0,6},{2,0},{4,2},{6,4},{1,7},{3,1},{5,3},{7,5},{8,14},{10,8},{12,... | collective-permute-start | bytes 1179656 | tf_op jit(solution)/shard_map/ppermute | solution.py:22
  79.9 14.7 %collective-permute-done.10.refs_7_ = bf16[512,384]{1,0:T(8,128)(2,1)S(1)} collective-permute-done((bf16[512,384]{1,0:T(8,128)(2,1)S(1)}, bf16[512,384]{1,0:T(8,128)(2,1)S(1)}, u32[]{:S(2)}, u32[]{:S(2)}) %collective-permute-start.10) | collective-permute-done | bytes 393248 | tf_op jit(solution)/shard_map/ppermute | solution.py:22
  96.6 3.2 %collective-permute-start.14 = (bf16[6,192,384]{2,1,0:T(8,128)(2,1)}, bf16[6,192,384]{2,1,0:T(8,128)(2,1)}, u32[]{:S(2)}, u32[]{:S(2)}) collective-permute-start(bf16[6,192,384]{2,1,0:T(8,128)(2,1)} %collective-permute-done.12.refs_7_), channel_id=1, source_target_pairs={{0,48},{16,0},{32,16},{48,32},{1,49},{17,1},{33,17},{49,33},{2,50}... | collective-permute-start | bytes 2654216 | tf_op jit(solution)/shard_map/ppermute | solution.py:22
  100.4 1.5 copy.35.state_ref
  101.9 1.8 copy-done.2
  103.7 1.0 text_projection.1
  104.7 1.0 broadcast_in_dim.5
  105.7 4.7 %all-to-all-start.2 = ((bf16[8,128,384]{2,1,0:T(8,128)(2,1)}), bf16[8,128,384]{2,1,0:T(8,128)(2,1)S(1)}, u32[]{:S(2)}, u32[]{:S(2)}) async-start(bf16[8,128,384]{2,1,0:T(8,128)(2,1)} %broadcast_in_dim.5), calls=%async_computation.2 | async-start | bytes 1572864 | tf_op jit(solution)/shard_map/all_to_all | solution.py:32
  110.5 1.0 copy-done.5
  111.5 1.0 copy-done.7
  112.5 1.0 copy-done.9
  113.5 1.0 copy-done.12
  114.5 1.0 copy-done.14
  115.5 1.0 copy-done.16
  116.5 6.4 %modulate.1.image_ref = bf16[512,3072]{1,0:T(8,128)(2,1)} custom-call(s32[8]{0:T(128)S(1)} %stack.131.place_ref, f32[4,3072]{1,0:T(4,128)S(1)} %copy-done.19, bf16[512,384]{1,0:T(8,128)(2,1)S(1)} %copy-done.3, bf16[512,384]{1,0:T(8,128)(2,1)S(1)} %copy-done.7, bf16[512,384]{1,0:T(8,128)(2,1)} %collective-permute-done.2.refs_2_, ...), custom_call_target="tpu_custom_call" | custom-call | tf_op jit(solution)/shard_map/modulate/pallas_call | solution.py:115
  123.6 0.9 all-to-all-done.2.refs_0_
  125.4 1.2 fusion.7
  127.1 1.3 collective-permute-done.20.refs_14_
  128.3 1.4 collective-permute-done.18.refs_12_
  129.7 1.3 collective-permute-done.22.refs_16_
  131.0 12.4 %qkv.1 = (bf16[640,384]{1,0:T(8,128)(2,1)S(1)}, bf16[2,640,384]{2,1,0:T(8,128)(2,1)}) custom-call(s32[16]{0:T(128)S(1)} %stack.116.place_ref, f32[4,3072]{1,0:T(4,128)S(1)} %copy-done.18, f32[640,128]{1,0:T(8,128)S(1)} %get-tuple-element.159.cos_ref, f32[640,128]{1,0:T(8,128)S(1)} %get-tuple-element.160.sin_ref, f32[2,128]{1,0:T(2,128)S(1)} %pad_maximum_fusion.5.gain_ref, ...), custom_call_target="tpu_custom_call" | custom-call | tf_op jit(solution)/shard_map/qkv/pallas_call | solution.py:191
  144.2 3.2 %collective-permute-start.27 = (bf16[2,640,384]{2,1,0:T(8,128)(2,1)}, bf16[2,640,384]{2,1,0:T(8,128)(2,1)S(1)}, u32[]{:S(2)}, u32[]{:S(2)}) collective-permute-start(bf16[2,640,384]{2,1,0:T(8,128)(2,1)} %get-tuple-element.101.refs_2_.refs_3_), channel_id=1, source_target_pairs={{0,48},{16,0},{32,16},{48,32},{1,49},{17,1},{33,17},{49,33},{2,50}... | collective-permute-start | bytes 2949128 | tf_op jit(solution)/shard_map/ppermute | solution.py:22
  147.5 1.2 copy-done.20
  148.7 4.7 %attention.5 = (f32[640,384]{1,0:T(8,128)S(1)}, f32[640,384]{1,0:T(8,128)S(1)}, f32[640,128]{1,0:T(8,128)S(1)}, f32[640,128]{1,0:T(8,128)S(1)}) custom-call(bf16[640,384]{1,0:T(8,128)(2,1)S(1)} %get-tuple-element.100.refs_0_, bf16[640,384]{1,0:T(8,128)(2,1)S(1)} %collective-permute-done.24.refs_1_, bf16[2,640,384]{2,1,0:T(8,128)(2,1)S(1)} %copy-done.20, ...), custom_call_target="tpu_custom_call" | custom-call | flops 2516582400 | bytes 3932160 | tf_op jit(solution)/shard_map/attention/pallas_call | solution.py:259
  153.4 5.2 %collective-permute-done.23.refs_0_ = bf16[640,384]{1,0:T(8,128)(2,1)S(1)} collective-permute-done((bf16[640,384]{1,0:T(8,128)(2,1)S(1)}, bf16[640,384]{1,0:T(8,128)(2,1)S(1)}, u32[]{:S(2)}, u32[]{:S(2)}) %collective-permute-start.23) | collective-permute-done | bytes 491552 | tf_op jit(solution)/shard_map/ppermute | solution.py:22
  158.6 1.9 collective-permute-done.25.refs_1_
  160.5 4.7 %attention.6 = (f32[640,384]{1,0:T(8,128)S(1)}, f32[640,384]{1,0:T(8,128)S(1)}, f32[640,128]{1,0:T(8,128)S(1)}, f32[640,128]{1,0:T(8,128)S(1)}) custom-call(bf16[640,384]{1,0:T(8,128)(2,1)S(1)} %collective-permute-done.23.refs_0_, bf16[640,384]{1,0:T(8,128)(2,1)S(1)} %collective-permute-done.25.refs_1_, bf16[2,640,384]{2,1,0:T(8,128)(2,1)S(1)} %copy-done.21, ...), custom_call_target="tpu_custom_call" | custom-call | flops 2516582400 | bytes 3932160 | tf_op jit(solution)/shard_map/attention/pallas_call | solution.py:259
  165.2 4.1 %collective-permute-done.26.refs_2_.refs_4_.refs_5_ = bf16[2,640,384]{2,1,0:T(8,128)(2,1)S(1)} collective-permute-done((bf16[2,640,384]{2,1,0:T(8,128)(2,1)}, bf16[2,640,384]{2,1,0:T(8,128)(2,1)S(1)}, u32[]{:S(2)}, u32[]{:S(2)}) %collective-permute-start.26) | collective-permute-done | bytes 983072 | tf_op jit(solution)/shard_map/ppermute | solution.py:22
  169.5 3.5 %collective-permute-start.29 = (bf16[640,384]{1,0:T(8,128)(2,1)S(1)}, bf16[640,384]{1,0:T(8,128)(2,1)S(1)}, u32[]{:S(2)}, u32[]{:S(2)}) collective-permute-start(bf16[640,384]{1,0:T(8,128)(2,1)S(1)} %slice_bitcast_fusion), channel_id=1, source_target_pairs={{0,48},{16,0},{32,16},{48,32},{1,49},{17,1},{33,17},{49,33},{2,50}... | collective-permute-start | bytes 1474568 | tf_op jit(solution)/shard_map/ppermute | solution.py:22
  173.0 7.7 %attention.7 = (f32[640,384]{1,0:T(8,128)S(1)}, f32[640,384]{1,0:T(8,128)S(1)}, f32[640,128]{1,0:T(8,128)S(1)}, f32[640,128]{1,0:T(8,128)S(1)}) custom-call(bf16[640,384]{1,0:T(8,128)(2,1)S(1)} %collective-permute-done.23.refs_0_, ...), custom_call_target="tpu_custom_call", output_to_operand_aliasing={{0}: (6, {}), {1}: (7, {}), {2}: (8, {}), {3}: (9, {})} | custom-call | flops 5033164800 | bytes 3932160 | tf_op jit(solution)/shard_map/attention/pallas_call | solution.py:259
  180.7 2.2 collective-permute-done.28
  182.8 4.9 %attention.8 = (f32[640,384]{1,0:T(8,128)S(1)}, f32[640,384]{1,0:T(8,128)S(1)}, f32[640,128]{1,0:T(8,128)S(1)}, f32[640,128]{1,0:T(8,128)S(1)}) custom-call(bf16[640,384]{1,0:T(8,128)(2,1)S(1)} %collective-permute-done.23.refs_0_, ...), custom_call_target="tpu_custom_call", output_to_operand_aliasing={{0}: (4, {}), {1}: (5, {}), {2}: (6, {}), {3}: (7, {})} | custom-call | flops 2516582400 | bytes 3932160 | tf_op jit(solution)/shard_map/attention/pallas_call | solution.py:259
  188.3 2.5 collective-permute-done.31
  191.2 3.0 %collective-permute-start.32 = (bf16[640,512]{1,0:T(8,128)(2,1)S(1)}, bf16[640,512]{1,0:T(8,128)(2,1)S(1)}, u32[]{:S(2)}, u32[]{:S(2)}) collective-permute-start(bf16[640,512]{1,0:T(8,128)(2,1)S(1)} %pad_maximum_fusion), channel_id=1, source_target_pairs={{0,64},{64,0},{1,65},{65,1},{2,66},{66,2},{3,67},{67,3},{4,68},{68... | collective-permute-start | bytes 1966088 | tf_op jit(solution)/shard_map/ppermute | solution.py:22
  194.2 11.0 %attention.9 = (f32[640,384]{1,0:T(8,128)S(1)}, f32[640,384]{1,0:T(8,128)S(1)}, f32[640,128]{1,0:T(8,128)S(1)}, f32[640,128]{1,0:T(8,128)S(1)}) custom-call(bf16[640,384]{1,0:T(8,128)(2,1)S(1)} %get-tuple-element.100.refs_0_, ...), custom_call_target="tpu_custom_call", output_to_operand_aliasing={{0}: (8, {}), {1}: (9, {}), {2}: (10, {}), {3}: (11, {})} | custom-call | flops 7549747200 | bytes 3932160 | tf_op jit(solution)/shard_map/attention/pallas_call | solution.py:259
  205.2 4.3 %collective-permute-done.32.back_ref = bf16[640,512]{1,0:T(8,128)(2,1)S(1)} collective-permute-done((bf16[640,512]{1,0:T(8,128)(2,1)S(1)}, bf16[640,512]{1,0:T(8,128)(2,1)S(1)}, u32[]{:S(2)}, u32[]{:S(2)}) %collective-permute-start.32) | collective-permute-done | bytes 655392 | tf_op jit(solution)/shard_map/ppermute | solution.py:22
  210.1 2.5 collective-permute-done.34.other_tot_ref
  213.2 2.7 %collective-permute-start.35 = (bf16[640,384]{1,0:T(8,128)(2,1)S(1)}, bf16[640,384]{1,0:T(8,128)(2,1)S(1)}, u32[]{:S(2)}, u32[]{:S(2)}) collective-permute-start(bf16[640,384]{1,0:T(8,128)(2,1)S(1)} %combine.1.own_ref), channel_id=1, source_target_pairs={{0,1},{1,0},{2,3},{3,2},{4,5},{5,4},{6,7},{7,6},{8,9},{9,8},{10,11... | collective-permute-start | bytes 1474568 | tf_op jit(solution)/shard_map/ppermute | solution.py:22
  215.9 11.5 %collective-permute-done.35.other_ref = bf16[640,384]{1,0:T(8,128)(2,1)S(1)} collective-permute-done((bf16[640,384]{1,0:T(8,128)(2,1)S(1)}, bf16[640,384]{1,0:T(8,128)(2,1)S(1)}, u32[]{:S(2)}, u32[]{:S(2)}) %collective-permute-start.35) | collective-permute-done | bytes 491552 | tf_op jit(solution)/shard_map/ppermute | solution.py:22
  227.4 6.0 %out_projection.1 = bf16[4,640,384]{2,1,0:T(8,128)(2,1)} custom-call(s32[1]{0:T(128)} %bitcast.place_ref, bf16[640,384]{1,0:T(8,128)(2,1)S(1)} %combine.1.own_ref, bf16[640,384]{1,0:T(8,128)(2,1)S(1)} %collective-permute-done.35.other_ref, bf16[16,2,192,384]{3,2,1,0:T(8,128)(2,1)} %bitcast.54), custom_call_target="tpu_custom_call" | custom-call | tf_op jit(solution)/shard_map/out_projection/pallas_call | solution.py:329
  233.4 4.4 %all-to-all-start.3 = ((bf16[4,640,384]{2,1,0:T(8,128)(2,1)}), bf16[4,640,384]{2,1,0:T(8,128)(2,1)}, u32[]{:S(2)}, u32[]{:S(2)}) async-start(bf16[4,640,384]{2,1,0:T(8,128)(2,1)} %out_projection.1), calls=%async_computation.3 | async-start | bytes 3932160 | tf_op jit(solution)/shard_map/all_to_all | solution.py:460
  238.1 24.8 %all-to-all-done.3 = bf16[4,640,384]{2,1,0:T(8,128)(2,1)} async-done(((bf16[4,640,384]{2,1,0:T(8,128)(2,1)}), bf16[4,640,384]{2,1,0:T(8,128)(2,1)}, u32[]{:S(2)}, u32[]{:S(2)}) %all-to-all-start.3) | async-done | bytes 1966112 | tf_op jit(solution)/shard_map/all_to_all | solution.py:460
  262.9 2.0 convert_reduce_fusion
  265.5 0.9 fusion.2
  (119 shorter events, 9.4 us)
Async XLA Ops:
  7.2 24.8 %copy-start = (bf16[128,1280]{1,0:T(8,128)(2,1)S(1)}, bf16[128,1280]{1,0:T(8,128)(2,1)}, u32[]{:S(2)}) copy-start(bf16[128,1280]{1,0:T(8,128)(2,1)} %param.17) | copy-start | bytes 983044
  7.2 21.5 %collective-permute-start = (bf16[512,384]{1,0:T(8,128)(2,1)}, bf16[512,384]{1,0:T(8,128)(2,1)S(1)}, u32[]{:S(2)}, u32[]{:S(2)}) collective-permute-start(bf16[512,384]{1,0:T(8,128)(2,1)} %refs_0_.1), channel_id=1, source_target_pairs={{0,1},{1,0},{2,3},{3,2},{4,5},{5,4},{6,7},{7,6},{8,9},{9,8},{10,11... | collective-permute-start | bytes 1179656 | tf_op jit(solution)/shard_map/ppermute | solution.py:22
  8.9 23.0 %collective-permute-start.1 = (bf16[512,384]{1,0:T(8,128)(2,1)}, bf16[512,384]{1,0:T(8,128)(2,1)S(1)}, u32[]{:S(2)}, u32[]{:S(2)}) collective-permute-start(bf16[512,384]{1,0:T(8,128)(2,1)} %refs_0_.1), channel_id=1, source_target_pairs={{0,2},{2,4},{4,6},{6,0},{1,3},{3,5},{5,7},{7,1},{8,10},{10,12},{12... | collective-permute-start | bytes 1179656 | tf_op jit(solution)/shard_map/ppermute | solution.py:22
  10.4 21.5 %collective-permute-start.2 = (bf16[512,384]{1,0:T(8,128)(2,1)}, bf16[512,384]{1,0:T(8,128)(2,1)}, u32[]{:S(2)}, u32[]{:S(2)}) collective-permute-start(bf16[512,384]{1,0:T(8,128)(2,1)} %refs_0_.1), channel_id=1, source_target_pairs={{0,6},{2,0},{4,2},{6,4},{1,7},{3,1},{5,3},{7,5},{8,14},{10,8},{12,... | collective-permute-start | bytes 1179656 | tf_op jit(solution)/shard_map/ppermute | solution.py:22
  13.2 5.2 %collective-permute-start.3 = (bf16[2,192,384]{2,1,0:T(8,128)(2,1)S(1)}, bf16[2,192,384]{2,1,0:T(8,128)(2,1)S(1)}, u32[]{:S(2)}, u32[]{:S(2)}) collective-permute-start(bf16[2,192,384]{2,1,0:T(8,128)(2,1)S(1)} %pad_maximum_fusion.3), channel_id=1, source_target_pairs={{0,0},{1,16},{16,1},{17,17},{32,32},{33,48},{48,33},{49,49},{2,2},... | collective-permute-start | bytes 884744 | tf_op jit(solution)/shard_map/ppermute | solution.py:384
  15.1 50.9 %collective-permute-start.6 = (bf16[6,192,384]{2,1,0:T(8,128)(2,1)S(1)}, bf16[6,192,384]{2,1,0:T(8,128)(2,1)S(1)}, u32[]{:S(2)}, u32[]{:S(2)}) collective-permute-start(bf16[6,192,384]{2,1,0:T(8,128)(2,1)S(1)} %maximum_bitcast_fusion.refs_1_), channel_id=1, source_target_pairs={{0,16},{16,32},{32,48},{48,0},{1,17},{17,33},{33,49},{49,1},{2,18}... | collective-permute-start | bytes 2654216 | tf_op jit(solution)/shard_map/ppermute | solution.py:22
  18.3 19.7 %copy-start.23 = (bf16[2,192,384]{2,1,0:T(8,128)(2,1)}, bf16[2,192,384]{2,1,0:T(8,128)(2,1)S(1)}, u32[]{:S(2)}) copy-start(bf16[2,192,384]{2,1,0:T(8,128)(2,1)S(1)} %collective-permute-done.3) | copy-start | bytes 884740
  18.4 47.7 %collective-permute-start.7 = (bf16[6,192,384]{2,1,0:T(8,128)(2,1)S(1)}, bf16[6,192,384]{2,1,0:T(8,128)(2,1)}, u32[]{:S(2)}, u32[]{:S(2)}) collective-permute-start(bf16[6,192,384]{2,1,0:T(8,128)(2,1)S(1)} %maximum_bitcast_fusion.refs_1_), channel_id=1, source_target_pairs={{0,48},{16,0},{32,16},{48,32},{1,49},{17,1},{33,17},{49,33},{2,50}... | collective-permute-start | bytes 2654216 | tf_op jit(solution)/shard_map/ppermute | solution.py:22
  28.7 18.0 %copy-start.4 = (bf16[512,384]{1,0:T(8,128)(2,1)}, bf16[512,384]{1,0:T(8,128)(2,1)S(1)}, u32[]{:S(2)}) copy-start(bf16[512,384]{1,0:T(8,128)(2,1)S(1)} %collective-permute-done.refs_4_) | copy-start | bytes 1179652
  28.7 38.1 %collective-permute-start.8 = (bf16[6,192,384]{2,1,0:T(8,128)(2,1)S(1)}, bf16[6,192,384]{2,1,0:T(8,128)(2,1)}, u32[]{:S(2)}, u32[]{:S(2)}) collective-permute-start(bf16[6,192,384]{2,1,0:T(8,128)(2,1)S(1)} %maximum_bitcast_fusion.refs_1_), channel_id=1, source_target_pairs={{0,64},{64,0},{1,65},{65,1},{2,66},{66,2},{3,67},{67,3},{4,68},{68... | collective-permute-start | bytes 2654216 | tf_op jit(solution)/shard_map/ppermute | solution.py:22
  31.9 48.0 %copy-start.6 = (bf16[512,384]{1,0:T(8,128)(2,1)}, bf16[512,384]{1,0:T(8,128)(2,1)S(1)}, u32[]{:S(2)}) copy-start(bf16[512,384]{1,0:T(8,128)(2,1)S(1)} %collective-permute-done.1.refs_1_) | copy-start | bytes 1179652
  40.3 31.2 %copy-start.24 = (bf16[128,448]{0,1:T(8,128)(2,1)S(1)}, bf16[128,448]{0,1:T(8,128)(2,1)}, u32[]{:S(2)}) copy-start(bf16[128,448]{0,1:T(8,128)(2,1)} %param.19) | copy-start | bytes 344068
  40.3 26.6 %all-to-all-start = ((bf16[8,128,448]{1,2,0:T(8,128)(2,1)}), bf16[8,128,448]{1,2,0:T(8,128)(2,1)}, u32[]{:S(2)}, u32[]{:S(2)}) async-start(bf16[8,128,448]{1,2,0:T(8,128)(2,1)} %bitcast.55), calls=%async_computation | async-start | bytes 1835008 | tf_op jit(solution)/shard_map/all_to_all | solution.py:395
  44.7 182.7 %all-gather.3.cloned.1.call-start = ((), (), s32[]{:S(2)}) async-start(), calls=%async_computation.4 | async-start | bytes 5013504 | tf_op jit(solution)/shard_map/all_gather | solution.py:400
  44.7 20.5 %collective-permute-start.4 = (bf16[512,384]{1,0:T(8,128)(2,1)S(1)}, bf16[512,384]{1,0:T(8,128)(2,1)S(1)}, u32[]{:S(2)}, u32[]{:S(2)}) collective-permute-start(bf16[512,384]{1,0:T(8,128)(2,1)S(1)} %collective-permute-done.refs_4_), channel_id=1, source_target_pairs={{0,2},{2,4},{4,6},{6,0},{1,3},{3,5},{5,7},{7,1},{8,10},{10,12},{12... | collective-permute-start | bytes 1179656 | tf_op jit(solution)/shard_map/ppermute | solution.py:22
  46.7 19.3 %collective-permute-start.5 = (bf16[512,384]{1,0:T(8,128)(2,1)S(1)}, bf16[512,384]{1,0:T(8,128)(2,1)S(1)}, u32[]{:S(2)}, u32[]{:S(2)}) collective-permute-start(bf16[512,384]{1,0:T(8,128)(2,1)S(1)} %collective-permute-done.refs_4_), channel_id=1, source_target_pairs={{0,6},{2,0},{4,2},{6,4},{1,7},{3,1},{5,3},{7,5},{8,14},{10,8},{12,... | collective-permute-start | bytes 1179656 | tf_op jit(solution)/shard_map/ppermute | solution.py:22
  66.8 29.7 %collective-permute-start.11 = (bf16[6,192,384]{2,1,0:T(8,128)(2,1)}, bf16[6,192,384]{2,1,0:T(8,128)(2,1)}, u32[]{:S(2)}, u32[]{:S(2)}) collective-permute-start(bf16[6,192,384]{2,1,0:T(8,128)(2,1)} %collective-permute-done.8.refs_5_), channel_id=1, source_target_pairs={{0,16},{16,32},{32,48},{48,0},{1,17},{17,33},{33,49},{49,1},{2,18}... | collective-permute-start | bytes 2654216 | tf_op jit(solution)/shard_map/ppermute | solution.py:22
  66.9 29.7 %collective-permute-start.12 = (bf16[6,192,384]{2,1,0:T(8,128)(2,1)}, bf16[6,192,384]{2,1,0:T(8,128)(2,1)}, u32[]{:S(2)}, u32[]{:S(2)}) collective-permute-start(bf16[6,192,384]{2,1,0:T(8,128)(2,1)} %collective-permute-done.8.refs_5_), channel_id=1, source_target_pairs={{0,48},{16,0},{32,16},{48,32},{1,49},{17,1},{33,17},{49,33},{2,50}... | collective-permute-start | bytes 2654216 | tf_op jit(solution)/shard_map/ppermute | solution.py:22
  71.4 5.4 %copy-start.11 = (bf16[512,384]{1,0:T(8,128)(2,1)S(1)}, bf16[512,384]{1,0:T(8,128)(2,1)}, u32[]{:S(2)}) copy-start(bf16[512,384]{1,0:T(8,128)(2,1)} %copy-done.10) | copy-start | bytes 1179652
  71.4 28.9 %copy-start.26 = (f32[3584]{0:T(1024)S(1)}, f32[3584]{0:T(1024)}, u32[]{:S(2)}) copy-start(f32[3584]{0:T(1024)} %param.20) | copy-start | bytes 43012
  72.5 24.0 %all-to-all-start.1 = ((bf16[8,128,448]{1,2,0:T(8,128)(2,1)}), bf16[8,128,448]{1,2,0:T(8,128)(2,1)}, u32[]{:S(2)}, u32[]{:S(2)}) async-start(bf16[8,128,448]{1,2,0:T(8,128)(2,1)} %broadcast_in_dim.4), calls=%async_computation.1 | async-start | bytes 1835008 | tf_op jit(solution)/shard_map/all_to_all | solution.py:32
  76.8 17.8 %collective-permute-start.10 = (bf16[512,384]{1,0:T(8,128)(2,1)S(1)}, bf16[512,384]{1,0:T(8,128)(2,1)S(1)}, u32[]{:S(2)}, u32[]{:S(2)}) collective-permute-start(bf16[512,384]{1,0:T(8,128)(2,1)S(1)} %copy-done.11), channel_id=1, source_target_pairs={{0,6},{2,0},{4,2},{6,4},{1,7},{3,1},{5,3},{7,5},{8,14},{10,8},{12,... | collective-permute-start | bytes 1179656 | tf_op jit(solution)/shard_map/ppermute | solution.py:22
  79.9 15.8 %collective-permute-start.9 = (bf16[512,384]{1,0:T(8,128)(2,1)S(1)}, bf16[512,384]{1,0:T(8,128)(2,1)S(1)}, u32[]{:S(2)}, u32[]{:S(2)}) collective-permute-start(bf16[512,384]{1,0:T(8,128)(2,1)S(1)} %collective-permute-done.1.refs_1_), channel_id=1, source_target_pairs={{0,2},{2,4},{4,6},{6,0},{1,3},{3,5},{5,7},{7,1},{8,10},{10,12},{12... | collective-permute-start | bytes 1179656 | tf_op jit(solution)/shard_map/ppermute | solution.py:22
  96.5 26.4 %collective-permute-start.13 = (bf16[6,192,384]{2,1,0:T(8,128)(2,1)S(1)}, bf16[6,192,384]{2,1,0:T(8,128)(2,1)}, u32[]{:S(2)}, u32[]{:S(2)}) collective-permute-start(bf16[6,192,384]{2,1,0:T(8,128)(2,1)S(1)} %collective-permute-done.6.refs_2_), channel_id=1, source_target_pairs={{0,16},{16,32},{32,48},{48,0},{1,17},{17,33},{33,49},{49,1},{2,18}... | collective-permute-start | bytes 2654216 | tf_op jit(solution)/shard_map/ppermute | solution.py:22
  96.6 26.7 %collective-permute-start.14 = (bf16[6,192,384]{2,1,0:T(8,128)(2,1)}, bf16[6,192,384]{2,1,0:T(8,128)(2,1)}, u32[]{:S(2)}, u32[]{:S(2)}) collective-permute-start(bf16[6,192,384]{2,1,0:T(8,128)(2,1)} %collective-permute-done.12.refs_7_), channel_id=1, source_target_pairs={{0,48},{16,0},{32,16},{48,32},{1,49},{17,1},{33,17},{49,33},{2,50}... | collective-permute-start | bytes 2654216 | tf_op jit(solution)/shard_map/ppermute | solution.py:22
  99.8 24.6 %collective-permute-start.15 = (bf16[6,192,384]{2,1,0:T(8,128)(2,1)S(1)}, bf16[6,192,384]{2,1,0:T(8,128)(2,1)}, u32[]{:S(2)}, u32[]{:S(2)}) collective-permute-start(bf16[6,192,384]{2,1,0:T(8,128)(2,1)S(1)} %maximum_bitcast_fusion.refs_1_), channel_id=1, source_target_pairs={{0,8},{8,0},{1,9},{9,1},{2,10},{10,2},{3,11},{11,3},{4,12},{12,4},... | collective-permute-start | bytes 2654216 | tf_op jit(solution)/shard_map/ppermute | solution.py:22
  99.8 24.6 %collective-permute-start.19 = (bf16[6,192,384]{2,1,0:T(8,128)(2,1)}, bf16[6,192,384]{2,1,0:T(8,128)(2,1)}, u32[]{:S(2)}, u32[]{:S(2)}) collective-permute-start(bf16[6,192,384]{2,1,0:T(8,128)(2,1)} %collective-permute-done.8.refs_5_), channel_id=1, source_target_pairs={{0,8},{8,0},{1,9},{9,1},{2,10},{10,2},{3,11},{11,3},{4,12},{12,4},... | collective-permute-start | bytes 2654216 | tf_op jit(solution)/shard_map/ppermute | solution.py:22
  100.4 24.6 %collective-permute-start.16 = (bf16[6,192,384]{2,1,0:T(8,128)(2,1)S(1)}, bf16[6,192,384]{2,1,0:T(8,128)(2,1)}, u32[]{:S(2)}, u32[]{:S(2)}) collective-permute-start(bf16[6,192,384]{2,1,0:T(8,128)(2,1)S(1)} %collective-permute-done.6.refs_2_), channel_id=1, source_target_pairs={{0,8},{8,0},{1,9},{9,1},{2,10},{10,2},{3,11},{11,3},{4,12},{12,4},... | collective-permute-start | bytes 2654216 | tf_op jit(solution)/shard_map/ppermute | solution.py:22
  101.9 1.8 copy-start.2
  104.7 5.8 %copy-start.3 = (bf16[512,384]{1,0:T(8,128)(2,1)S(1)}, bf16[512,384]{1,0:T(8,128)(2,1)}, u32[]{:S(2)}) copy-start(bf16[512,384]{1,0:T(8,128)(2,1)} %refs_0_.1) | copy-start | bytes 1179652
  104.7 5.8 %copy-start.19 = (f32[4,3072]{1,0:T(4,128)S(1)}, f32[4,3072]{1,0:T(4,128)}, u32[]{:S(2)}) copy-start(f32[4,3072]{1,0:T(4,128)} %mod_ref.2) | copy-start | bytes 147460
  105.7 18.7 %all-to-all-start.2 = ((bf16[8,128,384]{2,1,0:T(8,128)(2,1)}), bf16[8,128,384]{2,1,0:T(8,128)(2,1)S(1)}, u32[]{:S(2)}, u32[]{:S(2)}) async-start(bf16[8,128,384]{2,1,0:T(8,128)(2,1)} %broadcast_in_dim.5), calls=%async_computation.2 | async-start | bytes 1572864 | tf_op jit(solution)/shard_map/all_to_all | solution.py:32
  110.5 1.0 copy-start.5
  113.5 1.0 copy-start.12
  114.5 1.0 copy-start.14
  116.5 8.7 %copy-start.29 = (s32[128]{0:T(128)S(1)}, s32[128]{0:T(128)}, u32[]{:S(2)}) copy-start(s32[128]{0:T(128)} %param.31) | copy-start | bytes 1540
  116.5 8.8 %copy-start.27 = (f32[128]{0:T(128)S(1)}, f32[128]{0:T(128)}, u32[]{:S(2)}) copy-start(f32[128]{0:T(128)} %param.26) | copy-start | bytes 1540
  116.5 8.8 %copy-start.28 = (f32[128]{0:T(128)S(1)}, f32[128]{0:T(128)}, u32[]{:S(2)}) copy-start(f32[128]{0:T(128)} %param.25) | copy-start | bytes 1540
  122.9 8.0 %copy-start.18 = (f32[4,3072]{1,0:T(4,128)S(1)}, f32[4,3072]{1,0:T(4,128)}, u32[]{:S(2)}) copy-start(f32[4,3072]{1,0:T(4,128)} %mod_ref.3) | copy-start | bytes 147460
  123.0 3.9 %collective-permute-start.21 = (bf16[6,192,384]{2,1,0:T(8,128)(2,1)}, bf16[6,192,384]{2,1,0:T(8,128)(2,1)}, u32[]{:S(2)}, u32[]{:S(2)}) collective-permute-start(bf16[6,192,384]{2,1,0:T(8,128)(2,1)} %collective-permute-done.12.refs_7_), channel_id=1, source_target_pairs={{0,8},{8,0},{1,9},{9,1},{2,10},{10,2},{3,11},{11,3},{4,12},{12,4},... | collective-permute-start | bytes 2654216 | tf_op jit(solution)/shard_map/ppermute | solution.py:22
  123.3 3.8 %collective-permute-start.17 = (bf16[6,192,384]{2,1,0:T(8,128)(2,1)}, bf16[6,192,384]{2,1,0:T(8,128)(2,1)}, u32[]{:S(2)}, u32[]{:S(2)}) collective-permute-start(bf16[6,192,384]{2,1,0:T(8,128)(2,1)} %collective-permute-done.7.refs_3_), channel_id=1, source_target_pairs={{0,8},{8,0},{1,9},{9,1},{2,10},{10,2},{3,11},{11,3},{4,12},{12,4},... | collective-permute-start | bytes 2654216 | tf_op jit(solution)/shard_map/ppermute | solution.py:22
  124.4 3.9 %collective-permute-start.20 = (bf16[6,192,384]{2,1,0:T(8,128)(2,1)}, bf16[6,192,384]{2,1,0:T(8,128)(2,1)}, u32[]{:S(2)}, u32[]{:S(2)}) collective-permute-start(bf16[6,192,384]{2,1,0:T(8,128)(2,1)} %collective-permute-done.11.refs_6_), channel_id=1, source_target_pairs={{0,8},{8,0},{1,9},{9,1},{2,10},{10,2},{3,11},{11,3},{4,12},{12,4},... | collective-permute-start | bytes 2654216 | tf_op jit(solution)/shard_map/ppermute | solution.py:22
  124.4 5.3 %collective-permute-start.18 = (bf16[6,192,384]{2,1,0:T(8,128)(2,1)}, bf16[6,192,384]{2,1,0:T(8,128)(2,1)}, u32[]{:S(2)}, u32[]{:S(2)}) collective-permute-start(bf16[6,192,384]{2,1,0:T(8,128)(2,1)} %collective-permute-done.13.refs_4_), channel_id=1, source_target_pairs={{0,8},{8,0},{1,9},{9,1},{2,10},{10,2},{3,11},{11,3},{4,12},{12,4},... | collective-permute-start | bytes 2654216 | tf_op jit(solution)/shard_map/ppermute | solution.py:22
  124.9 6.0 %collective-permute-start.22 = (bf16[6,192,384]{2,1,0:T(8,128)(2,1)}, bf16[6,192,384]{2,1,0:T(8,128)(2,1)}, u32[]{:S(2)}, u32[]{:S(2)}) collective-permute-start(bf16[6,192,384]{2,1,0:T(8,128)(2,1)} %collective-permute-done.14.refs_8_), channel_id=1, source_target_pairs={{0,8},{8,0},{1,9},{9,1},{2,10},{10,2},{3,11},{11,3},{4,12},{12,4},... | collective-permute-start | bytes 2654216 | tf_op jit(solution)/shard_map/ppermute | solution.py:22
  143.4 4.1 %collective-permute-start.24 = (bf16[640,384]{1,0:T(8,128)(2,1)S(1)}, bf16[640,384]{1,0:T(8,128)(2,1)S(1)}, u32[]{:S(2)}, u32[]{:S(2)}) collective-permute-start(bf16[640,384]{1,0:T(8,128)(2,1)S(1)} %get-tuple-element.100.refs_0_), channel_id=1, source_target_pairs={{0,8},{8,0},{1,9},{9,1},{2,10},{10,2},{3,11},{11,3},{4,12},{12,4},... | collective-permute-start | bytes 1474568 | tf_op jit(solution)/shard_map/ppermute | solution.py:22
  143.9 14.7 %collective-permute-start.23 = (bf16[640,384]{1,0:T(8,128)(2,1)S(1)}, bf16[640,384]{1,0:T(8,128)(2,1)S(1)}, u32[]{:S(2)}, u32[]{:S(2)}) collective-permute-start(bf16[640,384]{1,0:T(8,128)(2,1)S(1)} %get-tuple-element.100.refs_0_), channel_id=1, source_target_pairs={{0,64},{64,0},{1,65},{65,1},{2,66},{66,2},{3,67},{67,3},{4,68},{68... | collective-permute-start | bytes 1474568 | tf_op jit(solution)/shard_map/ppermute | solution.py:22
  144.2 25.0 %collective-permute-start.26 = (bf16[2,640,384]{2,1,0:T(8,128)(2,1)}, bf16[2,640,384]{2,1,0:T(8,128)(2,1)S(1)}, u32[]{:S(2)}, u32[]{:S(2)}) collective-permute-start(bf16[2,640,384]{2,1,0:T(8,128)(2,1)} %get-tuple-element.101.refs_2_.refs_3_), channel_id=1, source_target_pairs={{0,16},{16,32},{32,48},{48,0},{1,17},{17,33},{33,49},{49,1},{2,18}... | collective-permute-start | bytes 2949128 | tf_op jit(solution)/shard_map/ppermute | solution.py:22
  144.2 25.0 %collective-permute-start.27 = (bf16[2,640,384]{2,1,0:T(8,128)(2,1)}, bf16[2,640,384]{2,1,0:T(8,128)(2,1)S(1)}, u32[]{:S(2)}, u32[]{:S(2)}) collective-permute-start(bf16[2,640,384]{2,1,0:T(8,128)(2,1)} %get-tuple-element.101.refs_2_.refs_3_), channel_id=1, source_target_pairs={{0,48},{16,0},{32,16},{48,32},{1,49},{17,1},{33,17},{49,33},{2,50}... | collective-permute-start | bytes 2949128 | tf_op jit(solution)/shard_map/ppermute | solution.py:22
  147.5 1.2 copy-start.20
  148.7 11.8 %copy-start.21 = (bf16[2,640,384]{2,1,0:T(8,128)(2,1)S(1)}, bf16[2,640,384]{2,1,0:T(8,128)(2,1)}, u32[]{:S(2)}) copy-start(bf16[2,640,384]{2,1,0:T(8,128)(2,1)} %get-tuple-element.101.refs_2_.refs_3_) | copy-start | bytes 2949124
  158.6 1.9 collective-permute-start.25
  169.3 11.4 %copy-start.17 = (bf16[2,640,384]{2,1,0:T(8,128)(2,1)}, bf16[2,640,384]{2,1,0:T(8,128)(2,1)S(1)}, u32[]{:S(2)}) copy-start(bf16[2,640,384]{2,1,0:T(8,128)(2,1)S(1)} %collective-permute-done.27.refs_3_.refs_5_.refs_6_) | copy-start | bytes 2949124
  169.3 13.5 %collective-permute-start.28 = (bf16[640,384]{1,0:T(8,128)(2,1)S(1)}, bf16[640,384]{1,0:T(8,128)(2,1)S(1)}, u32[]{:S(2)}, u32[]{:S(2)}) collective-permute-start(bf16[640,384]{1,0:T(8,128)(2,1)S(1)} %slice_bitcast_fusion.1), channel_id=1, source_target_pairs={{0,16},{16,32},{32,48},{48,0},{1,17},{17,33},{33,49},{49,1},{2,18}... | collective-permute-start | bytes 1474568 | tf_op jit(solution)/shard_map/ppermute | solution.py:22
  169.5 13.4 %collective-permute-start.29 = (bf16[640,384]{1,0:T(8,128)(2,1)S(1)}, bf16[640,384]{1,0:T(8,128)(2,1)S(1)}, u32[]{:S(2)}, u32[]{:S(2)}) collective-permute-start(bf16[640,384]{1,0:T(8,128)(2,1)S(1)} %slice_bitcast_fusion), channel_id=1, source_target_pairs={{0,48},{16,0},{32,16},{48,32},{1,49},{17,1},{33,17},{49,33},{2,50}... | collective-permute-start | bytes 1474568 | tf_op jit(solution)/shard_map/ppermute | solution.py:22
  187.7 3.2 %collective-permute-start.30 = (f32[640,384]{1,0:T(8,128)S(1)}, f32[640,384]{1,0:T(8,128)S(1)}, u32[]{:S(2)}, u32[]{:S(2)}) collective-permute-start(f32[640,384]{1,0:T(8,128)S(1)} %get-tuple-element.128), channel_id=1, source_target_pairs={{0,8},{8,0},{1,9},{9,1},{2,10},{10,2},{3,11},{11,3},{4,12},{12,4},... | collective-permute-start | bytes 2949128 | tf_op jit(solution)/shard_map/ppermute | solution.py:22
  187.8 3.0 %collective-permute-start.31 = (f32[640,128]{1,0:T(8,128)S(1)}, f32[640,128]{1,0:T(8,128)S(1)}, u32[]{:S(2)}, u32[]{:S(2)}) collective-permute-start(f32[640,128]{1,0:T(8,128)S(1)} %get-tuple-element.130), channel_id=1, source_target_pairs={{0,8},{8,0},{1,9},{9,1},{2,10},{10,2},{3,11},{11,3},{4,12},{12,4},... | collective-permute-start | bytes 983048 | tf_op jit(solution)/shard_map/ppermute | solution.py:22
  191.2 18.4 %collective-permute-start.32 = (bf16[640,512]{1,0:T(8,128)(2,1)S(1)}, bf16[640,512]{1,0:T(8,128)(2,1)S(1)}, u32[]{:S(2)}, u32[]{:S(2)}) collective-permute-start(bf16[640,512]{1,0:T(8,128)(2,1)S(1)} %pad_maximum_fusion), channel_id=1, source_target_pairs={{0,64},{64,0},{1,65},{65,1},{2,66},{66,2},{3,67},{67,3},{4,68},{68... | collective-permute-start | bytes 1966088 | tf_op jit(solution)/shard_map/ppermute | solution.py:22
  209.6 3.0 %collective-permute-start.33 = (f32[640,384]{1,0:T(8,128)S(1)}, f32[640,384]{1,0:T(8,128)S(1)}, u32[]{:S(2)}, u32[]{:S(2)}) collective-permute-start(f32[640,384]{1,0:T(8,128)S(1)} %get-tuple-element.145), channel_id=1, source_target_pairs={{0,8},{8,0},{1,9},{9,1},{2,10},{10,2},{3,11},{11,3},{4,12},{12,4},... | collective-permute-start | bytes 2949128 | tf_op jit(solution)/shard_map/ppermute | solution.py:22
  209.6 3.0 %collective-permute-start.34 = (f32[640,128]{1,0:T(8,128)S(1)}, f32[640,128]{1,0:T(8,128)S(1)}, u32[]{:S(2)}, u32[]{:S(2)}) collective-permute-start(f32[640,128]{1,0:T(8,128)S(1)} %get-tuple-element.148), channel_id=1, source_target_pairs={{0,8},{8,0},{1,9},{9,1},{2,10},{10,2},{3,11},{11,3},{4,12},{12,4},... | collective-permute-start | bytes 983048 | tf_op jit(solution)/shard_map/ppermute | solution.py:22
  213.2 14.3 %collective-permute-start.35 = (bf16[640,384]{1,0:T(8,128)(2,1)S(1)}, bf16[640,384]{1,0:T(8,128)(2,1)S(1)}, u32[]{:S(2)}, u32[]{:S(2)}) collective-permute-start(bf16[640,384]{1,0:T(8,128)(2,1)S(1)} %combine.1.own_ref), channel_id=1, source_target_pairs={{0,1},{1,0},{2,3},{3,2},{4,5},{5,4},{6,7},{7,6},{8,9},{9,8},{10,11... | collective-permute-start | bytes 1474568 | tf_op jit(solution)/shard_map/ppermute | solution.py:22
  233.4 29.5 %all-to-all-start.3 = ((bf16[4,640,384]{2,1,0:T(8,128)(2,1)}), bf16[4,640,384]{2,1,0:T(8,128)(2,1)}, u32[]{:S(2)}, u32[]{:S(2)}) async-start(bf16[4,640,384]{2,1,0:T(8,128)(2,1)} %out_projection.1), calls=%async_computation.3 | async-start | bytes 3932160 | tf_op jit(solution)/shard_map/all_to_all | solution.py:460
  237.8 27.0 %copy-start.25 = (bf16[128,384]{1,0:T(8,128)(2,1)S(1)}, bf16[128,384]{1,0:T(8,128)(2,1)}, u32[]{:S(2)}) copy-start(bf16[128,384]{1,0:T(8,128)(2,1)} %param.33) | copy-start | bytes 294916
  237.8 27.7 %copy-start.22 = (bf16[512,384]{1,0:T(8,128)(2,1)S(1)}, bf16[512,384]{1,0:T(8,128)(2,1)}, u32[]{:S(2)}) copy-start(bf16[512,384]{1,0:T(8,128)(2,1)} %param.32) | copy-start | bytes 1179652
  262.9 3.6 %copy-start.1 = (bf16[128,1280]{1,0:T(8,128)(2,1)S(1)}, bf16[128,1280]{1,0:T(8,128)(2,1)}, u32[]{:S(2)}) copy-start(bf16[128,1280]{1,0:T(8,128)(2,1)} %param.17) | copy-start | bytes 983044
  (7 other events, 6.1 us)
Sparse Core Ops, SparseCore 0:
  71.6 66.6 all-gather.2

commit v3 on v2

--- a/solution.py
+++ b/solution.py
@@ -375,17 +375,10 @@
     outs = jnp.stack([jnp.transpose(image_out), jnp.transpose(text_out)])
     weight = jnp.transpose(jnp.concatenate([image_qkv, text_qkv], axis=1), (1, 0, 2))
 
-    turned = [
-        (4 * zh + 2 * zl + y, 4 * zh + 2 * y + zl)
-        for zh in range(2)
-        for zl in range(2)
-        for y in range(2)
-    ]
-    outs = lax.ppermute(outs, ("z", "yl"), turned)
     a_pair = shift(image_states, "yl", 1)
     a_near = near(image_states, "x")
     w_pair = shift(weight, "yh", 1)
-    cond_hidden, a_pair, a_near, outs = together((cond_hidden, a_pair, a_near, outs))
+    cond_hidden, a_pair, a_near = together((cond_hidden, a_pair, a_near))
 
     w_near = near(weight, "z")
     a_next = near(a_pair, "x")
@@ -397,12 +390,19 @@
         (got, a_near, a_next, w_near, w_pair, outs)
     )
 
-    out_w = lax.all_gather(outs, SEQ)
     a_far = (shift(a_near[0], "x", 1), shift(a_next[1], "x", -1))
     w_next = near(w_pair, "z")
+    turned = [
+        (4 * zh + 2 * zl + y, 4 * zh + 2 * y + zl)
+        for zh in range(2)
+        for zl in range(2)
+        for y in range(2)
+    ]
+    outs = lax.ppermute(outs, ("z", "yl"), turned)
+    out_w = lax.all_gather(outs, SEQ)
     cond_state = (jnp.sum(got.astype(F32), axis=0) + cond_resid.astype(F32)).astype(BF)
     state = spread(cond_state, TP)
-    state, a_far, w_near, w_next = together((state, a_far, w_near, w_next))
+    state, a_far, w_near, w_next, outs = together((state, a_far, w_near, w_next, outs))
 
     text_states = text_projection(state, cond_gain, text_proj)
     text_a = spread(text_states, TP)

time: 275 us -> 274 us (level)
  starting transfers between devices: 69.6 us -> 62.9 us
  waiting for transfers between devices: 96.4 us -> 99.9 us
    ppermute x35, starting transfers between devices: 51.1 us -> 43.4 us  [shift(): lax.ppermute(value, axis, [(k, (k + step) % size) for k in range(size)])]
    ppermute x35, waiting for transfers between devices: 70.7 us -> 75.4 us  [shift(): lax.ppermute(value, axis, [(k, (k + step) % size) for k in range(size)])]
    unnamed x60 -> x68, local copies, waits for them, and re-layouts: 12.2 us -> 14.7 us
  transfers between devices with their start and end apart: 41 -> 41, of which waited for: 17 -> 16; matrix products, arithmetic and copies ran while one was open for 7% -> 6% of each run, Pallas kernels for 20% -> 20%
where the time goes in v3:
time: 274 us; the launch traced here: 272 us
  waiting for transfers between devices  99.9 us (36%)
  starting transfers between devices  62.9 us (23%)
  Pallas kernels  59.4 us (22%)
  local copies, waits for them, and re-layouts  21 us (8%)
  between operations  14.5 us (5%)
  other arithmetic  8.74 us (3%)
  matrix products  5.96 us (2%)
    ppermute x35, waiting for transfers between devices, shift(): lax.ppermute(value, axis, [(k, (k + step) % size) for k in range(size)])  75.4 us
    ppermute x35, starting transfers between devices, shift(): lax.ppermute(value, axis, [(k, (k + step) % size) for k in range(size)])  43.4 us
    pallas_call x5, Pallas kernels, attention(): pl.pallas_call(functools.partial(attention_kernel, nq, k_sizes, not befor...  33 us
    all_to_all x1, waiting for transfers between devices, shards(): got = lax.all_to_all(parts, 'x', split_axis=0, concat_axis=0, tiled=True)  24.5 us
    unnamed x68, local copies, waits for them, and re-layouts  14.7 us
    pallas_call x1, Pallas kernels, qkv(): pl.pallas_call(functools.partial(qkv_kernel, count), out_shape=(jax.Shape...  12.4 us
    all_to_all x2, starting transfers between devices, spread(): return lax.all_to_all(copies, axes, split_axis=0, concat_axis=0, tiled=True)  8.65 us
    pallas_call x1, Pallas kernels, modulate(): pl.pallas_call(functools.partial(modulate_kernel, count), out_shape=jax.S...  6.59 us
  transfers between devices with their start and end apart: 41, of which 16 were waited for; matrix products, arithmetic and copies ran while one was open for 6% of the time, Pallas kernels for 20%

profile of v3, /device:TPU:0, one launch (start us, length us, event | category | flops | bytes accessed | tf_op | source)
XLA Modules:
  0.0 272.4 jit_solution(5565203438836258324)
XLA Ops:
  7.2 1.7 collective-permute-start
  8.9 1.5 collective-permute-start.1
  10.4 1.7 collective-permute-start.2
  12.2 1.2 maximum_bitcast_fusion.refs_1_
  13.4 2.0 collective-permute-start.5
  15.4 2.2 collective-permute-start.6
  18.2 3.4 %collective-permute-start.7 = (bf16[6,192,384]{2,1,0:T(8,128)(2,1)S(1)}, bf16[6,192,384]{2,1,0:T(8,128)(2,1)}, u32[]{:S(2)}, u32[]{:S(2)}) collective-permute-start(bf16[6,192,384]{2,1,0:T(8,128)(2,1)S(1)} %maximum_bitcast_fusion.refs_1_), channel_id=1, source_target_pairs={{0,64},{64,0},{1,65},{65,1},{2,66},{66,2},{3,67},{67,3},{4,68},{68... | collective-permute-start | bytes 2654216 | tf_op jit(solution)/shard_map/ppermute | solution.py:22
  22.4 6.0 %convolution_convert_fusion = bf16[128,3584]{1,0:T(8,128)(2,1)} fusion(bf16[128,1280]{1,0:T(8,128)(2,1)S(1)} %copy-done, bf16[1280,3584]{1,0:T(8,128)(2,1)} %param.18), kind=kOutput, calls=%fused_computation | convolution fusion | flops 1174863872 | bytes 10420224 | tf_op jit(solution)/shard_map/dot_general | solution.py:385
  28.4 2.3 copy.34
  30.7 4.5 %all-to-all-start = ((bf16[8,128,448]{1,2,0:T(8,128)(2,1)}), bf16[8,128,448]{1,2,0:T(8,128)(2,1)}, u32[]{:S(2)}, u32[]{:S(2)}) async-start(bf16[8,128,448]{1,2,0:T(8,128)(2,1)} %bitcast.55), calls=%async_computation | async-start | bytes 1835008 | tf_op jit(solution)/shard_map/all_to_all | solution.py:388
  35.3 2.0 collective-permute-start.3
  37.2 1.3 collective-permute-start.4
  39.4 16.6 %collective-permute-done.3.refs_5_ = bf16[512,384]{1,0:T(8,128)(2,1)S(1)} collective-permute-done((bf16[512,384]{1,0:T(8,128)(2,1)S(1)}, bf16[512,384]{1,0:T(8,128)(2,1)S(1)}, u32[]{:S(2)}, u32[]{:S(2)}) %collective-permute-start.3) | collective-permute-done | bytes 393248 | tf_op jit(solution)/shard_map/ppermute | solution.py:22
  57.6 1.6 collective-permute-start.12
  59.2 3.3 %collective-permute-start.10 = (bf16[6,192,384]{2,1,0:T(8,128)(2,1)}, bf16[6,192,384]{2,1,0:T(8,128)(2,1)}, u32[]{:S(2)}, u32[]{:S(2)}) collective-permute-start(bf16[6,192,384]{2,1,0:T(8,128)(2,1)} %collective-permute-done.7.refs_5_), channel_id=1, source_target_pairs={{0,16},{16,32},{32,48},{48,0},{1,17},{17,33},{33,49},{49,1},{2,18}... | collective-permute-start | bytes 2654216 | tf_op jit(solution)/shard_map/ppermute | solution.py:22
  62.5 2.5 collective-permute-start.11
  65.0 1.3 convert_reduce_fusion.1
  67.1 1.0 broadcast_in_dim.4
  68.2 5.1 %all-to-all-start.1 = ((bf16[8,128,448]{1,2,0:T(8,128)(2,1)}), bf16[8,128,448]{1,2,0:T(8,128)(2,1)}, u32[]{:S(2)}, u32[]{:S(2)}) async-start(bf16[8,128,448]{1,2,0:T(8,128)(2,1)} %broadcast_in_dim.4), calls=%async_computation.1 | async-start | bytes 1835008 | tf_op jit(solution)/shard_map/all_to_all | solution.py:32
  73.3 2.0 collective-permute-start.8
  75.3 1.3 collective-permute-start.9
  76.6 16.5 %collective-permute-done.8.refs_3_ = bf16[512,384]{1,0:T(8,128)(2,1)S(1)} collective-permute-done((bf16[512,384]{1,0:T(8,128)(2,1)S(1)}, bf16[512,384]{1,0:T(8,128)(2,1)S(1)}, u32[]{:S(2)}, u32[]{:S(2)}) %collective-permute-start.8) | collective-permute-done | bytes 393248 | tf_op jit(solution)/shard_map/ppermute | solution.py:22
  94.6 1.1 collective-permute-start.13
  95.7 2.5 collective-permute-start.14
  98.9 1.5 copy.35.state_ref
  100.4 1.8 copy-done.2
  103.1 1.0 broadcast_in_dim.5
  104.1 3.5 %all-to-all-start.2 = ((bf16[8,128,384]{2,1,0:T(8,128)(2,1)}), bf16[8,128,384]{2,1,0:T(8,128)(2,1)S(1)}, u32[]{:S(2)}, u32[]{:S(2)}) async-start(bf16[8,128,384]{2,1,0:T(8,128)(2,1)} %broadcast_in_dim.5), calls=%async_computation.2 | async-start | bytes 1572864 | tf_op jit(solution)/shard_map/all_to_all | solution.py:32
  107.9 1.0 copy-done.5
  108.8 1.0 copy-done.7
  109.8 1.0 copy-done.9
  110.8 1.0 copy-done.11
  111.8 1.0 copy-done.14
  112.8 1.0 copy-done.16
  113.8 1.0 copy-done.18
  114.8 6.6 %modulate.1.image_ref = bf16[512,3072]{1,0:T(8,128)(2,1)} custom-call(s32[8]{0:T(128)S(1)} %stack.131.place_ref, f32[4,3072]{1,0:T(4,128)S(1)} %copy-done.21, bf16[512,384]{1,0:T(8,128)(2,1)S(1)} %copy-done.3, bf16[512,384]{1,0:T(8,128)(2,1)S(1)} %copy-done.7, bf16[512,384]{1,0:T(8,128)(2,1)S(1)} %copy-done.9, bf16[512,384]{1,0:T(8,128)(2,1)S(1)} %copy-done.16, ...), custom_call_target="tpu_custom_call" | custom-call | tf_op jit(solution)/shard_map/modulate/pallas_call | solution.py:115
  123.3 1.2 fusion.7
  124.7 1.1 collective-permute-done.17.refs_11_
  125.8 1.3 collective-permute-done.20.refs_14_
  127.1 1.3 collective-permute-done.18.refs_12_
  128.3 1.4 collective-permute-done.22.refs_16_
  129.7 12.4 %qkv.1 = (bf16[640,384]{1,0:T(8,128)(2,1)S(1)}, bf16[2,640,384]{2,1,0:T(8,128)(2,1)}) custom-call(s32[16]{0:T(128)S(1)} %stack.116.place_ref, f32[4,3072]{1,0:T(4,128)S(1)} %copy-done.20, f32[640,128]{1,0:T(8,128)S(1)} %get-tuple-element.157.cos_ref, f32[640,128]{1,0:T(8,128)S(1)} %get-tuple-element.158.sin_ref, f32[2,128]{1,0:T(2,128)S(1)} %pad_maximum_fusion.5.gain_ref, ...), custom_call_target="tpu_custom_call" | custom-call | tf_op jit(solution)/shard_map/qkv/pallas_call | solution.py:191
  142.6 1.9 collective-permute-start.23
  144.8 2.8 %collective-permute-start.27 = (bf16[2,640,384]{2,1,0:T(8,128)(2,1)}, bf16[2,640,384]{2,1,0:T(8,128)(2,1)S(1)}, u32[]{:S(2)}, u32[]{:S(2)}) collective-permute-start(bf16[2,640,384]{2,1,0:T(8,128)(2,1)} %get-tuple-element.100.refs_2_.refs_3_), channel_id=1, source_target_pairs={{0,48},{16,0},{32,16},{48,32},{1,49},{17,1},{33,17},{49,33},{2,50}... | collective-permute-start | bytes 2949128 | tf_op jit(solution)/shard_map/ppermute | solution.py:22
  147.7 1.2 copy-done.22
  148.9 4.7 %attention.5 = (f32[640,384]{1,0:T(8,128)S(1)}, f32[640,384]{1,0:T(8,128)S(1)}, f32[640,128]{1,0:T(8,128)S(1)}, f32[640,128]{1,0:T(8,128)S(1)}) custom-call(bf16[640,384]{1,0:T(8,128)(2,1)S(1)} %get-tuple-element.99.refs_0_, bf16[640,384]{1,0:T(8,128)(2,1)S(1)} %collective-permute-done.24.refs_1_, bf16[2,640,384]{2,1,0:T(8,128)(2,1)S(1)} %copy-done.22, ...), custom_call_target="tpu_custom_call" | custom-call | flops 2516582400 | bytes 3932160 | tf_op jit(solution)/shard_map/attention/pallas_call | solution.py:259
  153.6 3.7 %collective-permute-done.23.refs_0_ = bf16[640,384]{1,0:T(8,128)(2,1)S(1)} collective-permute-done((bf16[640,384]{1,0:T(8,128)(2,1)S(1)}, bf16[640,384]{1,0:T(8,128)(2,1)S(1)}, u32[]{:S(2)}, u32[]{:S(2)}) %collective-permute-start.23) | collective-permute-done | bytes 491552 | tf_op jit(solution)/shard_map/ppermute | solution.py:22
  157.3 1.9 collective-permute-done.25.refs_1_
  159.2 4.7 %attention.6 = (f32[640,384]{1,0:T(8,128)S(1)}, f32[640,384]{1,0:T(8,128)S(1)}, f32[640,128]{1,0:T(8,128)S(1)}, f32[640,128]{1,0:T(8,128)S(1)}) custom-call(bf16[640,384]{1,0:T(8,128)(2,1)S(1)} %collective-permute-done.23.refs_0_, bf16[640,384]{1,0:T(8,128)(2,1)S(1)} %collective-permute-done.25.refs_1_, bf16[2,640,384]{2,1,0:T(8,128)(2,1)S(1)} %copy-done.23, ...), custom_call_target="tpu_custom_call" | custom-call | flops 2516582400 | bytes 3932160 | tf_op jit(solution)/shard_map/attention/pallas_call | solution.py:259
  163.9 5.6 %collective-permute-done.26.refs_2_.refs_4_.refs_5_ = bf16[2,640,384]{2,1,0:T(8,128)(2,1)S(1)} collective-permute-done((bf16[2,640,384]{2,1,0:T(8,128)(2,1)}, bf16[2,640,384]{2,1,0:T(8,128)(2,1)S(1)}, u32[]{:S(2)}, u32[]{:S(2)}) %collective-permute-start.26) | collective-permute-done | bytes 983072 | tf_op jit(solution)/shard_map/ppermute | solution.py:22
  170.5 2.7 %collective-permute-start.29 = (bf16[640,384]{1,0:T(8,128)(2,1)S(1)}, bf16[640,384]{1,0:T(8,128)(2,1)S(1)}, u32[]{:S(2)}, u32[]{:S(2)}) collective-permute-start(bf16[640,384]{1,0:T(8,128)(2,1)S(1)} %slice_bitcast_fusion), channel_id=1, source_target_pairs={{0,48},{16,0},{32,16},{48,32},{1,49},{17,1},{33,17},{49,33},{2,50}... | collective-permute-start | bytes 1474568 | tf_op jit(solution)/shard_map/ppermute | solution.py:22
  173.2 7.7 %attention.7 = (f32[640,384]{1,0:T(8,128)S(1)}, f32[640,384]{1,0:T(8,128)S(1)}, f32[640,128]{1,0:T(8,128)S(1)}, f32[640,128]{1,0:T(8,128)S(1)}) custom-call(bf16[640,384]{1,0:T(8,128)(2,1)S(1)} %collective-permute-done.23.refs_0_, ...), custom_call_target="tpu_custom_call", output_to_operand_aliasing={{0}: (6, {}), {1}: (7, {}), {2}: (8, {}), {3}: (9, {})} | custom-call | flops 5033164800 | bytes 3932160 | tf_op jit(solution)/shard_map/attention/pallas_call | solution.py:259
  180.9 2.1 collective-permute-done.28
  183.0 4.9 %attention.8 = (f32[640,384]{1,0:T(8,128)S(1)}, f32[640,384]{1,0:T(8,128)S(1)}, f32[640,128]{1,0:T(8,128)S(1)}, f32[640,128]{1,0:T(8,128)S(1)}) custom-call(bf16[640,384]{1,0:T(8,128)(2,1)S(1)} %collective-permute-done.23.refs_0_, ...), custom_call_target="tpu_custom_call", output_to_operand_aliasing={{0}: (4, {}), {1}: (5, {}), {2}: (6, {}), {3}: (7, {})} | custom-call | flops 2516582400 | bytes 3932160 | tf_op jit(solution)/shard_map/attention/pallas_call | solution.py:259
  188.6 2.5 collective-permute-done.31
  191.4 1.5 collective-permute-start.32
  192.9 11.0 %attention.9 = (f32[640,384]{1,0:T(8,128)S(1)}, f32[640,384]{1,0:T(8,128)S(1)}, f32[640,128]{1,0:T(8,128)S(1)}, f32[640,128]{1,0:T(8,128)S(1)}) custom-call(bf16[640,384]{1,0:T(8,128)(2,1)S(1)} %get-tuple-element.99.refs_0_, ...), custom_call_target="tpu_custom_call", output_to_operand_aliasing={{0}: (8, {}), {1}: (9, {}), {2}: (10, {}), {3}: (11, {})} | custom-call | flops 7549747200 | bytes 3932160 | tf_op jit(solution)/shard_map/attention/pallas_call | solution.py:259
  203.9 5.9 %collective-permute-done.32.back_ref = bf16[640,512]{1,0:T(8,128)(2,1)S(1)} collective-permute-done((bf16[640,512]{1,0:T(8,128)(2,1)S(1)}, bf16[640,512]{1,0:T(8,128)(2,1)S(1)}, u32[]{:S(2)}, u32[]{:S(2)}) %collective-permute-start.32) | collective-permute-done | bytes 655392 | tf_op jit(solution)/shard_map/ppermute | solution.py:22
  210.3 2.5 collective-permute-done.34.other_tot_ref
  214.3 12.4 %collective-permute-done.35.other_ref = bf16[640,384]{1,0:T(8,128)(2,1)S(1)} collective-permute-done((bf16[640,384]{1,0:T(8,128)(2,1)S(1)}, bf16[640,384]{1,0:T(8,128)(2,1)S(1)}, u32[]{:S(2)}, u32[]{:S(2)}) %collective-permute-start.35) | collective-permute-done | bytes 491552 | tf_op jit(solution)/shard_map/ppermute | solution.py:22
  226.7 6.0 %out_projection.1 = bf16[4,640,384]{2,1,0:T(8,128)(2,1)} custom-call(s32[1]{0:T(128)} %bitcast.place_ref, bf16[640,384]{1,0:T(8,128)(2,1)S(1)} %combine.1.own_ref, bf16[640,384]{1,0:T(8,128)(2,1)S(1)} %collective-permute-done.35.other_ref, bf16[16,2,192,384]{3,2,1,0:T(8,128)(2,1)} %bitcast.54), custom_call_target="tpu_custom_call" | custom-call | tf_op jit(solution)/shard_map/out_projection/pallas_call | solution.py:329
  232.7 4.7 %all-to-all-start.3 = ((bf16[4,640,384]{2,1,0:T(8,128)(2,1)}), bf16[4,640,384]{2,1,0:T(8,128)(2,1)}, u32[]{:S(2)}, u32[]{:S(2)}) async-start(bf16[4,640,384]{2,1,0:T(8,128)(2,1)} %out_projection.1), calls=%async_computation.3 | async-start | bytes 3932160 | tf_op jit(solution)/shard_map/all_to_all | solution.py:460
  237.5 24.5 %all-to-all-done.3 = bf16[4,640,384]{2,1,0:T(8,128)(2,1)} async-done(((bf16[4,640,384]{2,1,0:T(8,128)(2,1)}), bf16[4,640,384]{2,1,0:T(8,128)(2,1)}, u32[]{:S(2)}, u32[]{:S(2)}) %all-to-all-start.3) | async-done | bytes 1966112 | tf_op jit(solution)/shard_map/all_to_all | solution.py:460
  262.0 2.0 convert_reduce_fusion
  (127 shorter events, 16.4 us)
Async XLA Ops:
  7.2 15.3 %copy-start = (bf16[128,1280]{1,0:T(8,128)(2,1)S(1)}, bf16[128,1280]{1,0:T(8,128)(2,1)}, u32[]{:S(2)}) copy-start(bf16[128,1280]{1,0:T(8,128)(2,1)} %param.17) | copy-start | bytes 983044
  7.2 11.1 %collective-permute-start = (bf16[512,384]{1,0:T(8,128)(2,1)}, bf16[512,384]{1,0:T(8,128)(2,1)S(1)}, u32[]{:S(2)}, u32[]{:S(2)}) collective-permute-start(bf16[512,384]{1,0:T(8,128)(2,1)} %refs_0_.1), channel_id=1, source_target_pairs={{0,1},{1,0},{2,3},{3,2},{4,5},{5,4},{6,7},{7,6},{8,9},{9,8},{10,11... | collective-permute-start | bytes 1179656 | tf_op jit(solution)/shard_map/ppermute | solution.py:22
  8.9 12.7 %collective-permute-start.1 = (bf16[512,384]{1,0:T(8,128)(2,1)}, bf16[512,384]{1,0:T(8,128)(2,1)S(1)}, u32[]{:S(2)}, u32[]{:S(2)}) collective-permute-start(bf16[512,384]{1,0:T(8,128)(2,1)} %refs_0_.1), channel_id=1, source_target_pairs={{0,2},{2,4},{4,6},{6,0},{1,3},{3,5},{5,7},{7,1},{8,10},{10,12},{12... | collective-permute-start | bytes 1179656 | tf_op jit(solution)/shard_map/ppermute | solution.py:22
  10.4 11.2 %collective-permute-start.2 = (bf16[512,384]{1,0:T(8,128)(2,1)}, bf16[512,384]{1,0:T(8,128)(2,1)S(1)}, u32[]{:S(2)}, u32[]{:S(2)}) collective-permute-start(bf16[512,384]{1,0:T(8,128)(2,1)} %refs_0_.1), channel_id=1, source_target_pairs={{0,6},{2,0},{4,2},{6,4},{1,7},{3,1},{5,3},{7,5},{8,14},{10,8},{12,... | collective-permute-start | bytes 1179656 | tf_op jit(solution)/shard_map/ppermute | solution.py:22
  13.4 43.4 %collective-permute-start.5 = (bf16[6,192,384]{2,1,0:T(8,128)(2,1)S(1)}, bf16[6,192,384]{2,1,0:T(8,128)(2,1)S(1)}, u32[]{:S(2)}, u32[]{:S(2)}) collective-permute-start(bf16[6,192,384]{2,1,0:T(8,128)(2,1)S(1)} %maximum_bitcast_fusion.refs_1_), channel_id=1, source_target_pairs={{0,16},{16,32},{32,48},{48,0},{1,17},{17,33},{33,49},{49,1},{2,18}... | collective-permute-start | bytes 2654216 | tf_op jit(solution)/shard_map/ppermute | solution.py:22
  15.4 41.4 %collective-permute-start.6 = (bf16[6,192,384]{2,1,0:T(8,128)(2,1)S(1)}, bf16[6,192,384]{2,1,0:T(8,128)(2,1)}, u32[]{:S(2)}, u32[]{:S(2)}) collective-permute-start(bf16[6,192,384]{2,1,0:T(8,128)(2,1)S(1)} %maximum_bitcast_fusion.refs_1_), channel_id=1, source_target_pairs={{0,48},{16,0},{32,16},{48,32},{1,49},{17,1},{33,17},{49,33},{2,50}... | collective-permute-start | bytes 2654216 | tf_op jit(solution)/shard_map/ppermute | solution.py:22
  18.2 19.0 %copy-start.4 = (bf16[512,384]{1,0:T(8,128)(2,1)}, bf16[512,384]{1,0:T(8,128)(2,1)S(1)}, u32[]{:S(2)}) copy-start(bf16[512,384]{1,0:T(8,128)(2,1)S(1)} %collective-permute-done.refs_4_) | copy-start | bytes 1179652
  18.2 39.3 %collective-permute-start.7 = (bf16[6,192,384]{2,1,0:T(8,128)(2,1)S(1)}, bf16[6,192,384]{2,1,0:T(8,128)(2,1)}, u32[]{:S(2)}, u32[]{:S(2)}) collective-permute-start(bf16[6,192,384]{2,1,0:T(8,128)(2,1)S(1)} %maximum_bitcast_fusion.refs_1_), channel_id=1, source_target_pairs={{0,64},{64,0},{1,65},{65,1},{2,66},{66,2},{3,67},{67,3},{4,68},{68... | collective-permute-start | bytes 2654216 | tf_op jit(solution)/shard_map/ppermute | solution.py:22
  21.6 51.7 %copy-start.6 = (bf16[512,384]{1,0:T(8,128)(2,1)}, bf16[512,384]{1,0:T(8,128)(2,1)S(1)}, u32[]{:S(2)}) copy-start(bf16[512,384]{1,0:T(8,128)(2,1)S(1)} %collective-permute-done.1.refs_1_) | copy-start | bytes 1179652
  28.4 10.2 %copy-start.26 = (bf16[384,192]{0,1:T(8,128)(2,1)S(1)}, bf16[384,192]{0,1:T(8,128)(2,1)}, u32[]{:S(2)}) copy-start(bf16[384,192]{0,1:T(8,128)(2,1)} %param.30) | copy-start | bytes 442372
  28.4 10.2 %copy-start.27 = (bf16[384,192]{0,1:T(8,128)(2,1)S(1)}, bf16[384,192]{0,1:T(8,128)(2,1)}, u32[]{:S(2)}) copy-start(bf16[384,192]{0,1:T(8,128)(2,1)} %param.29) | copy-start | bytes 442372
  30.7 36.4 %copy-start.28 = (bf16[128,448]{0,1:T(8,128)(2,1)S(1)}, bf16[128,448]{0,1:T(8,128)(2,1)}, u32[]{:S(2)}) copy-start(bf16[128,448]{0,1:T(8,128)(2,1)} %param.19) | copy-start | bytes 344068
  30.7 26.9 %all-to-all-start = ((bf16[8,128,448]{1,2,0:T(8,128)(2,1)}), bf16[8,128,448]{1,2,0:T(8,128)(2,1)}, u32[]{:S(2)}, u32[]{:S(2)}) async-start(bf16[8,128,448]{1,2,0:T(8,128)(2,1)} %bitcast.55), calls=%async_computation | async-start | bytes 1835008 | tf_op jit(solution)/shard_map/all_to_all | solution.py:388
  35.2 191.5 %all-gather.3.cloned.1.call-start = ((), (), s32[]{:S(2)}) async-start(), calls=%async_computation.4 | async-start | bytes 5013504 | tf_op jit(solution)/shard_map/all_gather | solution.py:402
  35.3 20.7 %collective-permute-start.3 = (bf16[512,384]{1,0:T(8,128)(2,1)S(1)}, bf16[512,384]{1,0:T(8,128)(2,1)S(1)}, u32[]{:S(2)}, u32[]{:S(2)}) collective-permute-start(bf16[512,384]{1,0:T(8,128)(2,1)S(1)} %collective-permute-done.refs_4_), channel_id=1, source_target_pairs={{0,2},{2,4},{4,6},{6,0},{1,3},{3,5},{5,7},{7,1},{8,10},{10,12},{12... | collective-permute-start | bytes 1179656 | tf_op jit(solution)/shard_map/ppermute | solution.py:22
  37.2 19.5 %collective-permute-start.4 = (bf16[512,384]{1,0:T(8,128)(2,1)S(1)}, bf16[512,384]{1,0:T(8,128)(2,1)S(1)}, u32[]{:S(2)}, u32[]{:S(2)}) collective-permute-start(bf16[512,384]{1,0:T(8,128)(2,1)S(1)} %collective-permute-done.refs_4_), channel_id=1, source_target_pairs={{0,6},{2,0},{4,2},{6,4},{1,7},{3,1},{5,3},{7,5},{8,14},{10,8},{12,... | collective-permute-start | bytes 1179656 | tf_op jit(solution)/shard_map/ppermute | solution.py:22
  57.6 8.7 %collective-permute-start.12 = (bf16[2,192,384]{2,1,0:T(8,128)(2,1)}, bf16[2,192,384]{2,1,0:T(8,128)(2,1)S(1)}, u32[]{:S(2)}, u32[]{:S(2)}) collective-permute-start(bf16[2,192,384]{2,1,0:T(8,128)(2,1)} %pad_maximum_fusion.3), channel_id=1, source_target_pairs={{0,0},{1,16},{16,1},{17,17},{32,32},{33,48},{48,33},{49,49},{2,2},... | collective-permute-start | bytes 884744 | tf_op jit(solution)/shard_map/ppermute | solution.py:401
  59.2 35.4 %collective-permute-start.10 = (bf16[6,192,384]{2,1,0:T(8,128)(2,1)}, bf16[6,192,384]{2,1,0:T(8,128)(2,1)}, u32[]{:S(2)}, u32[]{:S(2)}) collective-permute-start(bf16[6,192,384]{2,1,0:T(8,128)(2,1)} %collective-permute-done.7.refs_5_), channel_id=1, source_target_pairs={{0,16},{16,32},{32,48},{48,0},{1,17},{17,33},{33,49},{49,1},{2,18}... | collective-permute-start | bytes 2654216 | tf_op jit(solution)/shard_map/ppermute | solution.py:22
  62.5 32.2 %collective-permute-start.11 = (bf16[6,192,384]{2,1,0:T(8,128)(2,1)}, bf16[6,192,384]{2,1,0:T(8,128)(2,1)}, u32[]{:S(2)}, u32[]{:S(2)}) collective-permute-start(bf16[6,192,384]{2,1,0:T(8,128)(2,1)} %collective-permute-done.7.refs_5_), channel_id=1, source_target_pairs={{0,48},{16,0},{32,16},{48,32},{1,49},{17,1},{33,17},{49,33},{2,50}... | collective-permute-start | bytes 2654216 | tf_op jit(solution)/shard_map/ppermute | solution.py:22
  66.3 9.0 %copy-start.13 = (bf16[512,384]{1,0:T(8,128)(2,1)S(1)}, bf16[512,384]{1,0:T(8,128)(2,1)}, u32[]{:S(2)}) copy-start(bf16[512,384]{1,0:T(8,128)(2,1)} %copy-done.12) | copy-start | bytes 1179652
  66.3 32.5 %copy-start.30 = (f32[3584]{0:T(1024)S(1)}, f32[3584]{0:T(1024)}, u32[]{:S(2)}) copy-start(f32[3584]{0:T(1024)} %param.20) | copy-start | bytes 43012
  68.2 26.5 %all-to-all-start.1 = ((bf16[8,128,448]{1,2,0:T(8,128)(2,1)}), bf16[8,128,448]{1,2,0:T(8,128)(2,1)}, u32[]{:S(2)}, u32[]{:S(2)}) async-start(bf16[8,128,448]{1,2,0:T(8,128)(2,1)} %broadcast_in_dim.4), calls=%async_computation.1 | async-start | bytes 1835008 | tf_op jit(solution)/shard_map/all_to_all | solution.py:32
  73.3 19.8 %collective-permute-start.8 = (bf16[512,384]{1,0:T(8,128)(2,1)S(1)}, bf16[512,384]{1,0:T(8,128)(2,1)S(1)}, u32[]{:S(2)}, u32[]{:S(2)}) collective-permute-start(bf16[512,384]{1,0:T(8,128)(2,1)S(1)} %collective-permute-done.1.refs_1_), channel_id=1, source_target_pairs={{0,2},{2,4},{4,6},{6,0},{1,3},{3,5},{5,7},{7,1},{8,10},{10,12},{12... | collective-permute-start | bytes 1179656 | tf_op jit(solution)/shard_map/ppermute | solution.py:22
  75.3 18.6 %collective-permute-start.9 = (bf16[512,384]{1,0:T(8,128)(2,1)S(1)}, bf16[512,384]{1,0:T(8,128)(2,1)S(1)}, u32[]{:S(2)}, u32[]{:S(2)}) collective-permute-start(bf16[512,384]{1,0:T(8,128)(2,1)S(1)} %copy-done.13), channel_id=1, source_target_pairs={{0,6},{2,0},{4,2},{6,4},{1,7},{3,1},{5,3},{7,5},{8,14},{10,8},{12,... | collective-permute-start | bytes 1179656 | tf_op jit(solution)/shard_map/ppermute | solution.py:22
  94.6 26.8 %collective-permute-start.13 = (bf16[6,192,384]{2,1,0:T(8,128)(2,1)S(1)}, bf16[6,192,384]{2,1,0:T(8,128)(2,1)}, u32[]{:S(2)}, u32[]{:S(2)}) collective-permute-start(bf16[6,192,384]{2,1,0:T(8,128)(2,1)S(1)} %collective-permute-done.5.refs_2_), channel_id=1, source_target_pairs={{0,16},{16,32},{32,48},{48,0},{1,17},{17,33},{33,49},{49,1},{2,18}... | collective-permute-start | bytes 2654216 | tf_op jit(solution)/shard_map/ppermute | solution.py:22
  95.7 26.3 %collective-permute-start.14 = (bf16[6,192,384]{2,1,0:T(8,128)(2,1)}, bf16[6,192,384]{2,1,0:T(8,128)(2,1)}, u32[]{:S(2)}, u32[]{:S(2)}) collective-permute-start(bf16[6,192,384]{2,1,0:T(8,128)(2,1)} %collective-permute-done.11.refs_7_), channel_id=1, source_target_pairs={{0,48},{16,0},{32,16},{48,32},{1,49},{17,1},{33,17},{49,33},{2,50}... | collective-permute-start | bytes 2654216 | tf_op jit(solution)/shard_map/ppermute | solution.py:22
  98.3 23.9 %collective-permute-start.15 = (bf16[6,192,384]{2,1,0:T(8,128)(2,1)S(1)}, bf16[6,192,384]{2,1,0:T(8,128)(2,1)}, u32[]{:S(2)}, u32[]{:S(2)}) collective-permute-start(bf16[6,192,384]{2,1,0:T(8,128)(2,1)S(1)} %maximum_bitcast_fusion.refs_1_), channel_id=1, source_target_pairs={{0,8},{8,0},{1,9},{9,1},{2,10},{10,2},{3,11},{11,3},{4,12},{12,4},... | collective-permute-start | bytes 2654216 | tf_op jit(solution)/shard_map/ppermute | solution.py:22
  98.3 24.3 %collective-permute-start.19 = (bf16[6,192,384]{2,1,0:T(8,128)(2,1)}, bf16[6,192,384]{2,1,0:T(8,128)(2,1)}, u32[]{:S(2)}, u32[]{:S(2)}) collective-permute-start(bf16[6,192,384]{2,1,0:T(8,128)(2,1)} %collective-permute-done.7.refs_5_), channel_id=1, source_target_pairs={{0,8},{8,0},{1,9},{9,1},{2,10},{10,2},{3,11},{11,3},{4,12},{12,4},... | collective-permute-start | bytes 2654216 | tf_op jit(solution)/shard_map/ppermute | solution.py:22
  98.8 23.9 %collective-permute-start.16 = (bf16[6,192,384]{2,1,0:T(8,128)(2,1)S(1)}, bf16[6,192,384]{2,1,0:T(8,128)(2,1)}, u32[]{:S(2)}, u32[]{:S(2)}) collective-permute-start(bf16[6,192,384]{2,1,0:T(8,128)(2,1)S(1)} %collective-permute-done.5.refs_2_), channel_id=1, source_target_pairs={{0,8},{8,0},{1,9},{9,1},{2,10},{10,2},{3,11},{11,3},{4,12},{12,4},... | collective-permute-start | bytes 2654216 | tf_op jit(solution)/shard_map/ppermute | solution.py:22
  100.3 1.8 copy-start.2
  103.1 4.7 %copy-start.3 = (bf16[512,384]{1,0:T(8,128)(2,1)S(1)}, bf16[512,384]{1,0:T(8,128)(2,1)}, u32[]{:S(2)}) copy-start(bf16[512,384]{1,0:T(8,128)(2,1)} %refs_0_.1) | copy-start | bytes 1179652
  103.1 4.7 %copy-start.21 = (f32[4,3072]{1,0:T(4,128)S(1)}, f32[4,3072]{1,0:T(4,128)}, u32[]{:S(2)}) copy-start(f32[4,3072]{1,0:T(4,128)} %mod_ref.2) | copy-start | bytes 147460
  104.1 18.0 %all-to-all-start.2 = ((bf16[8,128,384]{2,1,0:T(8,128)(2,1)}), bf16[8,128,384]{2,1,0:T(8,128)(2,1)S(1)}, u32[]{:S(2)}, u32[]{:S(2)}) async-start(bf16[8,128,384]{2,1,0:T(8,128)(2,1)} %broadcast_in_dim.5), calls=%async_computation.2 | async-start | bytes 1572864 | tf_op jit(solution)/shard_map/all_to_all | solution.py:32
  107.8 1.0 copy-start.5
  109.8 1.0 copy-start.9
  114.8 8.3 %copy-start.33 = (s32[128]{0:T(128)S(1)}, s32[128]{0:T(128)}, u32[]{:S(2)}) copy-start(s32[128]{0:T(128)} %param.31) | copy-start | bytes 1540
  114.8 8.4 %copy-start.31 = (f32[128]{0:T(128)S(1)}, f32[128]{0:T(128)}, u32[]{:S(2)}) copy-start(f32[128]{0:T(128)} %param.26) | copy-start | bytes 1540
  114.8 8.4 %copy-start.32 = (f32[128]{0:T(128)S(1)}, f32[128]{0:T(128)}, u32[]{:S(2)}) copy-start(f32[128]{0:T(128)} %param.25) | copy-start | bytes 1540
  121.4 8.3 %copy-start.20 = (f32[4,3072]{1,0:T(4,128)S(1)}, f32[4,3072]{1,0:T(4,128)}, u32[]{:S(2)}) copy-start(f32[4,3072]{1,0:T(4,128)} %mod_ref.3) | copy-start | bytes 147460
  121.5 3.3 %collective-permute-start.21 = (bf16[6,192,384]{2,1,0:T(8,128)(2,1)}, bf16[6,192,384]{2,1,0:T(8,128)(2,1)}, u32[]{:S(2)}, u32[]{:S(2)}) collective-permute-start(bf16[6,192,384]{2,1,0:T(8,128)(2,1)} %collective-permute-done.11.refs_7_), channel_id=1, source_target_pairs={{0,8},{8,0},{1,9},{9,1},{2,10},{10,2},{3,11},{11,3},{4,12},{12,4},... | collective-permute-start | bytes 2654216 | tf_op jit(solution)/shard_map/ppermute | solution.py:22
  122.0 3.8 %collective-permute-start.17 = (bf16[6,192,384]{2,1,0:T(8,128)(2,1)}, bf16[6,192,384]{2,1,0:T(8,128)(2,1)}, u32[]{:S(2)}, u32[]{:S(2)}) collective-permute-start(bf16[6,192,384]{2,1,0:T(8,128)(2,1)} %collective-permute-done.6.refs_3_), channel_id=1, source_target_pairs={{0,8},{8,0},{1,9},{9,1},{2,10},{10,2},{3,11},{11,3},{4,12},{12,4},... | collective-permute-start | bytes 2654216 | tf_op jit(solution)/shard_map/ppermute | solution.py:22
  122.2 4.9 %collective-permute-start.20 = (bf16[6,192,384]{2,1,0:T(8,128)(2,1)}, bf16[6,192,384]{2,1,0:T(8,128)(2,1)}, u32[]{:S(2)}, u32[]{:S(2)}) collective-permute-start(bf16[6,192,384]{2,1,0:T(8,128)(2,1)} %collective-permute-done.10.refs_6_), channel_id=1, source_target_pairs={{0,8},{8,0},{1,9},{9,1},{2,10},{10,2},{3,11},{11,3},{4,12},{12,4},... | collective-permute-start | bytes 2654216 | tf_op jit(solution)/shard_map/ppermute | solution.py:22
  122.6 5.8 %collective-permute-start.18 = (bf16[6,192,384]{2,1,0:T(8,128)(2,1)}, bf16[6,192,384]{2,1,0:T(8,128)(2,1)}, u32[]{:S(2)}, u32[]{:S(2)}) collective-permute-start(bf16[6,192,384]{2,1,0:T(8,128)(2,1)} %collective-permute-done.13.refs_4_), channel_id=1, source_target_pairs={{0,8},{8,0},{1,9},{9,1},{2,10},{10,2},{3,11},{11,3},{4,12},{12,4},... | collective-permute-start | bytes 2654216 | tf_op jit(solution)/shard_map/ppermute | solution.py:22
  122.7 7.0 %collective-permute-start.22 = (bf16[6,192,384]{2,1,0:T(8,128)(2,1)}, bf16[6,192,384]{2,1,0:T(8,128)(2,1)}, u32[]{:S(2)}, u32[]{:S(2)}) collective-permute-start(bf16[6,192,384]{2,1,0:T(8,128)(2,1)} %collective-permute-done.14.refs_8_), channel_id=1, source_target_pairs={{0,8},{8,0},{1,9},{9,1},{2,10},{10,2},{3,11},{11,3},{4,12},{12,4},... | collective-permute-start | bytes 2654216 | tf_op jit(solution)/shard_map/ppermute | solution.py:22
  142.1 5.6 %collective-permute-start.24 = (bf16[640,384]{1,0:T(8,128)(2,1)S(1)}, bf16[640,384]{1,0:T(8,128)(2,1)S(1)}, u32[]{:S(2)}, u32[]{:S(2)}) collective-permute-start(bf16[640,384]{1,0:T(8,128)(2,1)S(1)} %get-tuple-element.99.refs_0_), channel_id=1, source_target_pairs={{0,8},{8,0},{1,9},{9,1},{2,10},{10,2},{3,11},{11,3},{4,12},{12,4},... | collective-permute-start | bytes 1474568 | tf_op jit(solution)/shard_map/ppermute | solution.py:22
  142.6 14.7 %collective-permute-start.23 = (bf16[640,384]{1,0:T(8,128)(2,1)S(1)}, bf16[640,384]{1,0:T(8,128)(2,1)S(1)}, u32[]{:S(2)}, u32[]{:S(2)}) collective-permute-start(bf16[640,384]{1,0:T(8,128)(2,1)S(1)} %get-tuple-element.99.refs_0_), channel_id=1, source_target_pairs={{0,64},{64,0},{1,65},{65,1},{2,66},{66,2},{3,67},{67,3},{4,68},{68... | collective-permute-start | bytes 1474568 | tf_op jit(solution)/shard_map/ppermute | solution.py:22
  144.5 25.0 %collective-permute-start.26 = (bf16[2,640,384]{2,1,0:T(8,128)(2,1)}, bf16[2,640,384]{2,1,0:T(8,128)(2,1)S(1)}, u32[]{:S(2)}, u32[]{:S(2)}) collective-permute-start(bf16[2,640,384]{2,1,0:T(8,128)(2,1)} %get-tuple-element.100.refs_2_.refs_3_), channel_id=1, source_target_pairs={{0,16},{16,32},{32,48},{48,0},{1,17},{17,33},{33,49},{49,1},{2,18}... | collective-permute-start | bytes 2949128 | tf_op jit(solution)/shard_map/ppermute | solution.py:22
  144.8 24.6 %collective-permute-start.27 = (bf16[2,640,384]{2,1,0:T(8,128)(2,1)}, bf16[2,640,384]{2,1,0:T(8,128)(2,1)S(1)}, u32[]{:S(2)}, u32[]{:S(2)}) collective-permute-start(bf16[2,640,384]{2,1,0:T(8,128)(2,1)} %get-tuple-element.100.refs_2_.refs_3_), channel_id=1, source_target_pairs={{0,48},{16,0},{32,16},{48,32},{1,49},{17,1},{33,17},{49,33},{2,50}... | collective-permute-start | bytes 2949128 | tf_op jit(solution)/shard_map/ppermute | solution.py:22
  147.7 1.2 copy-start.22
  148.9 10.2 %copy-start.23 = (bf16[2,640,384]{2,1,0:T(8,128)(2,1)S(1)}, bf16[2,640,384]{2,1,0:T(8,128)(2,1)}, u32[]{:S(2)}) copy-start(bf16[2,640,384]{2,1,0:T(8,128)(2,1)} %get-tuple-element.100.refs_2_.refs_3_) | copy-start | bytes 2949124
  157.3 1.9 collective-permute-start.25
  169.5 11.4 %copy-start.19 = (bf16[2,640,384]{2,1,0:T(8,128)(2,1)}, bf16[2,640,384]{2,1,0:T(8,128)(2,1)S(1)}, u32[]{:S(2)}) copy-start(bf16[2,640,384]{2,1,0:T(8,128)(2,1)S(1)} %collective-permute-done.27.refs_3_.refs_5_.refs_6_) | copy-start | bytes 2949124
  169.5 13.5 %collective-permute-start.28 = (bf16[640,384]{1,0:T(8,128)(2,1)S(1)}, bf16[640,384]{1,0:T(8,128)(2,1)S(1)}, u32[]{:S(2)}, u32[]{:S(2)}) collective-permute-start(bf16[640,384]{1,0:T(8,128)(2,1)S(1)} %slice_bitcast_fusion.1), channel_id=1, source_target_pairs={{0,16},{16,32},{32,48},{48,0},{1,17},{17,33},{33,49},{49,1},{2,18}... | collective-permute-start | bytes 1474568 | tf_op jit(solution)/shard_map/ppermute | solution.py:22
  170.5 12.6 %collective-permute-start.29 = (bf16[640,384]{1,0:T(8,128)(2,1)S(1)}, bf16[640,384]{1,0:T(8,128)(2,1)S(1)}, u32[]{:S(2)}, u32[]{:S(2)}) collective-permute-start(bf16[640,384]{1,0:T(8,128)(2,1)S(1)} %slice_bitcast_fusion), channel_id=1, source_target_pairs={{0,48},{16,0},{32,16},{48,32},{1,49},{17,1},{33,17},{49,33},{2,50}... | collective-permute-start | bytes 1474568 | tf_op jit(solution)/shard_map/ppermute | solution.py:22
  188.0 3.2 %collective-permute-start.30 = (f32[640,384]{1,0:T(8,128)S(1)}, f32[640,384]{1,0:T(8,128)S(1)}, u32[]{:S(2)}, u32[]{:S(2)}) collective-permute-start(f32[640,384]{1,0:T(8,128)S(1)} %get-tuple-element.127), channel_id=1, source_target_pairs={{0,8},{8,0},{1,9},{9,1},{2,10},{10,2},{3,11},{11,3},{4,12},{12,4},... | collective-permute-start | bytes 2949128 | tf_op jit(solution)/shard_map/ppermute | solution.py:22
  188.1 3.0 %collective-permute-start.31 = (f32[640,128]{1,0:T(8,128)S(1)}, f32[640,128]{1,0:T(8,128)S(1)}, u32[]{:S(2)}, u32[]{:S(2)}) collective-permute-start(f32[640,128]{1,0:T(8,128)S(1)} %get-tuple-element.129), channel_id=1, source_target_pairs={{0,8},{8,0},{1,9},{9,1},{2,10},{10,2},{3,11},{11,3},{4,12},{12,4},... | collective-permute-start | bytes 983048 | tf_op jit(solution)/shard_map/ppermute | solution.py:22
  191.4 18.4 %collective-permute-start.32 = (bf16[640,512]{1,0:T(8,128)(2,1)S(1)}, bf16[640,512]{1,0:T(8,128)(2,1)S(1)}, u32[]{:S(2)}, u32[]{:S(2)}) collective-permute-start(bf16[640,512]{1,0:T(8,128)(2,1)S(1)} %pad_maximum_fusion), channel_id=1, source_target_pairs={{0,64},{64,0},{1,65},{65,1},{2,66},{66,2},{3,67},{67,3},{4,68},{68... | collective-permute-start | bytes 1966088 | tf_op jit(solution)/shard_map/ppermute | solution.py:22
  209.8 3.0 %collective-permute-start.33 = (f32[640,384]{1,0:T(8,128)S(1)}, f32[640,384]{1,0:T(8,128)S(1)}, u32[]{:S(2)}, u32[]{:S(2)}) collective-permute-start(f32[640,384]{1,0:T(8,128)S(1)} %get-tuple-element.144), channel_id=1, source_target_pairs={{0,8},{8,0},{1,9},{9,1},{2,10},{10,2},{3,11},{11,3},{4,12},{12,4},... | collective-permute-start | bytes 2949128 | tf_op jit(solution)/shard_map/ppermute | solution.py:22
  209.8 3.0 %collective-permute-start.34 = (f32[640,128]{1,0:T(8,128)S(1)}, f32[640,128]{1,0:T(8,128)S(1)}, u32[]{:S(2)}, u32[]{:S(2)}) collective-permute-start(f32[640,128]{1,0:T(8,128)S(1)} %get-tuple-element.147), channel_id=1, source_target_pairs={{0,8},{8,0},{1,9},{9,1},{2,10},{10,2},{3,11},{11,3},{4,12},{12,4},... | collective-permute-start | bytes 983048 | tf_op jit(solution)/shard_map/ppermute | solution.py:22
  213.4 13.3 %collective-permute-start.35 = (bf16[640,384]{1,0:T(8,128)(2,1)S(1)}, bf16[640,384]{1,0:T(8,128)(2,1)S(1)}, u32[]{:S(2)}, u32[]{:S(2)}) collective-permute-start(bf16[640,384]{1,0:T(8,128)(2,1)S(1)} %combine.1.own_ref), channel_id=1, source_target_pairs={{0,1},{1,0},{2,3},{3,2},{4,5},{5,4},{6,7},{7,6},{8,9},{9,8},{10,11... | collective-permute-start | bytes 1474568 | tf_op jit(solution)/shard_map/ppermute | solution.py:22
  232.7 29.3 %all-to-all-start.3 = ((bf16[4,640,384]{2,1,0:T(8,128)(2,1)}), bf16[4,640,384]{2,1,0:T(8,128)(2,1)}, u32[]{:S(2)}, u32[]{:S(2)}) async-start(bf16[4,640,384]{2,1,0:T(8,128)(2,1)} %out_projection.1), calls=%async_computation.3 | async-start | bytes 3932160 | tf_op jit(solution)/shard_map/all_to_all | solution.py:460
  237.3 26.6 %copy-start.29 = (bf16[128,384]{1,0:T(8,128)(2,1)S(1)}, bf16[128,384]{1,0:T(8,128)(2,1)}, u32[]{:S(2)}) copy-start(bf16[128,384]{1,0:T(8,128)(2,1)} %param.33) | copy-start | bytes 294916
  237.3 27.3 %copy-start.24 = (bf16[512,384]{1,0:T(8,128)(2,1)S(1)}, bf16[512,384]{1,0:T(8,128)(2,1)}, u32[]{:S(2)}) copy-start(bf16[512,384]{1,0:T(8,128)(2,1)} %param.32) | copy-start | bytes 1179652
  262.0 3.6 %copy-start.1 = (bf16[128,1280]{1,0:T(8,128)(2,1)S(1)}, bf16[128,1280]{1,0:T(8,128)(2,1)}, u32[]{:S(2)}) copy-start(bf16[128,1280]{1,0:T(8,128)(2,1)} %param.17) | copy-start | bytes 983044
  (11 other events, 9.6 us)
Sparse Core Ops, SparseCore 0:
  67.2 70.3 all-gather.2

commit v4 on v3

--- a/solution.py
+++ b/solution.py
@@ -36,7 +36,7 @@
     return jnp.stack([jnp.asarray(p, jnp.int32) for p in places])
 
 
-def params(mib=48):
+def params(mib):
     return pltpu.CompilerParams(vmem_limit_bytes=mib * 1024 * 1024)
 
 
@@ -66,7 +66,7 @@
         out_shape=jax.ShapeDtypeStruct((rows, proj.shape[1]), BF),
         in_specs=[VMEM] * 3,
         out_specs=VMEM,
-        compiler_params=params(),
+        compiler_params=params(16),
         name="text_projection",
     )(state, gain.reshape(parts, 1, share), proj.reshape(parts, share, proj.shape[1]))
 
@@ -121,7 +121,7 @@
             pltpu.VMEM((count, rows, share), BF),
             pltpu.SemaphoreType.DMA((count,)),
         ],
-        compiler_params=params(),
+        compiler_params=params(16),
         name="modulate",
     )(table(places), mod, *pieces)
 
@@ -202,7 +202,7 @@
             pltpu.VMEM((6, width, share), BF),
             pltpu.SemaphoreType.DMA((2 * count + 2,)),
         ],
-        compiler_params=params(),
+        compiler_params=params(36),
         name="qkv",
     )(table(w_places), mod, cosine, sine, gains, image, text_a, *w_pieces)
 
@@ -273,7 +273,7 @@
             pltpu.VMEM((sum(k_sizes), HD), BF),
             pltpu.VMEM((sum(k_sizes), 2 * HD), BF),
         ],
-        compiler_params=params(),
+        compiler_params=params(24),
         cost_estimate=pl.CostEstimate(
             flops=8 * work, bytes_accessed=8 * nq * rows * width, transcendentals=work // HD
         ),
@@ -298,7 +298,7 @@
         out_shape=jax.ShapeDtypeStruct(num.shape, BF),
         in_specs=[VMEM] * 5,
         out_specs=VMEM,
-        compiler_params=params(),
+        compiler_params=params(16),
         name="combine",
     )(num, other, back, tot, other_tot)
 
@@ -334,7 +334,7 @@
         + [pl.BlockSpec((4,) + weight.shape[1:], lambda x: (x, 0, 0, 0))],
         out_specs=pl.BlockSpec((1, rows, share), lambda x: (x, 0, 0)),
         scratch_shapes=[pltpu.VMEM((rows, 2 * share), BF)],
-        compiler_params=params(),
+        compiler_params=params(24),
         name="out_projection",
     )(table([yl]), own, other, weight)
 

time: 274 us -> 272 us (level)
  Pallas kernels: 59.4 us -> 54.3 us
    unnamed x68 -> x66, local copies, waits for them, and re-layouts: 14.7 us -> 17.4 us
  transfers between devices with their start and end apart: 41 -> 41, of which waited for: 16 -> 16; matrix products, arithmetic and copies ran while one was open for 6% -> 6% of each run, Pallas kernels for 20% -> 19%
where the time goes in v4:
time: 272 us; the launch traced here: 271 us
  waiting for transfers between devices  101 us (37%)
  starting transfers between devices  63.1 us (23%)
  Pallas kernels  54.3 us (20%)
  local copies, waits for them, and re-layouts  23.7 us (9%)
  between operations  14.5 us (5%)
  other arithmetic  8.73 us (3%)
  matrix products  5.96 us (2%)
    ppermute x35, waiting for transfers between devices, shift(): lax.ppermute(value, axis, [(k, (k + step) % size) for k in range(size)])  76.1 us
    ppermute x35, starting transfers between devices, shift(): lax.ppermute(value, axis, [(k, (k + step) % size) for k in range(size)])  43.9 us
    pallas_call x5, Pallas kernels, attention(): pl.pallas_call(functools.partial(attention_kernel, nq, k_sizes, not befor...  32.6 us
    all_to_all x1, waiting for transfers between devices, shards(): got = lax.all_to_all(parts, 'x', split_axis=0, concat_axis=0, tiled=True)  24.5 us
    unnamed x66, local copies, waits for them, and re-layouts  17.4 us
    pallas_call x1, Pallas kernels, qkv(): pl.pallas_call(functools.partial(qkv_kernel, count), out_shape=(jax.Shape...  11.4 us
    all_to_all x2, starting transfers between devices, spread(): return lax.all_to_all(copies, axes, split_axis=0, concat_axis=0, tiled=True)  8.64 us
    dot_general x1, matrix products, shards(): jnp.dot(cond_hidden, cond_down, preferred_element_type=F32).astype(BF)  5.96 us
  transfers between devices with their start and end apart: 41, of which 16 were waited for; matrix products, arithmetic and copies ran while one was open for 6% of the time, Pallas kernels for 19%

profile of v4, /device:TPU:0, one launch (start us, length us, event | category | flops | bytes accessed | tf_op | source)
XLA Modules:
  0.0 270.9 jit_solution(13139889292648555960)
XLA Ops:
  7.2 1.7 collective-permute-start
  8.9 1.5 collective-permute-start.1
  10.4 1.7 collective-permute-start.2
  12.2 1.2 maximum_bitcast_fusion.refs_1_
  13.4 2.0 collective-permute-start.5
  15.4 2.2 collective-permute-start.6
  18.2 3.4 %collective-permute-start.7 = (bf16[6,192,384]{2,1,0:T(8,128)(2,1)S(1)}, bf16[6,192,384]{2,1,0:T(8,128)(2,1)}, u32[]{:S(2)}, u32[]{:S(2)}) collective-permute-start(bf16[6,192,384]{2,1,0:T(8,128)(2,1)S(1)} %maximum_bitcast_fusion.refs_1_), channel_id=1, source_target_pairs={{0,64},{64,0},{1,65},{65,1},{2,66},{66,2},{3,67},{67,3},{4,68},{68... | collective-permute-start | bytes 2654216 | tf_op jit(solution)/shard_map/ppermute | solution.py:22
  22.4 6.0 %convolution_convert_fusion = bf16[128,3584]{1,0:T(8,128)(2,1)} fusion(bf16[128,1280]{1,0:T(8,128)(2,1)S(1)} %copy-done, bf16[1280,3584]{1,0:T(8,128)(2,1)} %param.18), kind=kOutput, calls=%fused_computation | convolution fusion | flops 1174863872 | bytes 10420224 | tf_op jit(solution)/shard_map/dot_general | solution.py:385
  28.4 2.3 copy.34
  30.7 4.5 %all-to-all-start = ((bf16[8,128,448]{1,2,0:T(8,128)(2,1)}), bf16[8,128,448]{1,2,0:T(8,128)(2,1)}, u32[]{:S(2)}, u32[]{:S(2)}) async-start(bf16[8,128,448]{1,2,0:T(8,128)(2,1)} %bitcast.55), calls=%async_computation | async-start | bytes 1835008 | tf_op jit(solution)/shard_map/all_to_all | solution.py:388
  35.2 2.0 collective-permute-start.3
  37.2 1.3 collective-permute-start.4
  39.3 16.7 %collective-permute-done.3.refs_5_ = bf16[512,384]{1,0:T(8,128)(2,1)S(1)} collective-permute-done((bf16[512,384]{1,0:T(8,128)(2,1)S(1)}, bf16[512,384]{1,0:T(8,128)(2,1)S(1)}, u32[]{:S(2)}, u32[]{:S(2)}) %collective-permute-start.3) | collective-permute-done | bytes 393248 | tf_op jit(solution)/shard_map/ppermute | solution.py:22
  57.5 1.6 collective-permute-start.12
  59.1 3.3 %collective-permute-start.10 = (bf16[6,192,384]{2,1,0:T(8,128)(2,1)}, bf16[6,192,384]{2,1,0:T(8,128)(2,1)}, u32[]{:S(2)}, u32[]{:S(2)}) collective-permute-start(bf16[6,192,384]{2,1,0:T(8,128)(2,1)} %collective-permute-done.7.refs_5_), channel_id=1, source_target_pairs={{0,16},{16,32},{32,48},{48,0},{1,17},{17,33},{33,49},{49,1},{2,18}... | collective-permute-start | bytes 2654216 | tf_op jit(solution)/shard_map/ppermute | solution.py:22
  62.4 2.5 collective-permute-start.11
  64.9 1.3 convert_reduce_fusion.1
  67.1 1.0 broadcast_in_dim.4
  68.1 5.1 %all-to-all-start.1 = ((bf16[8,128,448]{1,2,0:T(8,128)(2,1)}), bf16[8,128,448]{1,2,0:T(8,128)(2,1)}, u32[]{:S(2)}, u32[]{:S(2)}) async-start(bf16[8,128,448]{1,2,0:T(8,128)(2,1)} %broadcast_in_dim.4), calls=%async_computation.1 | async-start | bytes 1835008 | tf_op jit(solution)/shard_map/all_to_all | solution.py:32
  73.2 2.0 collective-permute-start.8
  75.2 1.3 collective-permute-start.9
  76.5 16.5 %collective-permute-done.8.refs_3_ = bf16[512,384]{1,0:T(8,128)(2,1)S(1)} collective-permute-done((bf16[512,384]{1,0:T(8,128)(2,1)S(1)}, bf16[512,384]{1,0:T(8,128)(2,1)S(1)}, u32[]{:S(2)}, u32[]{:S(2)}) %collective-permute-start.8) | collective-permute-done | bytes 393248 | tf_op jit(solution)/shard_map/ppermute | solution.py:22
  94.6 1.1 collective-permute-start.13
  95.7 2.6 collective-permute-start.14
  98.8 1.5 copy.35.state_ref
  100.3 1.8 copy-done.4
  104.1 3.5 %all-to-all-start.2 = ((bf16[8,128,384]{2,1,0:T(8,128)(2,1)}), bf16[8,128,384]{2,1,0:T(8,128)(2,1)S(1)}, u32[]{:S(2)}, u32[]{:S(2)}) async-start(bf16[8,128,384]{2,1,0:T(8,128)(2,1)} %broadcast_in_dim.5), calls=%async_computation.2 | async-start | bytes 1572864 | tf_op jit(solution)/shard_map/all_to_all | solution.py:32
  108.8 1.0 copy-done.9
  109.8 1.0 copy-done.11
  110.8 1.0 copy-done.13
  111.8 1.0 copy-done.16
  112.8 1.0 copy-done.18
  113.8 1.0 copy-done.20
  114.8 4.9 %modulate.1.image_ref = bf16[512,3072]{1,0:T(8,128)(2,1)S(1)} custom-call(s32[8]{0:T(128)S(1)} %stack.131.place_ref, f32[4,3072]{1,0:T(4,128)S(1)} %copy-done.22, bf16[512,384]{1,0:T(8,128)(2,1)S(1)} %copy-done.5, bf16[512,384]{1,0:T(8,128)(2,1)S(1)} %copy-done.9, bf16[512,384]{1,0:T(8,128)(2,1)S(1)} %copy-done.11, bf16[512,384]{1,0:T(8,128)(2,1)S(1)} %copy-done.18, ...), custom_call_target="tpu_custom_call" | custom-call | tf_op jit(solution)/shard_map/modulate/pallas_call | solution.py:115
  119.6 1.7 copy-done.2
  123.1 1.2 fusion.7
  124.6 1.1 collective-permute-done.17.refs_11_
  125.6 1.3 collective-permute-done.20.refs_14_
  126.9 1.3 collective-permute-done.18.refs_12_
  128.2 1.4 collective-permute-done.22.refs_16_
  129.5 11.4 %qkv.1 = (bf16[640,384]{1,0:T(8,128)(2,1)S(1)}, bf16[2,640,384]{2,1,0:T(8,128)(2,1)S(1)}) custom-call(s32[16]{0:T(128)S(1)} %stack.116.place_ref, f32[4,3072]{1,0:T(4,128)S(1)} %copy-done.21, f32[640,128]{1,0:T(8,128)S(1)} %get-tuple-element.157.cos_ref, f32[640,128]{1,0:T(8,128)S(1)} %get-tuple-element.158.sin_ref, ...), custom_call_target="tpu_custom_call" | custom-call | tf_op jit(solution)/shard_map/qkv/pallas_call | solution.py:191
  141.4 1.9 collective-permute-start.23
  143.6 2.9 %collective-permute-start.27 = (bf16[2,640,384]{2,1,0:T(8,128)(2,1)S(1)}, bf16[2,640,384]{2,1,0:T(8,128)(2,1)S(1)}, u32[]{:S(2)}, u32[]{:S(2)}) collective-permute-start(bf16[2,640,384]{2,1,0:T(8,128)(2,1)S(1)} %get-tuple-element.100.refs_2_.refs_3_), channel_id=1, source_target_pairs={{0,48},{16,0},{32,16},{48,32},{1,49},{17,1},{33,17},{49,33},{2,50}... | collective-permute-start | bytes 2949128 | tf_op jit(solution)/shard_map/ppermute | solution.py:22
  146.5 4.7 %attention.5 = (f32[640,384]{1,0:T(8,128)S(1)}, f32[640,384]{1,0:T(8,128)S(1)}, f32[640,128]{1,0:T(8,128)S(1)}, f32[640,128]{1,0:T(8,128)S(1)}) custom-call(bf16[640,384]{1,0:T(8,128)(2,1)S(1)} %get-tuple-element.99.refs_0_, bf16[640,384]{1,0:T(8,128)(2,1)S(1)} %collective-permute-done.24.refs_1_, ...), custom_call_target="tpu_custom_call" | custom-call | flops 2516582400 | bytes 3932160 | tf_op jit(solution)/shard_map/attention/pallas_call | solution.py:259
  151.2 4.9 %collective-permute-done.23.refs_0_ = bf16[640,384]{1,0:T(8,128)(2,1)S(1)} collective-permute-done((bf16[640,384]{1,0:T(8,128)(2,1)S(1)}, bf16[640,384]{1,0:T(8,128)(2,1)S(1)}, u32[]{:S(2)}, u32[]{:S(2)}) %collective-permute-start.23) | collective-permute-done | bytes 491552 | tf_op jit(solution)/shard_map/ppermute | solution.py:22
  156.2 1.9 collective-permute-done.25.refs_1_
  158.0 4.7 %attention.6 = (f32[640,384]{1,0:T(8,128)S(1)}, f32[640,384]{1,0:T(8,128)S(1)}, f32[640,128]{1,0:T(8,128)S(1)}, f32[640,128]{1,0:T(8,128)S(1)}) custom-call(bf16[640,384]{1,0:T(8,128)(2,1)S(1)} %collective-permute-done.23.refs_0_, bf16[640,384]{1,0:T(8,128)(2,1)S(1)} %collective-permute-done.25.refs_1_, ...), custom_call_target="tpu_custom_call" | custom-call | flops 2516582400 | bytes 3932160 | tf_op jit(solution)/shard_map/attention/pallas_call | solution.py:259
  162.7 5.3 %collective-permute-done.26.refs_2_.refs_4_.refs_5_ = bf16[2,640,384]{2,1,0:T(8,128)(2,1)S(1)} collective-permute-done((bf16[2,640,384]{2,1,0:T(8,128)(2,1)S(1)}, bf16[2,640,384]{2,1,0:T(8,128)(2,1)S(1)}, u32[]{:S(2)}, u32[]{:S(2)}) %collective-permute-start.26) | collective-permute-done | bytes 983072 | tf_op jit(solution)/shard_map/ppermute | solution.py:22
  169.0 2.7 collective-permute-start.29
  171.7 7.7 %attention.7 = (f32[640,384]{1,0:T(8,128)S(1)}, f32[640,384]{1,0:T(8,128)S(1)}, f32[640,128]{1,0:T(8,128)S(1)}, f32[640,128]{1,0:T(8,128)S(1)}) custom-call(bf16[640,384]{1,0:T(8,128)(2,1)S(1)} %collective-permute-done.23.refs_0_, ...), custom_call_target="tpu_custom_call", output_to_operand_aliasing={{0}: (6, {}), {1}: (7, {}), {2}: (8, {}), {3}: (9, {})} | custom-call | flops 5033164800 | bytes 3932160 | tf_op jit(solution)/shard_map/attention/pallas_call | solution.py:259
  179.4 2.0 collective-permute-done.28
  181.4 4.9 %attention.8 = (f32[640,384]{1,0:T(8,128)S(1)}, f32[640,384]{1,0:T(8,128)S(1)}, f32[640,128]{1,0:T(8,128)S(1)}, f32[640,128]{1,0:T(8,128)S(1)}) custom-call(bf16[640,384]{1,0:T(8,128)(2,1)S(1)} %collective-permute-done.23.refs_0_, ...), custom_call_target="tpu_custom_call", output_to_operand_aliasing={{0}: (4, {}), {1}: (5, {}), {2}: (6, {}), {3}: (7, {})} | custom-call | flops 2516582400 | bytes 3932160 | tf_op jit(solution)/shard_map/attention/pallas_call | solution.py:259
  186.9 2.5 collective-permute-done.31
  189.8 1.8 collective-permute-start.32
  191.6 10.6 %attention.9 = (f32[640,384]{1,0:T(8,128)S(1)}, f32[640,384]{1,0:T(8,128)S(1)}, f32[640,128]{1,0:T(8,128)S(1)}, f32[640,128]{1,0:T(8,128)S(1)}) custom-call(bf16[640,384]{1,0:T(8,128)(2,1)S(1)} %get-tuple-element.99.refs_0_, ...), custom_call_target="tpu_custom_call", output_to_operand_aliasing={{0}: (8, {}), {1}: (9, {}), {2}: (10, {}), {3}: (11, {})} | custom-call | flops 7549747200 | bytes 3932160 | tf_op jit(solution)/shard_map/attention/pallas_call | solution.py:259
  202.2 6.0 %collective-permute-done.32.back_ref = bf16[640,512]{1,0:T(8,128)(2,1)S(1)} collective-permute-done((bf16[640,512]{1,0:T(8,128)(2,1)S(1)}, bf16[640,512]{1,0:T(8,128)(2,1)S(1)}, u32[]{:S(2)}, u32[]{:S(2)}) %collective-permute-start.32) | collective-permute-done | bytes 655392 | tf_op jit(solution)/shard_map/ppermute | solution.py:22
  208.6 2.5 collective-permute-done.34.other_tot_ref
  211.7 1.1 collective-permute-start.35
  212.9 12.2 %collective-permute-done.35.other_ref = bf16[640,384]{1,0:T(8,128)(2,1)S(1)} collective-permute-done((bf16[640,384]{1,0:T(8,128)(2,1)S(1)}, bf16[640,384]{1,0:T(8,128)(2,1)S(1)}, u32[]{:S(2)}, u32[]{:S(2)}) %collective-permute-start.35) | collective-permute-done | bytes 491552 | tf_op jit(solution)/shard_map/ppermute | solution.py:22
  225.1 2.3 copy-done.3
  227.4 3.9 %out_projection.1 = bf16[4,640,384]{2,1,0:T(8,128)(2,1)} custom-call(s32[1]{0:T(128)} %bitcast.place_ref, bf16[640,384]{1,0:T(8,128)(2,1)S(1)} %combine.1.own_ref, bf16[640,384]{1,0:T(8,128)(2,1)S(1)} %collective-permute-done.35.other_ref, bf16[16,2,192,384]{3,2,1,0:T(8,128)(2,1)S(1)} %bitcast.49), custom_call_target="tpu_custom_call" | custom-call | tf_op jit(solution)/shard_map/out_projection/pallas_call | solution.py:329
  231.3 4.4 %all-to-all-start.3 = ((bf16[4,640,384]{2,1,0:T(8,128)(2,1)}), bf16[4,640,384]{2,1,0:T(8,128)(2,1)}, u32[]{:S(2)}, u32[]{:S(2)}) async-start(bf16[4,640,384]{2,1,0:T(8,128)(2,1)} %out_projection.1), calls=%async_computation.3 | async-start | bytes 3932160 | tf_op jit(solution)/shard_map/all_to_all | solution.py:460
  236.0 24.5 %all-to-all-done.3 = bf16[4,640,384]{2,1,0:T(8,128)(2,1)} async-done(((bf16[4,640,384]{2,1,0:T(8,128)(2,1)}), bf16[4,640,384]{2,1,0:T(8,128)(2,1)}, u32[]{:S(2)}, u32[]{:S(2)}) %all-to-all-start.3) | async-done | bytes 1966112 | tf_op jit(solution)/shard_map/all_to_all | solution.py:460
  260.5 2.0 convert_reduce_fusion
  (125 shorter events, 17.2 us)
Async XLA Ops:
  7.2 15.3 %copy-start = (bf16[128,1280]{1,0:T(8,128)(2,1)S(1)}, bf16[128,1280]{1,0:T(8,128)(2,1)}, u32[]{:S(2)}) copy-start(bf16[128,1280]{1,0:T(8,128)(2,1)} %param.17) | copy-start | bytes 983044
  7.2 11.1 %collective-permute-start = (bf16[512,384]{1,0:T(8,128)(2,1)}, bf16[512,384]{1,0:T(8,128)(2,1)S(1)}, u32[]{:S(2)}, u32[]{:S(2)}) collective-permute-start(bf16[512,384]{1,0:T(8,128)(2,1)} %refs_0_.1), channel_id=1, source_target_pairs={{0,1},{1,0},{2,3},{3,2},{4,5},{5,4},{6,7},{7,6},{8,9},{9,8},{10,11... | collective-permute-start | bytes 1179656 | tf_op jit(solution)/shard_map/ppermute | solution.py:22
  8.9 12.7 %collective-permute-start.1 = (bf16[512,384]{1,0:T(8,128)(2,1)}, bf16[512,384]{1,0:T(8,128)(2,1)S(1)}, u32[]{:S(2)}, u32[]{:S(2)}) collective-permute-start(bf16[512,384]{1,0:T(8,128)(2,1)} %refs_0_.1), channel_id=1, source_target_pairs={{0,2},{2,4},{4,6},{6,0},{1,3},{3,5},{5,7},{7,1},{8,10},{10,12},{12... | collective-permute-start | bytes 1179656 | tf_op jit(solution)/shard_map/ppermute | solution.py:22
  10.4 11.2 %collective-permute-start.2 = (bf16[512,384]{1,0:T(8,128)(2,1)}, bf16[512,384]{1,0:T(8,128)(2,1)S(1)}, u32[]{:S(2)}, u32[]{:S(2)}) collective-permute-start(bf16[512,384]{1,0:T(8,128)(2,1)} %refs_0_.1), channel_id=1, source_target_pairs={{0,6},{2,0},{4,2},{6,4},{1,7},{3,1},{5,3},{7,5},{8,14},{10,8},{12,... | collective-permute-start | bytes 1179656 | tf_op jit(solution)/shard_map/ppermute | solution.py:22
  13.4 43.4 %collective-permute-start.5 = (bf16[6,192,384]{2,1,0:T(8,128)(2,1)S(1)}, bf16[6,192,384]{2,1,0:T(8,128)(2,1)S(1)}, u32[]{:S(2)}, u32[]{:S(2)}) collective-permute-start(bf16[6,192,384]{2,1,0:T(8,128)(2,1)S(1)} %maximum_bitcast_fusion.refs_1_), channel_id=1, source_target_pairs={{0,16},{16,32},{32,48},{48,0},{1,17},{17,33},{33,49},{49,1},{2,18}... | collective-permute-start | bytes 2654216 | tf_op jit(solution)/shard_map/ppermute | solution.py:22
  15.4 41.4 %collective-permute-start.6 = (bf16[6,192,384]{2,1,0:T(8,128)(2,1)S(1)}, bf16[6,192,384]{2,1,0:T(8,128)(2,1)}, u32[]{:S(2)}, u32[]{:S(2)}) collective-permute-start(bf16[6,192,384]{2,1,0:T(8,128)(2,1)S(1)} %maximum_bitcast_fusion.refs_1_), channel_id=1, source_target_pairs={{0,48},{16,0},{32,16},{48,32},{1,49},{17,1},{33,17},{49,33},{2,50}... | collective-permute-start | bytes 2654216 | tf_op jit(solution)/shard_map/ppermute | solution.py:22
  18.2 19.0 %copy-start.6 = (bf16[512,384]{1,0:T(8,128)(2,1)}, bf16[512,384]{1,0:T(8,128)(2,1)S(1)}, u32[]{:S(2)}) copy-start(bf16[512,384]{1,0:T(8,128)(2,1)S(1)} %collective-permute-done.refs_4_) | copy-start | bytes 1179652
  18.2 39.3 %collective-permute-start.7 = (bf16[6,192,384]{2,1,0:T(8,128)(2,1)S(1)}, bf16[6,192,384]{2,1,0:T(8,128)(2,1)}, u32[]{:S(2)}, u32[]{:S(2)}) collective-permute-start(bf16[6,192,384]{2,1,0:T(8,128)(2,1)S(1)} %maximum_bitcast_fusion.refs_1_), channel_id=1, source_target_pairs={{0,64},{64,0},{1,65},{65,1},{2,66},{66,2},{3,67},{67,3},{4,68},{68... | collective-permute-start | bytes 2654216 | tf_op jit(solution)/shard_map/ppermute | solution.py:22
  21.6 51.6 %copy-start.8 = (bf16[512,384]{1,0:T(8,128)(2,1)}, bf16[512,384]{1,0:T(8,128)(2,1)S(1)}, u32[]{:S(2)}) copy-start(bf16[512,384]{1,0:T(8,128)(2,1)S(1)} %collective-permute-done.1.refs_1_) | copy-start | bytes 1179652
  28.4 10.2 %copy-start.25 = (bf16[384,192]{0,1:T(8,128)(2,1)S(1)}, bf16[384,192]{0,1:T(8,128)(2,1)}, u32[]{:S(2)}) copy-start(bf16[384,192]{0,1:T(8,128)(2,1)} %param.30) | copy-start | bytes 442372
  28.4 10.2 %copy-start.26 = (bf16[384,192]{0,1:T(8,128)(2,1)S(1)}, bf16[384,192]{0,1:T(8,128)(2,1)}, u32[]{:S(2)}) copy-start(bf16[384,192]{0,1:T(8,128)(2,1)} %param.29) | copy-start | bytes 442372
  30.7 36.4 %copy-start.27 = (bf16[128,448]{0,1:T(8,128)(2,1)S(1)}, bf16[128,448]{0,1:T(8,128)(2,1)}, u32[]{:S(2)}) copy-start(bf16[128,448]{0,1:T(8,128)(2,1)} %param.19) | copy-start | bytes 344068
  30.7 26.9 %all-to-all-start = ((bf16[8,128,448]{1,2,0:T(8,128)(2,1)}), bf16[8,128,448]{1,2,0:T(8,128)(2,1)}, u32[]{:S(2)}, u32[]{:S(2)}) async-start(bf16[8,128,448]{1,2,0:T(8,128)(2,1)} %bitcast.55), calls=%async_computation | async-start | bytes 1835008 | tf_op jit(solution)/shard_map/all_to_all | solution.py:388
  35.2 189.9 %all-gather.3.cloned.1.call-start = ((), (), s32[]{:S(2)}) async-start(), calls=%async_computation.4 | async-start | bytes 5013504 | tf_op jit(solution)/shard_map/all_gather | solution.py:402
  35.2 20.7 %collective-permute-start.3 = (bf16[512,384]{1,0:T(8,128)(2,1)S(1)}, bf16[512,384]{1,0:T(8,128)(2,1)S(1)}, u32[]{:S(2)}, u32[]{:S(2)}) collective-permute-start(bf16[512,384]{1,0:T(8,128)(2,1)S(1)} %collective-permute-done.refs_4_), channel_id=1, source_target_pairs={{0,2},{2,4},{4,6},{6,0},{1,3},{3,5},{5,7},{7,1},{8,10},{10,12},{12... | collective-permute-start | bytes 1179656 | tf_op jit(solution)/shard_map/ppermute | solution.py:22
  37.2 19.5 %collective-permute-start.4 = (bf16[512,384]{1,0:T(8,128)(2,1)S(1)}, bf16[512,384]{1,0:T(8,128)(2,1)S(1)}, u32[]{:S(2)}, u32[]{:S(2)}) collective-permute-start(bf16[512,384]{1,0:T(8,128)(2,1)S(1)} %collective-permute-done.refs_4_), channel_id=1, source_target_pairs={{0,6},{2,0},{4,2},{6,4},{1,7},{3,1},{5,3},{7,5},{8,14},{10,8},{12,... | collective-permute-start | bytes 1179656 | tf_op jit(solution)/shard_map/ppermute | solution.py:22
  57.5 8.8 %collective-permute-start.12 = (bf16[2,192,384]{2,1,0:T(8,128)(2,1)}, bf16[2,192,384]{2,1,0:T(8,128)(2,1)S(1)}, u32[]{:S(2)}, u32[]{:S(2)}) collective-permute-start(bf16[2,192,384]{2,1,0:T(8,128)(2,1)} %pad_maximum_fusion.3), channel_id=1, source_target_pairs={{0,0},{1,16},{16,1},{17,17},{32,32},{33,48},{48,33},{49,49},{2,2},... | collective-permute-start | bytes 884744 | tf_op jit(solution)/shard_map/ppermute | solution.py:401
  59.1 35.4 %collective-permute-start.10 = (bf16[6,192,384]{2,1,0:T(8,128)(2,1)}, bf16[6,192,384]{2,1,0:T(8,128)(2,1)}, u32[]{:S(2)}, u32[]{:S(2)}) collective-permute-start(bf16[6,192,384]{2,1,0:T(8,128)(2,1)} %collective-permute-done.7.refs_5_), channel_id=1, source_target_pairs={{0,16},{16,32},{32,48},{48,0},{1,17},{17,33},{33,49},{49,1},{2,18}... | collective-permute-start | bytes 2654216 | tf_op jit(solution)/shard_map/ppermute | solution.py:22
  62.4 32.1 %collective-permute-start.11 = (bf16[6,192,384]{2,1,0:T(8,128)(2,1)}, bf16[6,192,384]{2,1,0:T(8,128)(2,1)}, u32[]{:S(2)}, u32[]{:S(2)}) collective-permute-start(bf16[6,192,384]{2,1,0:T(8,128)(2,1)} %collective-permute-done.7.refs_5_), channel_id=1, source_target_pairs={{0,48},{16,0},{32,16},{48,32},{1,49},{17,1},{33,17},{49,33},{2,50}... | collective-permute-start | bytes 2654216 | tf_op jit(solution)/shard_map/ppermute | solution.py:22
  66.3 9.0 %copy-start.15 = (bf16[512,384]{1,0:T(8,128)(2,1)S(1)}, bf16[512,384]{1,0:T(8,128)(2,1)}, u32[]{:S(2)}) copy-start(bf16[512,384]{1,0:T(8,128)(2,1)} %copy-done.14) | copy-start | bytes 1179652
  66.3 32.5 %copy-start.29 = (f32[3584]{0:T(1024)S(1)}, f32[3584]{0:T(1024)}, u32[]{:S(2)}) copy-start(f32[3584]{0:T(1024)} %param.20) | copy-start | bytes 43012
  68.1 26.4 %all-to-all-start.1 = ((bf16[8,128,448]{1,2,0:T(8,128)(2,1)}), bf16[8,128,448]{1,2,0:T(8,128)(2,1)}, u32[]{:S(2)}, u32[]{:S(2)}) async-start(bf16[8,128,448]{1,2,0:T(8,128)(2,1)} %broadcast_in_dim.4), calls=%async_computation.1 | async-start | bytes 1835008 | tf_op jit(solution)/shard_map/all_to_all | solution.py:32
  73.2 19.8 %collective-permute-start.8 = (bf16[512,384]{1,0:T(8,128)(2,1)S(1)}, bf16[512,384]{1,0:T(8,128)(2,1)S(1)}, u32[]{:S(2)}, u32[]{:S(2)}) collective-permute-start(bf16[512,384]{1,0:T(8,128)(2,1)S(1)} %collective-permute-done.1.refs_1_), channel_id=1, source_target_pairs={{0,2},{2,4},{4,6},{6,0},{1,3},{3,5},{5,7},{7,1},{8,10},{10,12},{12... | collective-permute-start | bytes 1179656 | tf_op jit(solution)/shard_map/ppermute | solution.py:22
  75.2 18.5 %collective-permute-start.9 = (bf16[512,384]{1,0:T(8,128)(2,1)S(1)}, bf16[512,384]{1,0:T(8,128)(2,1)S(1)}, u32[]{:S(2)}, u32[]{:S(2)}) collective-permute-start(bf16[512,384]{1,0:T(8,128)(2,1)S(1)} %copy-done.15), channel_id=1, source_target_pairs={{0,6},{2,0},{4,2},{6,4},{1,7},{3,1},{5,3},{7,5},{8,14},{10,8},{12,... | collective-permute-start | bytes 1179656 | tf_op jit(solution)/shard_map/ppermute | solution.py:22
  94.6 26.8 %collective-permute-start.13 = (bf16[6,192,384]{2,1,0:T(8,128)(2,1)S(1)}, bf16[6,192,384]{2,1,0:T(8,128)(2,1)}, u32[]{:S(2)}, u32[]{:S(2)}) collective-permute-start(bf16[6,192,384]{2,1,0:T(8,128)(2,1)S(1)} %collective-permute-done.5.refs_2_), channel_id=1, source_target_pairs={{0,16},{16,32},{32,48},{48,0},{1,17},{17,33},{33,49},{49,1},{2,18}... | collective-permute-start | bytes 2654216 | tf_op jit(solution)/shard_map/ppermute | solution.py:22
  95.7 26.2 %collective-permute-start.14 = (bf16[6,192,384]{2,1,0:T(8,128)(2,1)}, bf16[6,192,384]{2,1,0:T(8,128)(2,1)}, u32[]{:S(2)}, u32[]{:S(2)}) collective-permute-start(bf16[6,192,384]{2,1,0:T(8,128)(2,1)} %collective-permute-done.11.refs_7_), channel_id=1, source_target_pairs={{0,48},{16,0},{32,16},{48,32},{1,49},{17,1},{33,17},{49,33},{2,50}... | collective-permute-start | bytes 2654216 | tf_op jit(solution)/shard_map/ppermute | solution.py:22
  98.2 23.7 %collective-permute-start.15 = (bf16[6,192,384]{2,1,0:T(8,128)(2,1)S(1)}, bf16[6,192,384]{2,1,0:T(8,128)(2,1)}, u32[]{:S(2)}, u32[]{:S(2)}) collective-permute-start(bf16[6,192,384]{2,1,0:T(8,128)(2,1)S(1)} %maximum_bitcast_fusion.refs_1_), channel_id=1, source_target_pairs={{0,8},{8,0},{1,9},{9,1},{2,10},{10,2},{3,11},{11,3},{4,12},{12,4},... | collective-permute-start | bytes 2654216 | tf_op jit(solution)/shard_map/ppermute | solution.py:22
  98.2 24.2 %collective-permute-start.19 = (bf16[6,192,384]{2,1,0:T(8,128)(2,1)}, bf16[6,192,384]{2,1,0:T(8,128)(2,1)}, u32[]{:S(2)}, u32[]{:S(2)}) collective-permute-start(bf16[6,192,384]{2,1,0:T(8,128)(2,1)} %collective-permute-done.7.refs_5_), channel_id=1, source_target_pairs={{0,8},{8,0},{1,9},{9,1},{2,10},{10,2},{3,11},{11,3},{4,12},{12,4},... | collective-permute-start | bytes 2654216 | tf_op jit(solution)/shard_map/ppermute | solution.py:22
  98.8 23.8 %collective-permute-start.16 = (bf16[6,192,384]{2,1,0:T(8,128)(2,1)S(1)}, bf16[6,192,384]{2,1,0:T(8,128)(2,1)}, u32[]{:S(2)}, u32[]{:S(2)}) collective-permute-start(bf16[6,192,384]{2,1,0:T(8,128)(2,1)S(1)} %collective-permute-done.5.refs_2_), channel_id=1, source_target_pairs={{0,8},{8,0},{1,9},{9,1},{2,10},{10,2},{3,11},{11,3},{4,12},{12,4},... | collective-permute-start | bytes 2654216 | tf_op jit(solution)/shard_map/ppermute | solution.py:22
  100.3 1.8 copy-start.4
  103.1 4.7 %copy-start.5 = (bf16[512,384]{1,0:T(8,128)(2,1)S(1)}, bf16[512,384]{1,0:T(8,128)(2,1)}, u32[]{:S(2)}) copy-start(bf16[512,384]{1,0:T(8,128)(2,1)} %refs_0_.1) | copy-start | bytes 1179652
  103.1 4.7 %copy-start.22 = (f32[4,3072]{1,0:T(4,128)S(1)}, f32[4,3072]{1,0:T(4,128)}, u32[]{:S(2)}) copy-start(f32[4,3072]{1,0:T(4,128)} %mod_ref.2) | copy-start | bytes 147460
  104.1 17.9 %all-to-all-start.2 = ((bf16[8,128,384]{2,1,0:T(8,128)(2,1)}), bf16[8,128,384]{2,1,0:T(8,128)(2,1)S(1)}, u32[]{:S(2)}, u32[]{:S(2)}) async-start(bf16[8,128,384]{2,1,0:T(8,128)(2,1)} %broadcast_in_dim.5), calls=%async_computation.2 | async-start | bytes 1572864 | tf_op jit(solution)/shard_map/all_to_all | solution.py:32
  107.8 1.0 copy-start.7
  109.8 1.0 copy-start.11
  110.8 1.0 copy-start.13
  114.7 8.2 %copy-start.32 = (s32[128]{0:T(128)S(1)}, s32[128]{0:T(128)}, u32[]{:S(2)}) copy-start(s32[128]{0:T(128)} %param.31) | copy-start | bytes 1540
  114.8 8.3 %copy-start.30 = (f32[128]{0:T(128)S(1)}, f32[128]{0:T(128)}, u32[]{:S(2)}) copy-start(f32[128]{0:T(128)} %param.26) | copy-start | bytes 1540
  114.8 8.3 %copy-start.31 = (f32[128]{0:T(128)S(1)}, f32[128]{0:T(128)}, u32[]{:S(2)}) copy-start(f32[128]{0:T(128)} %param.25) | copy-start | bytes 1540
  119.6 1.7 copy-start.2
  121.4 8.2 %copy-start.21 = (f32[4,3072]{1,0:T(4,128)S(1)}, f32[4,3072]{1,0:T(4,128)}, u32[]{:S(2)}) copy-start(f32[4,3072]{1,0:T(4,128)} %mod_ref.3) | copy-start | bytes 147460
  121.4 3.2 %collective-permute-start.21 = (bf16[6,192,384]{2,1,0:T(8,128)(2,1)}, bf16[6,192,384]{2,1,0:T(8,128)(2,1)}, u32[]{:S(2)}, u32[]{:S(2)}) collective-permute-start(bf16[6,192,384]{2,1,0:T(8,128)(2,1)} %collective-permute-done.11.refs_7_), channel_id=1, source_target_pairs={{0,8},{8,0},{1,9},{9,1},{2,10},{10,2},{3,11},{11,3},{4,12},{12,4},... | collective-permute-start | bytes 2654216 | tf_op jit(solution)/shard_map/ppermute | solution.py:22
  121.9 3.8 %collective-permute-start.17 = (bf16[6,192,384]{2,1,0:T(8,128)(2,1)}, bf16[6,192,384]{2,1,0:T(8,128)(2,1)}, u32[]{:S(2)}, u32[]{:S(2)}) collective-permute-start(bf16[6,192,384]{2,1,0:T(8,128)(2,1)} %collective-permute-done.6.refs_3_), channel_id=1, source_target_pairs={{0,8},{8,0},{1,9},{9,1},{2,10},{10,2},{3,11},{11,3},{4,12},{12,4},... | collective-permute-start | bytes 2654216 | tf_op jit(solution)/shard_map/ppermute | solution.py:22
  122.0 4.9 %collective-permute-start.20 = (bf16[6,192,384]{2,1,0:T(8,128)(2,1)}, bf16[6,192,384]{2,1,0:T(8,128)(2,1)}, u32[]{:S(2)}, u32[]{:S(2)}) collective-permute-start(bf16[6,192,384]{2,1,0:T(8,128)(2,1)} %collective-permute-done.10.refs_6_), channel_id=1, source_target_pairs={{0,8},{8,0},{1,9},{9,1},{2,10},{10,2},{3,11},{11,3},{4,12},{12,4},... | collective-permute-start | bytes 2654216 | tf_op jit(solution)/shard_map/ppermute | solution.py:22
  122.4 5.8 %collective-permute-start.18 = (bf16[6,192,384]{2,1,0:T(8,128)(2,1)}, bf16[6,192,384]{2,1,0:T(8,128)(2,1)}, u32[]{:S(2)}, u32[]{:S(2)}) collective-permute-start(bf16[6,192,384]{2,1,0:T(8,128)(2,1)} %collective-permute-done.13.refs_4_), channel_id=1, source_target_pairs={{0,8},{8,0},{1,9},{9,1},{2,10},{10,2},{3,11},{11,3},{4,12},{12,4},... | collective-permute-start | bytes 2654216 | tf_op jit(solution)/shard_map/ppermute | solution.py:22
  122.5 7.0 %collective-permute-start.22 = (bf16[6,192,384]{2,1,0:T(8,128)(2,1)}, bf16[6,192,384]{2,1,0:T(8,128)(2,1)}, u32[]{:S(2)}, u32[]{:S(2)}) collective-permute-start(bf16[6,192,384]{2,1,0:T(8,128)(2,1)} %collective-permute-done.14.refs_8_), channel_id=1, source_target_pairs={{0,8},{8,0},{1,9},{9,1},{2,10},{10,2},{3,11},{11,3},{4,12},{12,4},... | collective-permute-start | bytes 2654216 | tf_op jit(solution)/shard_map/ppermute | solution.py:22
  140.9 5.6 %collective-permute-start.24 = (bf16[640,384]{1,0:T(8,128)(2,1)S(1)}, bf16[640,384]{1,0:T(8,128)(2,1)S(1)}, u32[]{:S(2)}, u32[]{:S(2)}) collective-permute-start(bf16[640,384]{1,0:T(8,128)(2,1)S(1)} %get-tuple-element.99.refs_0_), channel_id=1, source_target_pairs={{0,8},{8,0},{1,9},{9,1},{2,10},{10,2},{3,11},{11,3},{4,12},{12,4},... | collective-permute-start | bytes 1474568 | tf_op jit(solution)/shard_map/ppermute | solution.py:22
  141.4 14.8 %collective-permute-start.23 = (bf16[640,384]{1,0:T(8,128)(2,1)S(1)}, bf16[640,384]{1,0:T(8,128)(2,1)S(1)}, u32[]{:S(2)}, u32[]{:S(2)}) collective-permute-start(bf16[640,384]{1,0:T(8,128)(2,1)S(1)} %get-tuple-element.99.refs_0_), channel_id=1, source_target_pairs={{0,64},{64,0},{1,65},{65,1},{2,66},{66,2},{3,67},{67,3},{4,68},{68... | collective-permute-start | bytes 1474568 | tf_op jit(solution)/shard_map/ppermute | solution.py:22
  143.3 24.7 %collective-permute-start.26 = (bf16[2,640,384]{2,1,0:T(8,128)(2,1)S(1)}, bf16[2,640,384]{2,1,0:T(8,128)(2,1)S(1)}, u32[]{:S(2)}, u32[]{:S(2)}) collective-permute-start(bf16[2,640,384]{2,1,0:T(8,128)(2,1)S(1)} %get-tuple-element.100.refs_2_.refs_3_), channel_id=1, source_target_pairs={{0,16},{16,32},{32,48},{48,0},{1,17},{17,33},{33,49},{49,1},{2,18}... | collective-permute-start | bytes 2949128 | tf_op jit(solution)/shard_map/ppermute | solution.py:22
  143.6 24.4 %collective-permute-start.27 = (bf16[2,640,384]{2,1,0:T(8,128)(2,1)S(1)}, bf16[2,640,384]{2,1,0:T(8,128)(2,1)S(1)}, u32[]{:S(2)}, u32[]{:S(2)}) collective-permute-start(bf16[2,640,384]{2,1,0:T(8,128)(2,1)S(1)} %get-tuple-element.100.refs_2_.refs_3_), channel_id=1, source_target_pairs={{0,48},{16,0},{32,16},{48,32},{1,49},{17,1},{33,17},{49,33},{2,50}... | collective-permute-start | bytes 2949128 | tf_op jit(solution)/shard_map/ppermute | solution.py:22
  156.2 1.9 collective-permute-start.25
  168.0 13.3 %collective-permute-start.28 = (bf16[640,384]{1,0:T(8,128)(2,1)S(1)}, bf16[640,384]{1,0:T(8,128)(2,1)S(1)}, u32[]{:S(2)}, u32[]{:S(2)}) collective-permute-start(bf16[640,384]{1,0:T(8,128)(2,1)S(1)} %slice_bitcast_fusion.1), channel_id=1, source_target_pairs={{0,16},{16,32},{32,48},{48,0},{1,17},{17,33},{33,49},{49,1},{2,18}... | collective-permute-start | bytes 1474568 | tf_op jit(solution)/shard_map/ppermute | solution.py:22
  169.0 12.4 %collective-permute-start.29 = (bf16[640,384]{1,0:T(8,128)(2,1)S(1)}, bf16[640,384]{1,0:T(8,128)(2,1)S(1)}, u32[]{:S(2)}, u32[]{:S(2)}) collective-permute-start(bf16[640,384]{1,0:T(8,128)(2,1)S(1)} %slice_bitcast_fusion), channel_id=1, source_target_pairs={{0,48},{16,0},{32,16},{48,32},{1,49},{17,1},{33,17},{49,33},{2,50}... | collective-permute-start | bytes 1474568 | tf_op jit(solution)/shard_map/ppermute | solution.py:22
  186.3 3.2 %collective-permute-start.30 = (f32[640,384]{1,0:T(8,128)S(1)}, f32[640,384]{1,0:T(8,128)S(1)}, u32[]{:S(2)}, u32[]{:S(2)}) collective-permute-start(f32[640,384]{1,0:T(8,128)S(1)} %get-tuple-element.127), channel_id=1, source_target_pairs={{0,8},{8,0},{1,9},{9,1},{2,10},{10,2},{3,11},{11,3},{4,12},{12,4},... | collective-permute-start | bytes 2949128 | tf_op jit(solution)/shard_map/ppermute | solution.py:22
  186.4 3.0 %collective-permute-start.31 = (f32[640,128]{1,0:T(8,128)S(1)}, f32[640,128]{1,0:T(8,128)S(1)}, u32[]{:S(2)}, u32[]{:S(2)}) collective-permute-start(f32[640,128]{1,0:T(8,128)S(1)} %get-tuple-element.129), channel_id=1, source_target_pairs={{0,8},{8,0},{1,9},{9,1},{2,10},{10,2},{3,11},{11,3},{4,12},{12,4},... | collective-permute-start | bytes 983048 | tf_op jit(solution)/shard_map/ppermute | solution.py:22
  189.8 18.4 %collective-permute-start.32 = (bf16[640,512]{1,0:T(8,128)(2,1)S(1)}, bf16[640,512]{1,0:T(8,128)(2,1)S(1)}, u32[]{:S(2)}, u32[]{:S(2)}) collective-permute-start(bf16[640,512]{1,0:T(8,128)(2,1)S(1)} %pad_maximum_fusion), channel_id=1, source_target_pairs={{0,64},{64,0},{1,65},{65,1},{2,66},{66,2},{3,67},{67,3},{4,68},{68... | collective-permute-start | bytes 1966088 | tf_op jit(solution)/shard_map/ppermute | solution.py:22
  208.1 3.0 %collective-permute-start.33 = (f32[640,384]{1,0:T(8,128)S(1)}, f32[640,384]{1,0:T(8,128)S(1)}, u32[]{:S(2)}, u32[]{:S(2)}) collective-permute-start(f32[640,384]{1,0:T(8,128)S(1)} %get-tuple-element.144), channel_id=1, source_target_pairs={{0,8},{8,0},{1,9},{9,1},{2,10},{10,2},{3,11},{11,3},{4,12},{12,4},... | collective-permute-start | bytes 2949128 | tf_op jit(solution)/shard_map/ppermute | solution.py:22
  208.1 3.0 %collective-permute-start.34 = (f32[640,128]{1,0:T(8,128)S(1)}, f32[640,128]{1,0:T(8,128)S(1)}, u32[]{:S(2)}, u32[]{:S(2)}) collective-permute-start(f32[640,128]{1,0:T(8,128)S(1)} %get-tuple-element.147), channel_id=1, source_target_pairs={{0,8},{8,0},{1,9},{9,1},{2,10},{10,2},{3,11},{11,3},{4,12},{12,4},... | collective-permute-start | bytes 983048 | tf_op jit(solution)/shard_map/ppermute | solution.py:22
  211.7 13.3 %collective-permute-start.35 = (bf16[640,384]{1,0:T(8,128)(2,1)S(1)}, bf16[640,384]{1,0:T(8,128)(2,1)S(1)}, u32[]{:S(2)}, u32[]{:S(2)}) collective-permute-start(bf16[640,384]{1,0:T(8,128)(2,1)S(1)} %combine.1.own_ref), channel_id=1, source_target_pairs={{0,1},{1,0},{2,3},{3,2},{4,5},{5,4},{6,7},{7,6},{8,9},{9,8},{10,11... | collective-permute-start | bytes 1474568 | tf_op jit(solution)/shard_map/ppermute | solution.py:22
  225.1 2.3 copy-start.3
  231.3 29.2 %all-to-all-start.3 = ((bf16[4,640,384]{2,1,0:T(8,128)(2,1)}), bf16[4,640,384]{2,1,0:T(8,128)(2,1)}, u32[]{:S(2)}, u32[]{:S(2)}) async-start(bf16[4,640,384]{2,1,0:T(8,128)(2,1)} %out_projection.1), calls=%async_computation.3 | async-start | bytes 3932160 | tf_op jit(solution)/shard_map/all_to_all | solution.py:460
  235.8 26.7 %copy-start.28 = (bf16[128,384]{1,0:T(8,128)(2,1)S(1)}, bf16[128,384]{1,0:T(8,128)(2,1)}, u32[]{:S(2)}) copy-start(bf16[128,384]{1,0:T(8,128)(2,1)} %param.33) | copy-start | bytes 294916
  235.8 27.4 %copy-start.23 = (bf16[512,384]{1,0:T(8,128)(2,1)S(1)}, bf16[512,384]{1,0:T(8,128)(2,1)}, u32[]{:S(2)}) copy-start(bf16[512,384]{1,0:T(8,128)(2,1)} %param.32) | copy-start | bytes 1179652
  260.5 3.6 %copy-start.1 = (bf16[128,1280]{1,0:T(8,128)(2,1)S(1)}, bf16[128,1280]{1,0:T(8,128)(2,1)}, u32[]{:S(2)}) copy-start(bf16[128,1280]{1,0:T(8,128)(2,1)} %param.17) | copy-start | bytes 983044
  (10 other events, 8.6 us)
Sparse Core Ops, SparseCore 0:
  67.2 70.3 all-gather.2

commit v5 on v4

--- a/solution.py
+++ b/solution.py
@@ -412,10 +412,13 @@
     a_arrays = [image_states, *a_near, a_far[0], a_pair, *a_next, a_far[1]]
     a_places = [(x + d) % 4 * 2 + (yl + p) % 2 for p, d in blocks]
     image_modded = modulate(a_arrays, a_places, image_mod)
-    text_a, w_far, image_modded = together((text_a, w_far, image_modded))
-
+    w_early = [weight, *w_near, w_pair, *w_next]
+    w_swapped = [shift(w, "c", 1) for w in w_early]
+    text_a, w_far, image_modded, w_swapped = together((text_a, w_far, image_modded, w_swapped))
+
+    w_last = [shift(w, "c", 1) for w in w_far]
     w_arrays = [weight, *w_near, w_far[0], w_pair, *w_next, w_far[1]]
-    w_arrays += [shift(w, "c", 1) for w in w_arrays]
+    w_arrays += w_swapped[:3] + w_last[:1] + w_swapped[3:] + w_last[1:]
 
     gains = jnp.stack([query_gain, key_gain])
     image_pos = (seq_index * image_rows + jnp.arange(image_rows)).astype(F32)

time: 272 us -> 284 us (1.044)
  waiting for transfers between devices: 101 us -> 122 us
  starting transfers between devices: 63.1 us -> 58 us
  local copies, waits for them, and re-layouts: 23.7 us -> 18.7 us
    ppermute x35, waiting for transfers between devices: 76.1 us -> 95.1 us  [shift(): lax.ppermute(value, axis, [(k, (k + step) % size) for k in range(size)])]
    unnamed x66 -> x54, local copies, waits for them, and re-layouts: 17.4 us -> 12.3 us
    ppermute x35, starting transfers between devices: 43.9 us -> 39.8 us  [shift(): lax.ppermute(value, axis, [(k, (k + step) % size) for k in range(size)])]
    all_to_all x2, waiting for transfers between devices: 0.01 us -> 2.86 us  [spread(): return lax.all_to_all(copies, axes, split_axis=0, concat_axis=0, tiled=True)]
  transfers between devices with their start and end apart: 41 -> 41, of which waited for: 16 -> 16; matrix products, arithmetic and copies ran while one was open for 6% -> 6% of each run, Pallas kernels for 19% -> 18%
where the time goes in v5:
time: 284 us; the launch traced here: 283 us
  waiting for transfers between devices  122 us (43%)
  starting transfers between devices  58 us (20%)
  Pallas kernels  54.8 us (19%)
  local copies, waits for them, and re-layouts  18.7 us (7%)
  between operations  14.6 us (5%)
  other arithmetic  8.45 us (3%)
  matrix products  6.07 us (2%)
    ppermute x35, waiting for transfers between devices, shift(): lax.ppermute(value, axis, [(k, (k + step) % size) for k in range(size)])  95.1 us
    ppermute x35, starting transfers between devices, shift(): lax.ppermute(value, axis, [(k, (k + step) % size) for k in range(size)])  39.8 us
    pallas_call x5, Pallas kernels, attention(): pl.pallas_call(functools.partial(attention_kernel, nq, k_sizes, not befor...  32.6 us
    all_to_all x1, waiting for transfers between devices, shards(): got = lax.all_to_all(parts, 'x', split_axis=0, concat_axis=0, tiled=True)  24.5 us
    unnamed x54, local copies, waits for them, and re-layouts  12.3 us
    pallas_call x1, Pallas kernels, qkv(): pl.pallas_call(functools.partial(qkv_kernel, count), out_shape=(jax.Shape...  11.4 us
    all_to_all x2, starting transfers between devices, spread(): return lax.all_to_all(copies, axes, split_axis=0, concat_axis=0, tiled=True)  7.78 us
    dot_general x1, matrix products, shards(): jnp.dot(cond_hidden, cond_down, preferred_element_type=F32).astype(BF)  6.07 us
  transfers between devices with their start and end apart: 41, of which 16 were waited for; matrix products, arithmetic and copies ran while one was open for 6% of the time, Pallas kernels for 18%

profile of v5, /device:TPU:0, one launch (start us, length us, event | category | flops | bytes accessed | tf_op | source)
XLA Modules:
  0.0 283.0 jit_solution(16625563903957685461)
XLA Ops:
  7.2 1.7 collective-permute-start
  8.9 1.5 collective-permute-start.1
  10.4 1.7 collective-permute-start.2
  12.2 1.2 maximum_bitcast_fusion.refs_1_
  13.4 2.0 collective-permute-start.5
  15.4 2.2 collective-permute-start.6
  18.2 3.4 %collective-permute-start.7 = (bf16[6,192,384]{2,1,0:T(8,128)(2,1)S(1)}, bf16[6,192,384]{2,1,0:T(8,128)(2,1)}, u32[]{:S(2)}, u32[]{:S(2)}) collective-permute-start(bf16[6,192,384]{2,1,0:T(8,128)(2,1)S(1)} %maximum_bitcast_fusion.refs_1_), channel_id=1, source_target_pairs={{0,64},{64,0},{1,65},{65,1},{2,66},{66,2},{3,67},{67,3},{4,68},{68... | collective-permute-start | bytes 2654216 | tf_op jit(solution)/shard_map/ppermute | solution.py:22
  21.6 6.1 %convolution_convert_fusion = bf16[128,3584]{1,0:T(8,128)(2,1)} fusion(bf16[128,1280]{1,0:T(8,128)(2,1)S(1)} %copy-done, bf16[1280,3584]{1,0:T(8,128)(2,1)} %param.18), kind=kOutput, calls=%fused_computation | convolution fusion | flops 1174863872 | bytes 10420224 | tf_op jit(solution)/shard_map/dot_general | solution.py:385
  27.7 2.3 copy.34
  30.0 4.6 %all-to-all-start = ((bf16[8,128,448]{1,2,0:T(8,128)(2,1)}), bf16[8,128,448]{1,2,0:T(8,128)(2,1)S(1)}, u32[]{:S(2)}, u32[]{:S(2)}) async-start(bf16[8,128,448]{1,2,0:T(8,128)(2,1)} %bitcast.55), calls=%async_computation | async-start | bytes 1835008 | tf_op jit(solution)/shard_map/all_to_all | solution.py:388
  34.5 2.0 collective-permute-start.3
  36.5 1.3 collective-permute-start.4
  37.8 1.7 pad_maximum_fusion.3
  39.5 15.8 %collective-permute-done.3.refs_5_ = bf16[512,384]{1,0:T(8,128)(2,1)S(1)} collective-permute-done((bf16[512,384]{1,0:T(8,128)(2,1)S(1)}, bf16[512,384]{1,0:T(8,128)(2,1)S(1)}, u32[]{:S(2)}, u32[]{:S(2)}) %collective-permute-start.3) | collective-permute-done | bytes 393248 | tf_op jit(solution)/shard_map/ppermute | solution.py:22
  55.3 0.8 copy-done.12
  56.1 2.0 collective-permute-start.10
  58.1 2.2 collective-permute-start.11
  60.4 1.1 broadcast_in_dim.4
  61.5 4.2 %all-to-all-start.1 = ((bf16[8,128,448]{1,2,0:T(8,128)(2,1)}), bf16[8,128,448]{1,2,0:T(8,128)(2,1)}, u32[]{:S(2)}, u32[]{:S(2)}) async-start(bf16[8,128,448]{1,2,0:T(8,128)(2,1)} %broadcast_in_dim.4), calls=%async_computation.1 | async-start | bytes 1835008 | tf_op jit(solution)/shard_map/all_to_all | solution.py:32
  65.8 1.9 collective-permute-start.8
  67.7 1.4 collective-permute-start.9
  69.1 1.4 collective-permute-start.12
  70.5 14.7 %collective-permute-done.8.refs_3_ = bf16[512,384]{1,0:T(8,128)(2,1)S(1)} collective-permute-done((bf16[512,384]{1,0:T(8,128)(2,1)}, bf16[512,384]{1,0:T(8,128)(2,1)S(1)}, u32[]{:S(2)}, u32[]{:S(2)}) %collective-permute-start.8) | collective-permute-done | bytes 393248 | tf_op jit(solution)/shard_map/ppermute | solution.py:22
  86.7 2.9 %collective-permute-start.14 = (bf16[6,192,384]{2,1,0:T(8,128)(2,1)}, bf16[6,192,384]{2,1,0:T(8,128)(2,1)}, u32[]{:S(2)}, u32[]{:S(2)}) collective-permute-start(bf16[6,192,384]{2,1,0:T(8,128)(2,1)} %collective-permute-done.11.refs_7_), channel_id=1, source_target_pairs={{0,48},{16,0},{32,16},{48,32},{1,49},{17,1},{33,17},{49,33},{2,50}... | collective-permute-start | bytes 2654216 | tf_op jit(solution)/shard_map/ppermute | solution.py:22
  89.7 0.9 copy-done.6
  91.1 23.1 %collective-permute-done.13.refs_4_ = bf16[6,192,384]{2,1,0:T(8,128)(2,1)} collective-permute-done((bf16[6,192,384]{2,1,0:T(8,128)(2,1)S(1)}, bf16[6,192,384]{2,1,0:T(8,128)(2,1)}, u32[]{:S(2)}, u32[]{:S(2)}) %collective-permute-start.13) | collective-permute-done | bytes 884768 | tf_op jit(solution)/shard_map/ppermute | solution.py:22
  114.3 1.5 copy.35.state_ref
  115.8 1.8 copy-done.4
  117.6 1.0 text_projection.1
  118.6 1.0 broadcast_in_dim.5
  119.5 3.5 %all-to-all-start.2 = ((bf16[8,128,384]{2,1,0:T(8,128)(2,1)}), bf16[8,128,384]{2,1,0:T(8,128)(2,1)S(1)}, u32[]{:S(2)}, u32[]{:S(2)}) async-start(bf16[8,128,384]{2,1,0:T(8,128)(2,1)} %broadcast_in_dim.5), calls=%async_computation.2 | async-start | bytes 1572864 | tf_op jit(solution)/shard_map/all_to_all | solution.py:32
  123.3 1.0 copy-done.9
  124.3 1.0 copy-done.11
  125.3 1.0 copy-done.13
  126.3 1.0 copy-done.15
  127.3 5.4 %modulate.1.image_ref = bf16[512,3072]{1,0:T(8,128)(2,1)S(1)} custom-call(s32[8]{0:T(128)S(1)} %stack.131.place_ref, f32[4,3072]{1,0:T(4,128)S(1)} %copy-done.17, bf16[512,384]{1,0:T(8,128)(2,1)S(1)} %copy-done.5, bf16[512,384]{1,0:T(8,128)(2,1)} %collective-permute-done.1.refs_1_, bf16[512,384]{1,0:T(8,128)(2,1)S(1)} %copy-done.11, ...), custom_call_target="tpu_custom_call" | custom-call | tf_op jit(solution)/shard_map/modulate/pallas_call | solution.py:115
  132.7 1.7 copy-done.2
  134.4 2.9 %all-to-all-done.2.refs_0_ = bf16[8,128,384]{2,1,0:T(8,128)(2,1)S(1)} async-done(((bf16[8,128,384]{2,1,0:T(8,128)(2,1)}), bf16[8,128,384]{2,1,0:T(8,128)(2,1)S(1)}, u32[]{:S(2)}, u32[]{:S(2)}) %all-to-all-start.2) | async-done | bytes 786464 | tf_op jit(solution)/shard_map/all_to_all | solution.py:32
  138.1 1.2 fusion.7
  140.2 1.3 collective-permute-done.22.refs_16_
  141.4 11.4 %qkv.1 = (bf16[640,384]{1,0:T(8,128)(2,1)S(1)}, bf16[2,640,384]{2,1,0:T(8,128)(2,1)S(1)}) custom-call(s32[16]{0:T(128)S(1)} %stack.116.place_ref, f32[4,3072]{1,0:T(4,128)S(1)} %copy-done.16, f32[640,128]{1,0:T(8,128)S(1)} %get-tuple-element.169.cos_ref, f32[640,128]{1,0:T(8,128)S(1)} %get-tuple-element.170.sin_ref, ...), custom_call_target="tpu_custom_call" | custom-call | tf_op jit(solution)/shard_map/qkv/pallas_call | solution.py:191
  153.1 1.5 collective-permute-start.23
  154.6 3.2 %collective-permute-start.27 = (bf16[2,640,384]{2,1,0:T(8,128)(2,1)S(1)}, bf16[2,640,384]{2,1,0:T(8,128)(2,1)S(1)}, u32[]{:S(2)}, u32[]{:S(2)}) collective-permute-start(bf16[2,640,384]{2,1,0:T(8,128)(2,1)S(1)} %get-tuple-element.112.refs_2_.refs_3_), channel_id=1, source_target_pairs={{0,48},{16,0},{32,16},{48,32},{1,49},{17,1},{33,17},{49,33},{2,50}... | collective-permute-start | bytes 2949128 | tf_op jit(solution)/shard_map/ppermute | solution.py:22
  157.9 4.7 %attention.5 = (f32[640,384]{1,0:T(8,128)S(1)}, f32[640,384]{1,0:T(8,128)S(1)}, f32[640,128]{1,0:T(8,128)S(1)}, f32[640,128]{1,0:T(8,128)S(1)}) custom-call(bf16[640,384]{1,0:T(8,128)(2,1)S(1)} %get-tuple-element.111.refs_0_, bf16[640,384]{1,0:T(8,128)(2,1)S(1)} %collective-permute-done.24.refs_1_, ...), custom_call_target="tpu_custom_call" | custom-call | flops 2516582400 | bytes 3932160 | tf_op jit(solution)/shard_map/attention/pallas_call | solution.py:259
  162.6 5.5 %collective-permute-done.23.refs_0_ = bf16[640,384]{1,0:T(8,128)(2,1)S(1)} collective-permute-done((bf16[640,384]{1,0:T(8,128)(2,1)S(1)}, bf16[640,384]{1,0:T(8,128)(2,1)S(1)}, u32[]{:S(2)}, u32[]{:S(2)}) %collective-permute-start.23) | collective-permute-done | bytes 491552 | tf_op jit(solution)/shard_map/ppermute | solution.py:22
  168.1 1.9 collective-permute-done.25.refs_1_
  169.9 4.7 %attention.6 = (f32[640,384]{1,0:T(8,128)S(1)}, f32[640,384]{1,0:T(8,128)S(1)}, f32[640,128]{1,0:T(8,128)S(1)}, f32[640,128]{1,0:T(8,128)S(1)}) custom-call(bf16[640,384]{1,0:T(8,128)(2,1)S(1)} %collective-permute-done.23.refs_0_, bf16[640,384]{1,0:T(8,128)(2,1)S(1)} %collective-permute-done.25.refs_1_, ...), custom_call_target="tpu_custom_call" | custom-call | flops 2516582400 | bytes 3932160 | tf_op jit(solution)/shard_map/attention/pallas_call | solution.py:259
  174.6 5.0 %collective-permute-done.26.refs_2_.refs_4_.refs_5_ = bf16[2,640,384]{2,1,0:T(8,128)(2,1)S(1)} collective-permute-done((bf16[2,640,384]{2,1,0:T(8,128)(2,1)S(1)}, bf16[2,640,384]{2,1,0:T(8,128)(2,1)S(1)}, u32[]{:S(2)}, u32[]{:S(2)}) %collective-permute-start.26) | collective-permute-done | bytes 983072 | tf_op jit(solution)/shard_map/ppermute | solution.py:22
  179.8 3.5 %collective-permute-start.29 = (bf16[640,384]{1,0:T(8,128)(2,1)S(1)}, bf16[640,384]{1,0:T(8,128)(2,1)S(1)}, u32[]{:S(2)}, u32[]{:S(2)}) collective-permute-start(bf16[640,384]{1,0:T(8,128)(2,1)S(1)} %slice_bitcast_fusion), channel_id=1, source_target_pairs={{0,48},{16,0},{32,16},{48,32},{1,49},{17,1},{33,17},{49,33},{2,50}... | collective-permute-start | bytes 1474568 | tf_op jit(solution)/shard_map/ppermute | solution.py:22
  183.4 7.7 %attention.7 = (f32[640,384]{1,0:T(8,128)S(1)}, f32[640,384]{1,0:T(8,128)S(1)}, f32[640,128]{1,0:T(8,128)S(1)}, f32[640,128]{1,0:T(8,128)S(1)}) custom-call(bf16[640,384]{1,0:T(8,128)(2,1)S(1)} %collective-permute-done.23.refs_0_, ...), custom_call_target="tpu_custom_call", output_to_operand_aliasing={{0}: (6, {}), {1}: (7, {}), {2}: (8, {}), {3}: (9, {})} | custom-call | flops 5033164800 | bytes 3932160 | tf_op jit(solution)/shard_map/attention/pallas_call | solution.py:259
  191.0 2.4 collective-permute-done.28
  193.4 4.9 %attention.8 = (f32[640,384]{1,0:T(8,128)S(1)}, f32[640,384]{1,0:T(8,128)S(1)}, f32[640,128]{1,0:T(8,128)S(1)}, f32[640,128]{1,0:T(8,128)S(1)}) custom-call(bf16[640,384]{1,0:T(8,128)(2,1)S(1)} %collective-permute-done.23.refs_0_, ...), custom_call_target="tpu_custom_call", output_to_operand_aliasing={{0}: (4, {}), {1}: (5, {}), {2}: (6, {}), {3}: (7, {})} | custom-call | flops 2516582400 | bytes 3932160 | tf_op jit(solution)/shard_map/attention/pallas_call | solution.py:259
  198.9 2.5 collective-permute-done.31
  201.8 1.9 collective-permute-start.32
  203.7 10.6 %attention.9 = (f32[640,384]{1,0:T(8,128)S(1)}, f32[640,384]{1,0:T(8,128)S(1)}, f32[640,128]{1,0:T(8,128)S(1)}, f32[640,128]{1,0:T(8,128)S(1)}) custom-call(bf16[640,384]{1,0:T(8,128)(2,1)S(1)} %get-tuple-element.111.refs_0_, ...), custom_call_target="tpu_custom_call", output_to_operand_aliasing={{0}: (8, {}), {1}: (9, {}), {2}: (10, {}), {3}: (11, {})} | custom-call | flops 7549747200 | bytes 3932160 | tf_op jit(solution)/shard_map/attention/pallas_call | solution.py:259
  214.3 5.9 %collective-permute-done.32.back_ref = bf16[640,512]{1,0:T(8,128)(2,1)S(1)} collective-permute-done((bf16[640,512]{1,0:T(8,128)(2,1)S(1)}, bf16[640,512]{1,0:T(8,128)(2,1)S(1)}, u32[]{:S(2)}, u32[]{:S(2)}) %collective-permute-start.32) | collective-permute-done | bytes 655392 | tf_op jit(solution)/shard_map/ppermute | solution.py:22
  220.7 2.5 collective-permute-done.34.other_tot_ref
  224.0 13.1 %collective-permute-done.35.other_ref = bf16[640,384]{1,0:T(8,128)(2,1)S(1)} collective-permute-done((bf16[640,384]{1,0:T(8,128)(2,1)S(1)}, bf16[640,384]{1,0:T(8,128)(2,1)S(1)}, u32[]{:S(2)}, u32[]{:S(2)}) %collective-permute-start.35) | collective-permute-done | bytes 491552 | tf_op jit(solution)/shard_map/ppermute | solution.py:22
  237.1 2.3 copy-done.3
  239.5 3.9 %out_projection.1 = bf16[4,640,384]{2,1,0:T(8,128)(2,1)} custom-call(s32[1]{0:T(128)} %bitcast.place_ref, bf16[640,384]{1,0:T(8,128)(2,1)S(1)} %combine.1.own_ref, bf16[640,384]{1,0:T(8,128)(2,1)S(1)} %collective-permute-done.35.other_ref, bf16[16,2,192,384]{3,2,1,0:T(8,128)(2,1)S(1)} %bitcast.49), custom_call_target="tpu_custom_call" | custom-call | tf_op jit(solution)/shard_map/out_projection/pallas_call | solution.py:329
  243.4 4.4 %all-to-all-start.3 = ((bf16[4,640,384]{2,1,0:T(8,128)(2,1)}), bf16[4,640,384]{2,1,0:T(8,128)(2,1)}, u32[]{:S(2)}, u32[]{:S(2)}) async-start(bf16[4,640,384]{2,1,0:T(8,128)(2,1)} %out_projection.1), calls=%async_computation.3 | async-start | bytes 3932160 | tf_op jit(solution)/shard_map/all_to_all | solution.py:463
  248.0 24.5 %all-to-all-done.3 = bf16[4,640,384]{2,1,0:T(8,128)(2,1)} async-done(((bf16[4,640,384]{2,1,0:T(8,128)(2,1)}), bf16[4,640,384]{2,1,0:T(8,128)(2,1)}, u32[]{:S(2)}, u32[]{:S(2)}) %all-to-all-start.3) | async-done | bytes 1966112 | tf_op jit(solution)/shard_map/all_to_all | solution.py:463
  272.5 2.0 convert_reduce_fusion
  275.2 0.9 fusion.2
  (113 shorter events, 8.2 us)
Async XLA Ops:
  7.2 14.5 %copy-start = (bf16[128,1280]{1,0:T(8,128)(2,1)S(1)}, bf16[128,1280]{1,0:T(8,128)(2,1)}, u32[]{:S(2)}) copy-start(bf16[128,1280]{1,0:T(8,128)(2,1)} %param.17) | copy-start | bytes 983044
  7.2 11.1 %collective-permute-start = (bf16[512,384]{1,0:T(8,128)(2,1)}, bf16[512,384]{1,0:T(8,128)(2,1)S(1)}, u32[]{:S(2)}, u32[]{:S(2)}) collective-permute-start(bf16[512,384]{1,0:T(8,128)(2,1)} %refs_0_.1), channel_id=1, source_target_pairs={{0,1},{1,0},{2,3},{3,2},{4,5},{5,4},{6,7},{7,6},{8,9},{9,8},{10,11... | collective-permute-start | bytes 1179656 | tf_op jit(solution)/shard_map/ppermute | solution.py:22
  8.9 12.7 %collective-permute-start.1 = (bf16[512,384]{1,0:T(8,128)(2,1)}, bf16[512,384]{1,0:T(8,128)(2,1)}, u32[]{:S(2)}, u32[]{:S(2)}) collective-permute-start(bf16[512,384]{1,0:T(8,128)(2,1)} %refs_0_.1), channel_id=1, source_target_pairs={{0,2},{2,4},{4,6},{6,0},{1,3},{3,5},{5,7},{7,1},{8,10},{10,12},{12... | collective-permute-start | bytes 1179656 | tf_op jit(solution)/shard_map/ppermute | solution.py:22
  10.4 11.2 %collective-permute-start.2 = (bf16[512,384]{1,0:T(8,128)(2,1)}, bf16[512,384]{1,0:T(8,128)(2,1)S(1)}, u32[]{:S(2)}, u32[]{:S(2)}) collective-permute-start(bf16[512,384]{1,0:T(8,128)(2,1)} %refs_0_.1), channel_id=1, source_target_pairs={{0,6},{2,0},{4,2},{6,4},{1,7},{3,1},{5,3},{7,5},{8,14},{10,8},{12,... | collective-permute-start | bytes 1179656 | tf_op jit(solution)/shard_map/ppermute | solution.py:22
  13.4 42.6 %collective-permute-start.5 = (bf16[6,192,384]{2,1,0:T(8,128)(2,1)S(1)}, bf16[6,192,384]{2,1,0:T(8,128)(2,1)S(1)}, u32[]{:S(2)}, u32[]{:S(2)}) collective-permute-start(bf16[6,192,384]{2,1,0:T(8,128)(2,1)S(1)} %maximum_bitcast_fusion.refs_1_), channel_id=1, source_target_pairs={{0,16},{16,32},{32,48},{48,0},{1,17},{17,33},{33,49},{49,1},{2,18}... | collective-permute-start | bytes 2654216 | tf_op jit(solution)/shard_map/ppermute | solution.py:22
  15.4 40.6 %collective-permute-start.6 = (bf16[6,192,384]{2,1,0:T(8,128)(2,1)S(1)}, bf16[6,192,384]{2,1,0:T(8,128)(2,1)}, u32[]{:S(2)}, u32[]{:S(2)}) collective-permute-start(bf16[6,192,384]{2,1,0:T(8,128)(2,1)S(1)} %maximum_bitcast_fusion.refs_1_), channel_id=1, source_target_pairs={{0,48},{16,0},{32,16},{48,32},{1,49},{17,1},{33,17},{49,33},{2,50}... | collective-permute-start | bytes 2654216 | tf_op jit(solution)/shard_map/ppermute | solution.py:22
  18.2 18.3 %copy-start.8 = (bf16[512,384]{1,0:T(8,128)(2,1)}, bf16[512,384]{1,0:T(8,128)(2,1)S(1)}, u32[]{:S(2)}) copy-start(bf16[512,384]{1,0:T(8,128)(2,1)S(1)} %collective-permute-done.refs_4_) | copy-start | bytes 1179652
  18.2 37.8 %collective-permute-start.7 = (bf16[6,192,384]{2,1,0:T(8,128)(2,1)S(1)}, bf16[6,192,384]{2,1,0:T(8,128)(2,1)}, u32[]{:S(2)}, u32[]{:S(2)}) collective-permute-start(bf16[6,192,384]{2,1,0:T(8,128)(2,1)S(1)} %maximum_bitcast_fusion.refs_1_), channel_id=1, source_target_pairs={{0,64},{64,0},{1,65},{65,1},{2,66},{66,2},{3,67},{67,3},{4,68},{68... | collective-permute-start | bytes 2654216 | tf_op jit(solution)/shard_map/ppermute | solution.py:22
  21.6 6.1 %copy-start.10 = (bf16[512,384]{1,0:T(8,128)(2,1)}, bf16[512,384]{1,0:T(8,128)(2,1)S(1)}, u32[]{:S(2)}) copy-start(bf16[512,384]{1,0:T(8,128)(2,1)S(1)} %collective-permute-done.2.refs_2_) | copy-start | bytes 1179652
  27.7 10.1 %copy-start.20 = (bf16[384,192]{0,1:T(8,128)(2,1)S(1)}, bf16[384,192]{0,1:T(8,128)(2,1)}, u32[]{:S(2)}) copy-start(bf16[384,192]{0,1:T(8,128)(2,1)} %param.30) | copy-start | bytes 442372
  30.0 30.4 %copy-start.21 = (bf16[128,448]{0,1:T(8,128)(2,1)S(1)}, bf16[128,448]{0,1:T(8,128)(2,1)}, u32[]{:S(2)}) copy-start(bf16[128,448]{0,1:T(8,128)(2,1)} %param.19) | copy-start | bytes 344068
  30.0 26.1 %all-to-all-start = ((bf16[8,128,448]{1,2,0:T(8,128)(2,1)}), bf16[8,128,448]{1,2,0:T(8,128)(2,1)S(1)}, u32[]{:S(2)}, u32[]{:S(2)}) async-start(bf16[8,128,448]{1,2,0:T(8,128)(2,1)} %bitcast.55), calls=%async_computation | async-start | bytes 1835008 | tf_op jit(solution)/shard_map/all_to_all | solution.py:388
  34.5 20.8 %collective-permute-start.3 = (bf16[512,384]{1,0:T(8,128)(2,1)S(1)}, bf16[512,384]{1,0:T(8,128)(2,1)S(1)}, u32[]{:S(2)}, u32[]{:S(2)}) collective-permute-start(bf16[512,384]{1,0:T(8,128)(2,1)S(1)} %collective-permute-done.refs_4_), channel_id=1, source_target_pairs={{0,2},{2,4},{4,6},{6,0},{1,3},{3,5},{5,7},{7,1},{8,10},{10,12},{12... | collective-permute-start | bytes 1179656 | tf_op jit(solution)/shard_map/ppermute | solution.py:22
  36.5 19.5 %collective-permute-start.4 = (bf16[512,384]{1,0:T(8,128)(2,1)S(1)}, bf16[512,384]{1,0:T(8,128)(2,1)}, u32[]{:S(2)}, u32[]{:S(2)}) collective-permute-start(bf16[512,384]{1,0:T(8,128)(2,1)S(1)} %collective-permute-done.refs_4_), channel_id=1, source_target_pairs={{0,6},{2,0},{4,2},{6,4},{1,7},{3,1},{5,3},{7,5},{8,14},{10,8},{12,... | collective-permute-start | bytes 1179656 | tf_op jit(solution)/shard_map/ppermute | solution.py:22
  56.1 30.0 %collective-permute-start.10 = (bf16[6,192,384]{2,1,0:T(8,128)(2,1)}, bf16[6,192,384]{2,1,0:T(8,128)(2,1)}, u32[]{:S(2)}, u32[]{:S(2)}) collective-permute-start(bf16[6,192,384]{2,1,0:T(8,128)(2,1)} %collective-permute-done.7.refs_5_), channel_id=1, source_target_pairs={{0,16},{16,32},{32,48},{48,0},{1,17},{17,33},{33,49},{49,1},{2,18}... | collective-permute-start | bytes 2654216 | tf_op jit(solution)/shard_map/ppermute | solution.py:22
  58.1 28.0 %collective-permute-start.11 = (bf16[6,192,384]{2,1,0:T(8,128)(2,1)}, bf16[6,192,384]{2,1,0:T(8,128)(2,1)}, u32[]{:S(2)}, u32[]{:S(2)}) collective-permute-start(bf16[6,192,384]{2,1,0:T(8,128)(2,1)} %collective-permute-done.7.refs_5_), channel_id=1, source_target_pairs={{0,48},{16,0},{32,16},{48,32},{1,49},{17,1},{33,17},{49,33},{2,50}... | collective-permute-start | bytes 2654216 | tf_op jit(solution)/shard_map/ppermute | solution.py:22
  60.4 8.8 %copy-start.19 = (bf16[2,192,384]{2,1,0:T(8,128)(2,1)S(1)}, bf16[2,192,384]{2,1,0:T(8,128)(2,1)}, u32[]{:S(2)}) copy-start(bf16[2,192,384]{2,1,0:T(8,128)(2,1)} %pad_maximum_fusion.3) | copy-start | bytes 884740
  60.4 53.8 %copy-start.23 = (f32[3584]{0:T(1024)S(1)}, f32[3584]{0:T(1024)}, u32[]{:S(2)}) copy-start(f32[3584]{0:T(1024)} %param.20) | copy-start | bytes 43012
  61.5 24.5 %all-to-all-start.1 = ((bf16[8,128,448]{1,2,0:T(8,128)(2,1)}), bf16[8,128,448]{1,2,0:T(8,128)(2,1)}, u32[]{:S(2)}, u32[]{:S(2)}) async-start(bf16[8,128,448]{1,2,0:T(8,128)(2,1)} %broadcast_in_dim.4), calls=%async_computation.1 | async-start | bytes 1835008 | tf_op jit(solution)/shard_map/all_to_all | solution.py:32
  65.8 171.3 %all-gather.3.cloned.1.call-start = ((), (), s32[]{:S(2)}) async-start(), calls=%async_computation.4 | async-start | bytes 5013504 | tf_op jit(solution)/shard_map/all_gather | solution.py:402
  65.8 19.4 %collective-permute-start.8 = (bf16[512,384]{1,0:T(8,128)(2,1)}, bf16[512,384]{1,0:T(8,128)(2,1)S(1)}, u32[]{:S(2)}, u32[]{:S(2)}) collective-permute-start(bf16[512,384]{1,0:T(8,128)(2,1)} %collective-permute-done.1.refs_1_), channel_id=1, source_target_pairs={{0,2},{2,4},{4,6},{6,0},{1,3},{3,5},{5,7},{7,1},{8,10},{10,12},{12... | collective-permute-start | bytes 1179656 | tf_op jit(solution)/shard_map/ppermute | solution.py:22
  67.7 18.3 %collective-permute-start.9 = (bf16[512,384]{1,0:T(8,128)(2,1)}, bf16[512,384]{1,0:T(8,128)(2,1)}, u32[]{:S(2)}, u32[]{:S(2)}) collective-permute-start(bf16[512,384]{1,0:T(8,128)(2,1)} %collective-permute-done.4.refs_6_), channel_id=1, source_target_pairs={{0,6},{2,0},{4,2},{6,4},{1,7},{3,1},{5,3},{7,5},{8,14},{10,8},{12,... | collective-permute-start | bytes 1179656 | tf_op jit(solution)/shard_map/ppermute | solution.py:22
  69.1 1.4 collective-permute-start.12
  70.5 19.2 %collective-permute-start.15 = (bf16[6,192,384]{2,1,0:T(8,128)(2,1)S(1)}, bf16[6,192,384]{2,1,0:T(8,128)(2,1)S(1)}, u32[]{:S(2)}, u32[]{:S(2)}) collective-permute-start(bf16[6,192,384]{2,1,0:T(8,128)(2,1)S(1)} %maximum_bitcast_fusion.refs_1_), channel_id=1, source_target_pairs={{0,8},{8,0},{1,9},{9,1},{2,10},{10,2},{3,11},{11,3},{4,12},{12,4},... | collective-permute-start | bytes 2654216 | tf_op jit(solution)/shard_map/ppermute | solution.py:22
  86.0 4.6 %collective-permute-start.18 = (bf16[6,192,384]{2,1,0:T(8,128)(2,1)}, bf16[6,192,384]{2,1,0:T(8,128)(2,1)}, u32[]{:S(2)}, u32[]{:S(2)}) collective-permute-start(bf16[6,192,384]{2,1,0:T(8,128)(2,1)} %collective-permute-done.7.refs_5_), channel_id=1, source_target_pairs={{0,8},{8,0},{1,9},{9,1},{2,10},{10,2},{3,11},{11,3},{4,12},{12,4},... | collective-permute-start | bytes 2654216 | tf_op jit(solution)/shard_map/ppermute | solution.py:22
  86.0 28.2 %collective-permute-start.13 = (bf16[6,192,384]{2,1,0:T(8,128)(2,1)S(1)}, bf16[6,192,384]{2,1,0:T(8,128)(2,1)}, u32[]{:S(2)}, u32[]{:S(2)}) collective-permute-start(bf16[6,192,384]{2,1,0:T(8,128)(2,1)S(1)} %collective-permute-done.5.refs_2_), channel_id=1, source_target_pairs={{0,16},{16,32},{32,48},{48,0},{1,17},{17,33},{33,49},{49,1},{2,18}... | collective-permute-start | bytes 2654216 | tf_op jit(solution)/shard_map/ppermute | solution.py:22
  86.2 51.1 %collective-permute-start.16 = (bf16[6,192,384]{2,1,0:T(8,128)(2,1)S(1)}, bf16[6,192,384]{2,1,0:T(8,128)(2,1)}, u32[]{:S(2)}, u32[]{:S(2)}) collective-permute-start(bf16[6,192,384]{2,1,0:T(8,128)(2,1)S(1)} %collective-permute-done.5.refs_2_), channel_id=1, source_target_pairs={{0,8},{8,0},{1,9},{9,1},{2,10},{10,2},{3,11},{11,3},{4,12},{12,4},... | collective-permute-start | bytes 2654216 | tf_op jit(solution)/shard_map/ppermute | solution.py:22
  86.7 50.6 %collective-permute-start.14 = (bf16[6,192,384]{2,1,0:T(8,128)(2,1)}, bf16[6,192,384]{2,1,0:T(8,128)(2,1)}, u32[]{:S(2)}, u32[]{:S(2)}) collective-permute-start(bf16[6,192,384]{2,1,0:T(8,128)(2,1)} %collective-permute-done.11.refs_7_), channel_id=1, source_target_pairs={{0,48},{16,0},{32,16},{48,32},{1,49},{17,1},{33,17},{49,33},{2,50}... | collective-permute-start | bytes 2654216 | tf_op jit(solution)/shard_map/ppermute | solution.py:22
  90.6 46.7 %collective-permute-start.20 = (bf16[6,192,384]{2,1,0:T(8,128)(2,1)}, bf16[6,192,384]{2,1,0:T(8,128)(2,1)}, u32[]{:S(2)}, u32[]{:S(2)}) collective-permute-start(bf16[6,192,384]{2,1,0:T(8,128)(2,1)} %collective-permute-done.11.refs_7_), channel_id=1, source_target_pairs={{0,8},{8,0},{1,9},{9,1},{2,10},{10,2},{3,11},{11,3},{4,12},{12,4},... | collective-permute-start | bytes 2654216 | tf_op jit(solution)/shard_map/ppermute | solution.py:22
  90.6 46.7 %collective-permute-start.17 = (bf16[6,192,384]{2,1,0:T(8,128)(2,1)}, bf16[6,192,384]{2,1,0:T(8,128)(2,1)}, u32[]{:S(2)}, u32[]{:S(2)}) collective-permute-start(bf16[6,192,384]{2,1,0:T(8,128)(2,1)} %collective-permute-done.6.refs_3_), channel_id=1, source_target_pairs={{0,8},{8,0},{1,9},{9,1},{2,10},{10,2},{3,11},{11,3},{4,12},{12,4},... | collective-permute-start | bytes 2654216 | tf_op jit(solution)/shard_map/ppermute | solution.py:22
  114.2 23.1 %collective-permute-start.19 = (bf16[6,192,384]{2,1,0:T(8,128)(2,1)}, bf16[6,192,384]{2,1,0:T(8,128)(2,1)}, u32[]{:S(2)}, u32[]{:S(2)}) collective-permute-start(bf16[6,192,384]{2,1,0:T(8,128)(2,1)} %collective-permute-done.10.refs_6_), channel_id=1, source_target_pairs={{0,8},{8,0},{1,9},{9,1},{2,10},{10,2},{3,11},{11,3},{4,12},{12,4},... | collective-permute-start | bytes 2654216 | tf_op jit(solution)/shard_map/ppermute | solution.py:22
  115.8 1.8 copy-start.4
  118.5 4.7 %copy-start.5 = (bf16[512,384]{1,0:T(8,128)(2,1)S(1)}, bf16[512,384]{1,0:T(8,128)(2,1)}, u32[]{:S(2)}) copy-start(bf16[512,384]{1,0:T(8,128)(2,1)} %refs_0_.1) | copy-start | bytes 1179652
  118.6 4.7 %copy-start.17 = (f32[4,3072]{1,0:T(4,128)S(1)}, f32[4,3072]{1,0:T(4,128)}, u32[]{:S(2)}) copy-start(f32[4,3072]{1,0:T(4,128)} %mod_ref.2) | copy-start | bytes 147460
  119.5 17.7 %all-to-all-start.2 = ((bf16[8,128,384]{2,1,0:T(8,128)(2,1)}), bf16[8,128,384]{2,1,0:T(8,128)(2,1)S(1)}, u32[]{:S(2)}, u32[]{:S(2)}) async-start(bf16[8,128,384]{2,1,0:T(8,128)(2,1)} %broadcast_in_dim.5), calls=%async_computation.2 | async-start | bytes 1572864 | tf_op jit(solution)/shard_map/all_to_all | solution.py:32
  123.2 1.0 copy-start.9
  124.3 1.0 copy-start.11
  126.3 1.0 copy-start.15
  127.3 10.7 %copy-start.26 = (s32[128]{0:T(128)S(1)}, s32[128]{0:T(128)}, u32[]{:S(2)}) copy-start(s32[128]{0:T(128)} %param.31) | copy-start | bytes 1540
  127.3 10.8 %copy-start.24 = (f32[128]{0:T(128)S(1)}, f32[128]{0:T(128)}, u32[]{:S(2)}) copy-start(f32[128]{0:T(128)} %param.26) | copy-start | bytes 1540
  127.3 10.8 %copy-start.25 = (f32[128]{0:T(128)S(1)}, f32[128]{0:T(128)}, u32[]{:S(2)}) copy-start(f32[128]{0:T(128)} %param.25) | copy-start | bytes 1540
  132.7 1.7 copy-start.2
  134.4 7.0 %copy-start.16 = (f32[4,3072]{1,0:T(4,128)S(1)}, f32[4,3072]{1,0:T(4,128)}, u32[]{:S(2)}) copy-start(f32[4,3072]{1,0:T(4,128)} %mod_ref.3) | copy-start | bytes 147460
  137.3 2.8 %collective-permute-start.21 = (bf16[6,192,384]{2,1,0:T(8,128)(2,1)}, bf16[6,192,384]{2,1,0:T(8,128)(2,1)}, u32[]{:S(2)}, u32[]{:S(2)}) collective-permute-start(bf16[6,192,384]{2,1,0:T(8,128)(2,1)} %collective-permute-done.13.refs_4_), channel_id=1, source_target_pairs={{0,8},{8,0},{1,9},{9,1},{2,10},{10,2},{3,11},{11,3},{4,12},{12,4},... | collective-permute-start | bytes 2654216 | tf_op jit(solution)/shard_map/ppermute | solution.py:22
  137.4 4.0 %collective-permute-start.22 = (bf16[6,192,384]{2,1,0:T(8,128)(2,1)}, bf16[6,192,384]{2,1,0:T(8,128)(2,1)}, u32[]{:S(2)}, u32[]{:S(2)}) collective-permute-start(bf16[6,192,384]{2,1,0:T(8,128)(2,1)} %collective-permute-done.14.refs_8_), channel_id=1, source_target_pairs={{0,8},{8,0},{1,9},{9,1},{2,10},{10,2},{3,11},{11,3},{4,12},{12,4},... | collective-permute-start | bytes 2654216 | tf_op jit(solution)/shard_map/ppermute | solution.py:22
  138.0 3.4 %copy-start.7 = (bf16[6,192,384]{2,1,0:T(8,128)(2,1)S(1)}, bf16[6,192,384]{2,1,0:T(8,128)(2,1)}, u32[]{:S(2)}) copy-start(bf16[6,192,384]{2,1,0:T(8,128)(2,1)} %copy-done.6) | copy-start | bytes 2654212
  152.8 5.0 %collective-permute-start.24 = (bf16[640,384]{1,0:T(8,128)(2,1)S(1)}, bf16[640,384]{1,0:T(8,128)(2,1)S(1)}, u32[]{:S(2)}, u32[]{:S(2)}) collective-permute-start(bf16[640,384]{1,0:T(8,128)(2,1)S(1)} %get-tuple-element.111.refs_0_), channel_id=1, source_target_pairs={{0,8},{8,0},{1,9},{9,1},{2,10},{10,2},{3,11},{11,3},{4,12},{12,4},... | collective-permute-start | bytes 1474568 | tf_op jit(solution)/shard_map/ppermute | solution.py:22
  153.1 15.0 %collective-permute-start.23 = (bf16[640,384]{1,0:T(8,128)(2,1)S(1)}, bf16[640,384]{1,0:T(8,128)(2,1)S(1)}, u32[]{:S(2)}, u32[]{:S(2)}) collective-permute-start(bf16[640,384]{1,0:T(8,128)(2,1)S(1)} %get-tuple-element.111.refs_0_), channel_id=1, source_target_pairs={{0,64},{64,0},{1,65},{65,1},{2,66},{66,2},{3,67},{67,3},{4,68},{68... | collective-permute-start | bytes 1474568 | tf_op jit(solution)/shard_map/ppermute | solution.py:22
  154.6 25.0 %collective-permute-start.26 = (bf16[2,640,384]{2,1,0:T(8,128)(2,1)S(1)}, bf16[2,640,384]{2,1,0:T(8,128)(2,1)S(1)}, u32[]{:S(2)}, u32[]{:S(2)}) collective-permute-start(bf16[2,640,384]{2,1,0:T(8,128)(2,1)S(1)} %get-tuple-element.112.refs_2_.refs_3_), channel_id=1, source_target_pairs={{0,16},{16,32},{32,48},{48,0},{1,17},{17,33},{33,49},{49,1},{2,18}... | collective-permute-start | bytes 2949128 | tf_op jit(solution)/shard_map/ppermute | solution.py:22
  154.6 25.0 %collective-permute-start.27 = (bf16[2,640,384]{2,1,0:T(8,128)(2,1)S(1)}, bf16[2,640,384]{2,1,0:T(8,128)(2,1)S(1)}, u32[]{:S(2)}, u32[]{:S(2)}) collective-permute-start(bf16[2,640,384]{2,1,0:T(8,128)(2,1)S(1)} %get-tuple-element.112.refs_2_.refs_3_), channel_id=1, source_target_pairs={{0,48},{16,0},{32,16},{48,32},{1,49},{17,1},{33,17},{49,33},{2,50}... | collective-permute-start | bytes 2949128 | tf_op jit(solution)/shard_map/ppermute | solution.py:22
  168.1 1.9 collective-permute-start.25
  179.7 13.7 %collective-permute-start.28 = (bf16[640,384]{1,0:T(8,128)(2,1)S(1)}, bf16[640,384]{1,0:T(8,128)(2,1)S(1)}, u32[]{:S(2)}, u32[]{:S(2)}) collective-permute-start(bf16[640,384]{1,0:T(8,128)(2,1)S(1)} %slice_bitcast_fusion.1), channel_id=1, source_target_pairs={{0,16},{16,32},{32,48},{48,0},{1,17},{17,33},{33,49},{49,1},{2,18}... | collective-permute-start | bytes 1474568 | tf_op jit(solution)/shard_map/ppermute | solution.py:22
  179.8 13.6 %collective-permute-start.29 = (bf16[640,384]{1,0:T(8,128)(2,1)S(1)}, bf16[640,384]{1,0:T(8,128)(2,1)S(1)}, u32[]{:S(2)}, u32[]{:S(2)}) collective-permute-start(bf16[640,384]{1,0:T(8,128)(2,1)S(1)} %slice_bitcast_fusion), channel_id=1, source_target_pairs={{0,48},{16,0},{32,16},{48,32},{1,49},{17,1},{33,17},{49,33},{2,50}... | collective-permute-start | bytes 1474568 | tf_op jit(solution)/shard_map/ppermute | solution.py:22
  198.4 3.2 %collective-permute-start.30 = (f32[640,384]{1,0:T(8,128)S(1)}, f32[640,384]{1,0:T(8,128)S(1)}, u32[]{:S(2)}, u32[]{:S(2)}) collective-permute-start(f32[640,384]{1,0:T(8,128)S(1)} %get-tuple-element.139), channel_id=1, source_target_pairs={{0,8},{8,0},{1,9},{9,1},{2,10},{10,2},{3,11},{11,3},{4,12},{12,4},... | collective-permute-start | bytes 2949128 | tf_op jit(solution)/shard_map/ppermute | solution.py:22
  198.5 3.0 %collective-permute-start.31 = (f32[640,128]{1,0:T(8,128)S(1)}, f32[640,128]{1,0:T(8,128)S(1)}, u32[]{:S(2)}, u32[]{:S(2)}) collective-permute-start(f32[640,128]{1,0:T(8,128)S(1)} %get-tuple-element.141), channel_id=1, source_target_pairs={{0,8},{8,0},{1,9},{9,1},{2,10},{10,2},{3,11},{11,3},{4,12},{12,4},... | collective-permute-start | bytes 983048 | tf_op jit(solution)/shard_map/ppermute | solution.py:22
  201.8 18.4 %collective-permute-start.32 = (bf16[640,512]{1,0:T(8,128)(2,1)S(1)}, bf16[640,512]{1,0:T(8,128)(2,1)S(1)}, u32[]{:S(2)}, u32[]{:S(2)}) collective-permute-start(bf16[640,512]{1,0:T(8,128)(2,1)S(1)} %pad_maximum_fusion), channel_id=1, source_target_pairs={{0,64},{64,0},{1,65},{65,1},{2,66},{66,2},{3,67},{67,3},{4,68},{68... | collective-permute-start | bytes 1966088 | tf_op jit(solution)/shard_map/ppermute | solution.py:22
  220.2 3.0 %collective-permute-start.33 = (f32[640,384]{1,0:T(8,128)S(1)}, f32[640,384]{1,0:T(8,128)S(1)}, u32[]{:S(2)}, u32[]{:S(2)}) collective-permute-start(f32[640,384]{1,0:T(8,128)S(1)} %get-tuple-element.156), channel_id=1, source_target_pairs={{0,8},{8,0},{1,9},{9,1},{2,10},{10,2},{3,11},{11,3},{4,12},{12,4},... | collective-permute-start | bytes 2949128 | tf_op jit(solution)/shard_map/ppermute | solution.py:22
  220.2 3.0 %collective-permute-start.34 = (f32[640,128]{1,0:T(8,128)S(1)}, f32[640,128]{1,0:T(8,128)S(1)}, u32[]{:S(2)}, u32[]{:S(2)}) collective-permute-start(f32[640,128]{1,0:T(8,128)S(1)} %get-tuple-element.159), channel_id=1, source_target_pairs={{0,8},{8,0},{1,9},{9,1},{2,10},{10,2},{3,11},{11,3},{4,12},{12,4},... | collective-permute-start | bytes 983048 | tf_op jit(solution)/shard_map/ppermute | solution.py:22
  223.8 13.3 %collective-permute-start.35 = (bf16[640,384]{1,0:T(8,128)(2,1)S(1)}, bf16[640,384]{1,0:T(8,128)(2,1)S(1)}, u32[]{:S(2)}, u32[]{:S(2)}) collective-permute-start(bf16[640,384]{1,0:T(8,128)(2,1)S(1)} %combine.1.own_ref), channel_id=1, source_target_pairs={{0,1},{1,0},{2,3},{3,2},{4,5},{5,4},{6,7},{7,6},{8,9},{9,8},{10,11... | collective-permute-start | bytes 1474568 | tf_op jit(solution)/shard_map/ppermute | solution.py:22
  237.1 2.3 copy-start.3
  243.4 29.2 %all-to-all-start.3 = ((bf16[4,640,384]{2,1,0:T(8,128)(2,1)}), bf16[4,640,384]{2,1,0:T(8,128)(2,1)}, u32[]{:S(2)}, u32[]{:S(2)}) async-start(bf16[4,640,384]{2,1,0:T(8,128)(2,1)} %out_projection.1), calls=%async_computation.3 | async-start | bytes 3932160 | tf_op jit(solution)/shard_map/all_to_all | solution.py:463
  247.8 26.7 %copy-start.22 = (bf16[128,384]{1,0:T(8,128)(2,1)S(1)}, bf16[128,384]{1,0:T(8,128)(2,1)}, u32[]{:S(2)}) copy-start(bf16[128,384]{1,0:T(8,128)(2,1)} %param.33) | copy-start | bytes 294916
  247.8 27.4 %copy-start.18 = (bf16[512,384]{1,0:T(8,128)(2,1)S(1)}, bf16[512,384]{1,0:T(8,128)(2,1)}, u32[]{:S(2)}) copy-start(bf16[512,384]{1,0:T(8,128)(2,1)} %param.32) | copy-start | bytes 1179652
  272.5 3.6 %copy-start.1 = (bf16[128,1280]{1,0:T(8,128)(2,1)S(1)}, bf16[128,1280]{1,0:T(8,128)(2,1)}, u32[]{:S(2)}) copy-start(bf16[128,1280]{1,0:T(8,128)(2,1)} %param.17) | copy-start | bytes 983044
  (4 other events, 3.4 us)
Sparse Core Ops, SparseCore 0:
  86.3 65.7 all-gather.2

commit v6 on v5

--- a/solution.py
+++ b/solution.py
@@ -413,6 +413,7 @@
     a_places = [(x + d) % 4 * 2 + (yl + p) % 2 for p, d in blocks]
     image_modded = modulate(a_arrays, a_places, image_mod)
     w_early = [weight, *w_near, w_pair, *w_next]
+    w_early, text_states = together((w_early, text_states))
     w_swapped = [shift(w, "c", 1) for w in w_early]
     text_a, w_far, image_modded, w_swapped = together((text_a, w_far, image_modded, w_swapped))
 

time: 284 us -> 276 us (0.972)
  waiting for transfers between devices: 122 us -> 114 us
    ppermute x35, waiting for transfers between devices: 95.1 us -> 89.4 us  [shift(): lax.ppermute(value, axis, [(k, (k + step) % size) for k in range(size)])]
    unnamed x54 -> x64, local copies, waits for them, and re-layouts: 12.3 us -> 13.2 us
  transfers between devices with their start and end apart: 41 -> 41, of which waited for: 16 -> 20; matrix products, arithmetic and copies ran while one was open for 6% -> 6% of each run, Pallas kernels for 18% -> 18%
where the time goes in v6:
time: 276 us; the launch traced here: 275 us
  waiting for transfers between devices  114 us (41%)
  starting transfers between devices  57 us (21%)
  Pallas kernels  55.3 us (20%)
  local copies, waits for them, and re-layouts  19.5 us (7%)
  between operations  14.5 us (5%)
  other arithmetic  8.79 us (3%)
  matrix products  5.96 us (2%)
    ppermute x35, waiting for transfers between devices, shift(): lax.ppermute(value, axis, [(k, (k + step) % size) for k in range(size)])  89.4 us
    ppermute x35, starting transfers between devices, shift(): lax.ppermute(value, axis, [(k, (k + step) % size) for k in range(size)])  39.1 us
    pallas_call x5, Pallas kernels, attention(): pl.pallas_call(functools.partial(attention_kernel, nq, k_sizes, not befor...  32.6 us
    all_to_all x1, waiting for transfers between devices, shards(): got = lax.all_to_all(parts, 'x', split_axis=0, concat_axis=0, tiled=True)  24.5 us
    unnamed x64, local copies, waits for them, and re-layouts  13.2 us
    pallas_call x1, Pallas kernels, qkv(): pl.pallas_call(functools.partial(qkv_kernel, count), out_shape=(jax.Shape...  11.8 us
    all_to_all x2, starting transfers between devices, spread(): return lax.all_to_all(copies, axes, split_axis=0, concat_axis=0, tiled=True)  8.18 us
    dot_general x1, matrix products, shards(): jnp.dot(cond_hidden, cond_down, preferred_element_type=F32).astype(BF)  5.96 us
  transfers between devices with their start and end apart: 41, of which 20 were waited for; matrix products, arithmetic and copies ran while one was open for 6% of the time, Pallas kernels for 18%

profile of v6, /device:TPU:0, one launch (start us, length us, event | category | flops | bytes accessed | tf_op | source)
XLA Modules:
  0.0 275.0 jit_solution(12129381612490409434)
XLA Ops:
  7.2 1.7 collective-permute-start
  8.9 1.5 collective-permute-start.1
  10.4 1.7 collective-permute-start.2
  12.2 1.2 maximum_bitcast_fusion.refs_1_
  13.4 2.0 collective-permute-start.5
  15.4 2.2 collective-permute-start.6
  18.2 3.4 %collective-permute-start.7 = (bf16[6,192,384]{2,1,0:T(8,128)(2,1)S(1)}, bf16[6,192,384]{2,1,0:T(8,128)(2,1)}, u32[]{:S(2)}, u32[]{:S(2)}) collective-permute-start(bf16[6,192,384]{2,1,0:T(8,128)(2,1)S(1)} %maximum_bitcast_fusion.refs_1_), channel_id=1, source_target_pairs={{0,64},{64,0},{1,65},{65,1},{2,66},{66,2},{3,67},{67,3},{4,68},{68... | collective-permute-start | bytes 2654216 | tf_op jit(solution)/shard_map/ppermute | solution.py:22
  22.4 6.0 %convolution_convert_fusion = bf16[128,3584]{1,0:T(8,128)(2,1)} fusion(bf16[128,1280]{1,0:T(8,128)(2,1)S(1)} %copy-done, bf16[1280,3584]{1,0:T(8,128)(2,1)} %param.18), kind=kOutput, calls=%fused_computation | convolution fusion | flops 1174863872 | bytes 10420224 | tf_op jit(solution)/shard_map/dot_general | solution.py:385
  28.4 2.3 copy.34
  30.6 4.5 %all-to-all-start = ((bf16[8,128,448]{1,2,0:T(8,128)(2,1)}), bf16[8,128,448]{1,2,0:T(8,128)(2,1)}, u32[]{:S(2)}, u32[]{:S(2)}) async-start(bf16[8,128,448]{1,2,0:T(8,128)(2,1)} %bitcast.55), calls=%async_computation | async-start | bytes 1835008 | tf_op jit(solution)/shard_map/all_to_all | solution.py:388
  35.2 2.0 collective-permute-start.3
  37.2 1.3 collective-permute-start.4
  39.3 16.6 %collective-permute-done.3.refs_5_ = bf16[512,384]{1,0:T(8,128)(2,1)S(1)} collective-permute-done((bf16[512,384]{1,0:T(8,128)(2,1)S(1)}, bf16[512,384]{1,0:T(8,128)(2,1)S(1)}, u32[]{:S(2)}, u32[]{:S(2)}) %collective-permute-start.3) | collective-permute-done | bytes 393248 | tf_op jit(solution)/shard_map/ppermute | solution.py:22
  57.5 2.0 collective-permute-start.10
  59.5 2.2 collective-permute-start.11
  61.7 1.3 convert_reduce_fusion.1
  63.1 1.1 broadcast_in_dim.4
  64.1 4.2 %all-to-all-start.1 = ((bf16[8,128,448]{1,2,0:T(8,128)(2,1)}), bf16[8,128,448]{1,2,0:T(8,128)(2,1)}, u32[]{:S(2)}, u32[]{:S(2)}) async-start(bf16[8,128,448]{1,2,0:T(8,128)(2,1)} %broadcast_in_dim.4), calls=%async_computation.1 | async-start | bytes 1835008 | tf_op jit(solution)/shard_map/all_to_all | solution.py:32
  68.4 1.9 collective-permute-start.8
  70.4 1.4 collective-permute-start.9
  72.5 15.4 %collective-permute-done.8.refs_3_ = bf16[512,384]{1,0:T(8,128)(2,1)} collective-permute-done((bf16[512,384]{1,0:T(8,128)(2,1)S(1)}, bf16[512,384]{1,0:T(8,128)(2,1)}, u32[]{:S(2)}, u32[]{:S(2)}) %collective-permute-start.8) | collective-permute-done | bytes 393248 | tf_op jit(solution)/shard_map/ppermute | solution.py:22
  88.0 1.5 copy.35.state_ref
  89.5 1.8 copy-done.4
  91.3 1.0 text_projection.1
  93.5 1.5 collective-permute-done.15.refs_9_
  95.2 1.9 collective-permute-done.16.refs_10_
  97.6 1.7 collective-permute-start.14
  99.3 1.0 broadcast_in_dim.5
  100.3 4.0 %all-to-all-start.2 = ((bf16[8,128,384]{2,1,0:T(8,128)(2,1)}), bf16[8,128,384]{2,1,0:T(8,128)(2,1)S(1)}, u32[]{:S(2)}, u32[]{:S(2)}) async-start(bf16[8,128,384]{2,1,0:T(8,128)(2,1)} %broadcast_in_dim.5), calls=%async_computation.2 | async-start | bytes 1572864 | tf_op jit(solution)/shard_map/all_to_all | solution.py:32
  104.3 1.0 copy-done.9
  105.3 1.0 copy-done.11
  106.3 1.0 copy-done.13
  107.3 1.0 copy-done.15
  108.3 1.0 copy-done.18
  109.3 5.5 %modulate.1.image_ref = bf16[512,3072]{1,0:T(8,128)(2,1)S(1)} custom-call(s32[8]{0:T(128)S(1)} %stack.131.place_ref, f32[4,3072]{1,0:T(4,128)S(1)} %copy-done.20, bf16[512,384]{1,0:T(8,128)(2,1)S(1)} %copy-done.5, bf16[512,384]{1,0:T(8,128)(2,1)S(1)} %copy-done.11, bf16[512,384]{1,0:T(8,128)(2,1)S(1)} %copy-done.13, ...), custom_call_target="tpu_custom_call" | custom-call | tf_op jit(solution)/shard_map/modulate/pallas_call | solution.py:115
  114.8 1.7 copy-done.2
  116.7 2.0 collective-permute-done.13.refs_4_
  118.6 5.8 %collective-permute-done.14.refs_8_ = bf16[6,192,384]{2,1,0:T(8,128)(2,1)} collective-permute-done((bf16[6,192,384]{2,1,0:T(8,128)(2,1)}, bf16[6,192,384]{2,1,0:T(8,128)(2,1)}, u32[]{:S(2)}, u32[]{:S(2)}) %collective-permute-start.14) | collective-permute-done | bytes 884768 | tf_op jit(solution)/shard_map/ppermute | solution.py:22
  125.1 1.2 fusion.7
  127.1 1.3 collective-permute-done.22.refs_16_
  128.4 11.8 %qkv.1 = (bf16[640,384]{1,0:T(8,128)(2,1)S(1)}, bf16[2,640,384]{2,1,0:T(8,128)(2,1)S(1)}) custom-call(s32[16]{0:T(128)S(1)} %stack.116.place_ref, f32[4,3072]{1,0:T(4,128)S(1)} %copy-done.19, f32[640,128]{1,0:T(8,128)S(1)} %get-tuple-element.183.cos_ref, f32[640,128]{1,0:T(8,128)S(1)} %get-tuple-element.184.sin_ref, ...), custom_call_target="tpu_custom_call" | custom-call | tf_op jit(solution)/shard_map/qkv/pallas_call | solution.py:191
  140.5 1.6 collective-permute-start.23
  142.1 3.2 %collective-permute-start.27 = (bf16[2,640,384]{2,1,0:T(8,128)(2,1)S(1)}, bf16[2,640,384]{2,1,0:T(8,128)(2,1)S(1)}, u32[]{:S(2)}, u32[]{:S(2)}) collective-permute-start(bf16[2,640,384]{2,1,0:T(8,128)(2,1)S(1)} %get-tuple-element.125.refs_2_.refs_3_), channel_id=1, source_target_pairs={{0,48},{16,0},{32,16},{48,32},{1,49},{17,1},{33,17},{49,33},{2,50}... | collective-permute-start | bytes 2949128 | tf_op jit(solution)/shard_map/ppermute | solution.py:22
  145.3 4.7 %attention.5 = (f32[640,384]{1,0:T(8,128)S(1)}, f32[640,384]{1,0:T(8,128)S(1)}, f32[640,128]{1,0:T(8,128)S(1)}, f32[640,128]{1,0:T(8,128)S(1)}) custom-call(bf16[640,384]{1,0:T(8,128)(2,1)S(1)} %get-tuple-element.124.refs_0_, bf16[640,384]{1,0:T(8,128)(2,1)S(1)} %collective-permute-done.24.refs_1_, ...), custom_call_target="tpu_custom_call" | custom-call | flops 2516582400 | bytes 3932160 | tf_op jit(solution)/shard_map/attention/pallas_call | solution.py:259
  150.0 8.4 %collective-permute-done.23.refs_0_ = bf16[640,384]{1,0:T(8,128)(2,1)S(1)} collective-permute-done((bf16[640,384]{1,0:T(8,128)(2,1)S(1)}, bf16[640,384]{1,0:T(8,128)(2,1)S(1)}, u32[]{:S(2)}, u32[]{:S(2)}) %collective-permute-start.23) | collective-permute-done | bytes 491552 | tf_op jit(solution)/shard_map/ppermute | solution.py:22
  158.4 1.9 collective-permute-done.25.refs_1_
  160.3 4.7 %attention.6 = (f32[640,384]{1,0:T(8,128)S(1)}, f32[640,384]{1,0:T(8,128)S(1)}, f32[640,128]{1,0:T(8,128)S(1)}, f32[640,128]{1,0:T(8,128)S(1)}) custom-call(bf16[640,384]{1,0:T(8,128)(2,1)S(1)} %collective-permute-done.23.refs_0_, bf16[640,384]{1,0:T(8,128)(2,1)S(1)} %collective-permute-done.25.refs_1_, ...), custom_call_target="tpu_custom_call" | custom-call | flops 2516582400 | bytes 3932160 | tf_op jit(solution)/shard_map/attention/pallas_call | solution.py:259
  165.0 6.5 %collective-permute-done.26.refs_2_.refs_4_.refs_5_ = bf16[2,640,384]{2,1,0:T(8,128)(2,1)S(1)} collective-permute-done((bf16[2,640,384]{2,1,0:T(8,128)(2,1)S(1)}, bf16[2,640,384]{2,1,0:T(8,128)(2,1)S(1)}, u32[]{:S(2)}, u32[]{:S(2)}) %collective-permute-start.26) | collective-permute-done | bytes 983072 | tf_op jit(solution)/shard_map/ppermute | solution.py:22
  172.4 2.8 %collective-permute-start.29 = (bf16[640,384]{1,0:T(8,128)(2,1)S(1)}, bf16[640,384]{1,0:T(8,128)(2,1)S(1)}, u32[]{:S(2)}, u32[]{:S(2)}) collective-permute-start(bf16[640,384]{1,0:T(8,128)(2,1)S(1)} %slice_bitcast_fusion), channel_id=1, source_target_pairs={{0,48},{16,0},{32,16},{48,32},{1,49},{17,1},{33,17},{49,33},{2,50}... | collective-permute-start | bytes 1474568 | tf_op jit(solution)/shard_map/ppermute | solution.py:22
  175.2 7.7 %attention.7 = (f32[640,384]{1,0:T(8,128)S(1)}, f32[640,384]{1,0:T(8,128)S(1)}, f32[640,128]{1,0:T(8,128)S(1)}, f32[640,128]{1,0:T(8,128)S(1)}) custom-call(bf16[640,384]{1,0:T(8,128)(2,1)S(1)} %collective-permute-done.23.refs_0_, ...), custom_call_target="tpu_custom_call", output_to_operand_aliasing={{0}: (6, {}), {1}: (7, {}), {2}: (8, {}), {3}: (9, {})} | custom-call | flops 5033164800 | bytes 3932160 | tf_op jit(solution)/shard_map/attention/pallas_call | solution.py:259
  182.8 2.6 collective-permute-done.28
  185.5 4.9 %attention.8 = (f32[640,384]{1,0:T(8,128)S(1)}, f32[640,384]{1,0:T(8,128)S(1)}, f32[640,128]{1,0:T(8,128)S(1)}, f32[640,128]{1,0:T(8,128)S(1)}) custom-call(bf16[640,384]{1,0:T(8,128)(2,1)S(1)} %collective-permute-done.23.refs_0_, ...), custom_call_target="tpu_custom_call", output_to_operand_aliasing={{0}: (4, {}), {1}: (5, {}), {2}: (6, {}), {3}: (7, {})} | custom-call | flops 2516582400 | bytes 3932160 | tf_op jit(solution)/shard_map/attention/pallas_call | solution.py:259
  191.0 2.5 collective-permute-done.31
  193.9 1.2 collective-permute-start.32
  195.1 10.6 %attention.9 = (f32[640,384]{1,0:T(8,128)S(1)}, f32[640,384]{1,0:T(8,128)S(1)}, f32[640,128]{1,0:T(8,128)S(1)}, f32[640,128]{1,0:T(8,128)S(1)}) custom-call(bf16[640,384]{1,0:T(8,128)(2,1)S(1)} %get-tuple-element.124.refs_0_, ...), custom_call_target="tpu_custom_call", output_to_operand_aliasing={{0}: (8, {}), {1}: (9, {}), {2}: (10, {}), {3}: (11, {})} | custom-call | flops 7549747200 | bytes 3932160 | tf_op jit(solution)/shard_map/attention/pallas_call | solution.py:259
  205.7 6.6 %collective-permute-done.32.back_ref = bf16[640,512]{1,0:T(8,128)(2,1)S(1)} collective-permute-done((bf16[640,512]{1,0:T(8,128)(2,1)S(1)}, bf16[640,512]{1,0:T(8,128)(2,1)S(1)}, u32[]{:S(2)}, u32[]{:S(2)}) %collective-permute-start.32) | collective-permute-done | bytes 655392 | tf_op jit(solution)/shard_map/ppermute | solution.py:22
  212.7 2.5 collective-permute-done.34.other_tot_ref
  215.8 1.0 collective-permute-start.35
  216.8 12.4 %collective-permute-done.35.other_ref = bf16[640,384]{1,0:T(8,128)(2,1)S(1)} collective-permute-done((bf16[640,384]{1,0:T(8,128)(2,1)S(1)}, bf16[640,384]{1,0:T(8,128)(2,1)S(1)}, u32[]{:S(2)}, u32[]{:S(2)}) %collective-permute-start.35) | collective-permute-done | bytes 491552 | tf_op jit(solution)/shard_map/ppermute | solution.py:22
  229.2 2.3 copy-done.3
  231.5 3.9 %out_projection.1 = bf16[4,640,384]{2,1,0:T(8,128)(2,1)} custom-call(s32[1]{0:T(128)} %bitcast.place_ref, bf16[640,384]{1,0:T(8,128)(2,1)S(1)} %combine.1.own_ref, bf16[640,384]{1,0:T(8,128)(2,1)S(1)} %collective-permute-done.35.other_ref, bf16[16,2,192,384]{3,2,1,0:T(8,128)(2,1)S(1)} %bitcast.49), custom_call_target="tpu_custom_call" | custom-call | tf_op jit(solution)/shard_map/out_projection/pallas_call | solution.py:329
  235.4 4.4 %all-to-all-start.3 = ((bf16[4,640,384]{2,1,0:T(8,128)(2,1)}), bf16[4,640,384]{2,1,0:T(8,128)(2,1)}, u32[]{:S(2)}, u32[]{:S(2)}) async-start(bf16[4,640,384]{2,1,0:T(8,128)(2,1)} %out_projection.1), calls=%async_computation.3 | async-start | bytes 3932160 | tf_op jit(solution)/shard_map/all_to_all | solution.py:464
  240.1 24.5 %all-to-all-done.3 = bf16[4,640,384]{2,1,0:T(8,128)(2,1)} async-done(((bf16[4,640,384]{2,1,0:T(8,128)(2,1)}), bf16[4,640,384]{2,1,0:T(8,128)(2,1)}, u32[]{:S(2)}, u32[]{:S(2)}) %all-to-all-start.3) | async-done | bytes 1966112 | tf_op jit(solution)/shard_map/all_to_all | solution.py:464
  264.6 2.0 convert_reduce_fusion
  (123 shorter events, 13.3 us)
Async XLA Ops:
  7.2 15.2 %copy-start = (bf16[128,1280]{1,0:T(8,128)(2,1)S(1)}, bf16[128,1280]{1,0:T(8,128)(2,1)}, u32[]{:S(2)}) copy-start(bf16[128,1280]{1,0:T(8,128)(2,1)} %param.17) | copy-start | bytes 983044
  7.2 11.1 %collective-permute-start = (bf16[512,384]{1,0:T(8,128)(2,1)}, bf16[512,384]{1,0:T(8,128)(2,1)S(1)}, u32[]{:S(2)}, u32[]{:S(2)}) collective-permute-start(bf16[512,384]{1,0:T(8,128)(2,1)} %refs_0_.1), channel_id=1, source_target_pairs={{0,1},{1,0},{2,3},{3,2},{4,5},{5,4},{6,7},{7,6},{8,9},{9,8},{10,11... | collective-permute-start | bytes 1179656 | tf_op jit(solution)/shard_map/ppermute | solution.py:22
  8.9 12.7 %collective-permute-start.1 = (bf16[512,384]{1,0:T(8,128)(2,1)}, bf16[512,384]{1,0:T(8,128)(2,1)S(1)}, u32[]{:S(2)}, u32[]{:S(2)}) collective-permute-start(bf16[512,384]{1,0:T(8,128)(2,1)} %refs_0_.1), channel_id=1, source_target_pairs={{0,2},{2,4},{4,6},{6,0},{1,3},{3,5},{5,7},{7,1},{8,10},{10,12},{12... | collective-permute-start | bytes 1179656 | tf_op jit(solution)/shard_map/ppermute | solution.py:22
  10.4 11.2 %collective-permute-start.2 = (bf16[512,384]{1,0:T(8,128)(2,1)}, bf16[512,384]{1,0:T(8,128)(2,1)S(1)}, u32[]{:S(2)}, u32[]{:S(2)}) collective-permute-start(bf16[512,384]{1,0:T(8,128)(2,1)} %refs_0_.1), channel_id=1, source_target_pairs={{0,6},{2,0},{4,2},{6,4},{1,7},{3,1},{5,3},{7,5},{8,14},{10,8},{12,... | collective-permute-start | bytes 1179656 | tf_op jit(solution)/shard_map/ppermute | solution.py:22
  13.4 43.3 %collective-permute-start.5 = (bf16[6,192,384]{2,1,0:T(8,128)(2,1)S(1)}, bf16[6,192,384]{2,1,0:T(8,128)(2,1)S(1)}, u32[]{:S(2)}, u32[]{:S(2)}) collective-permute-start(bf16[6,192,384]{2,1,0:T(8,128)(2,1)S(1)} %maximum_bitcast_fusion.refs_1_), channel_id=1, source_target_pairs={{0,16},{16,32},{32,48},{48,0},{1,17},{17,33},{33,49},{49,1},{2,18}... | collective-permute-start | bytes 2654216 | tf_op jit(solution)/shard_map/ppermute | solution.py:22
  15.4 41.3 %collective-permute-start.6 = (bf16[6,192,384]{2,1,0:T(8,128)(2,1)S(1)}, bf16[6,192,384]{2,1,0:T(8,128)(2,1)}, u32[]{:S(2)}, u32[]{:S(2)}) collective-permute-start(bf16[6,192,384]{2,1,0:T(8,128)(2,1)S(1)} %maximum_bitcast_fusion.refs_1_), channel_id=1, source_target_pairs={{0,48},{16,0},{32,16},{48,32},{1,49},{17,1},{33,17},{49,33},{2,50}... | collective-permute-start | bytes 2654216 | tf_op jit(solution)/shard_map/ppermute | solution.py:22
  18.2 19.0 %copy-start.8 = (bf16[512,384]{1,0:T(8,128)(2,1)}, bf16[512,384]{1,0:T(8,128)(2,1)S(1)}, u32[]{:S(2)}) copy-start(bf16[512,384]{1,0:T(8,128)(2,1)S(1)} %collective-permute-done.refs_4_) | copy-start | bytes 1179652
  18.2 39.3 %collective-permute-start.7 = (bf16[6,192,384]{2,1,0:T(8,128)(2,1)S(1)}, bf16[6,192,384]{2,1,0:T(8,128)(2,1)}, u32[]{:S(2)}, u32[]{:S(2)}) collective-permute-start(bf16[6,192,384]{2,1,0:T(8,128)(2,1)S(1)} %maximum_bitcast_fusion.refs_1_), channel_id=1, source_target_pairs={{0,64},{64,0},{1,65},{65,1},{2,66},{66,2},{3,67},{67,3},{4,68},{68... | collective-permute-start | bytes 2654216 | tf_op jit(solution)/shard_map/ppermute | solution.py:22
  21.6 46.8 %copy-start.10 = (bf16[512,384]{1,0:T(8,128)(2,1)}, bf16[512,384]{1,0:T(8,128)(2,1)S(1)}, u32[]{:S(2)}) copy-start(bf16[512,384]{1,0:T(8,128)(2,1)S(1)} %collective-permute-done.1.refs_1_) | copy-start | bytes 1179652
  28.4 10.1 %copy-start.24 = (bf16[384,192]{0,1:T(8,128)(2,1)S(1)}, bf16[384,192]{0,1:T(8,128)(2,1)}, u32[]{:S(2)}) copy-start(bf16[384,192]{0,1:T(8,128)(2,1)} %param.30) | copy-start | bytes 442372
  28.4 10.1 %copy-start.25 = (bf16[384,192]{0,1:T(8,128)(2,1)S(1)}, bf16[384,192]{0,1:T(8,128)(2,1)}, u32[]{:S(2)}) copy-start(bf16[384,192]{0,1:T(8,128)(2,1)} %param.29) | copy-start | bytes 442372
  30.6 32.4 %copy-start.26 = (bf16[128,448]{0,1:T(8,128)(2,1)S(1)}, bf16[128,448]{0,1:T(8,128)(2,1)}, u32[]{:S(2)}) copy-start(bf16[128,448]{0,1:T(8,128)(2,1)} %param.19) | copy-start | bytes 344068
  30.6 26.9 %all-to-all-start = ((bf16[8,128,448]{1,2,0:T(8,128)(2,1)}), bf16[8,128,448]{1,2,0:T(8,128)(2,1)}, u32[]{:S(2)}, u32[]{:S(2)}) async-start(bf16[8,128,448]{1,2,0:T(8,128)(2,1)} %bitcast.55), calls=%async_computation | async-start | bytes 1835008 | tf_op jit(solution)/shard_map/all_to_all | solution.py:388
  35.2 20.8 %collective-permute-start.3 = (bf16[512,384]{1,0:T(8,128)(2,1)S(1)}, bf16[512,384]{1,0:T(8,128)(2,1)S(1)}, u32[]{:S(2)}, u32[]{:S(2)}) collective-permute-start(bf16[512,384]{1,0:T(8,128)(2,1)S(1)} %collective-permute-done.refs_4_), channel_id=1, source_target_pairs={{0,2},{2,4},{4,6},{6,0},{1,3},{3,5},{5,7},{7,1},{8,10},{10,12},{12... | collective-permute-start | bytes 1179656 | tf_op jit(solution)/shard_map/ppermute | solution.py:22
  37.2 19.5 %collective-permute-start.4 = (bf16[512,384]{1,0:T(8,128)(2,1)S(1)}, bf16[512,384]{1,0:T(8,128)(2,1)S(1)}, u32[]{:S(2)}, u32[]{:S(2)}) collective-permute-start(bf16[512,384]{1,0:T(8,128)(2,1)S(1)} %collective-permute-done.refs_4_), channel_id=1, source_target_pairs={{0,6},{2,0},{4,2},{6,4},{1,7},{3,1},{5,3},{7,5},{8,14},{10,8},{12,... | collective-permute-start | bytes 1179656 | tf_op jit(solution)/shard_map/ppermute | solution.py:22
  39.3 33.1 %copy-start.28 = (f32[3584]{0:T(1024)S(1)}, f32[3584]{0:T(1024)}, u32[]{:S(2)}) copy-start(f32[3584]{0:T(1024)} %param.20) | copy-start | bytes 43012
  57.5 12.9 %copy-start.17 = (bf16[512,384]{1,0:T(8,128)(2,1)S(1)}, bf16[512,384]{1,0:T(8,128)(2,1)}, u32[]{:S(2)}) copy-start(bf16[512,384]{1,0:T(8,128)(2,1)} %copy-done.16) | copy-start | bytes 1179652
  57.5 30.5 %collective-permute-start.10 = (bf16[6,192,384]{2,1,0:T(8,128)(2,1)}, bf16[6,192,384]{2,1,0:T(8,128)(2,1)}, u32[]{:S(2)}, u32[]{:S(2)}) collective-permute-start(bf16[6,192,384]{2,1,0:T(8,128)(2,1)} %collective-permute-done.7.refs_5_), channel_id=1, source_target_pairs={{0,16},{16,32},{32,48},{48,0},{1,17},{17,33},{33,49},{49,1},{2,18}... | collective-permute-start | bytes 2654216 | tf_op jit(solution)/shard_map/ppermute | solution.py:22
  59.5 28.5 %collective-permute-start.11 = (bf16[6,192,384]{2,1,0:T(8,128)(2,1)}, bf16[6,192,384]{2,1,0:T(8,128)(2,1)}, u32[]{:S(2)}, u32[]{:S(2)}) collective-permute-start(bf16[6,192,384]{2,1,0:T(8,128)(2,1)} %collective-permute-done.7.refs_5_), channel_id=1, source_target_pairs={{0,48},{16,0},{32,16},{48,32},{1,49},{17,1},{33,17},{49,33},{2,50}... | collective-permute-start | bytes 2654216 | tf_op jit(solution)/shard_map/ppermute | solution.py:22
  63.1 8.7 %copy-start.23 = (bf16[2,192,384]{2,1,0:T(8,128)(2,1)S(1)}, bf16[2,192,384]{2,1,0:T(8,128)(2,1)}, u32[]{:S(2)}) copy-start(bf16[2,192,384]{2,1,0:T(8,128)(2,1)} %pad_maximum_fusion.3) | copy-start | bytes 884740
  64.1 23.8 %all-to-all-start.1 = ((bf16[8,128,448]{1,2,0:T(8,128)(2,1)}), bf16[8,128,448]{1,2,0:T(8,128)(2,1)}, u32[]{:S(2)}, u32[]{:S(2)}) async-start(bf16[8,128,448]{1,2,0:T(8,128)(2,1)} %broadcast_in_dim.4), calls=%async_computation.1 | async-start | bytes 1835008 | tf_op jit(solution)/shard_map/all_to_all | solution.py:32
  68.4 160.8 %all-gather.3.cloned.1.call-start = ((), (), s32[]{:S(2)}) async-start(), calls=%async_computation.4 | async-start | bytes 5013504 | tf_op jit(solution)/shard_map/all_gather | solution.py:402
  68.4 19.5 %collective-permute-start.8 = (bf16[512,384]{1,0:T(8,128)(2,1)S(1)}, bf16[512,384]{1,0:T(8,128)(2,1)}, u32[]{:S(2)}, u32[]{:S(2)}) collective-permute-start(bf16[512,384]{1,0:T(8,128)(2,1)S(1)} %collective-permute-done.1.refs_1_), channel_id=1, source_target_pairs={{0,2},{2,4},{4,6},{6,0},{1,3},{3,5},{5,7},{7,1},{8,10},{10,12},{12... | collective-permute-start | bytes 1179656 | tf_op jit(solution)/shard_map/ppermute | solution.py:22
  70.4 17.6 %collective-permute-start.9 = (bf16[512,384]{1,0:T(8,128)(2,1)S(1)}, bf16[512,384]{1,0:T(8,128)(2,1)}, u32[]{:S(2)}, u32[]{:S(2)}) collective-permute-start(bf16[512,384]{1,0:T(8,128)(2,1)S(1)} %copy-done.17), channel_id=1, source_target_pairs={{0,6},{2,0},{4,2},{6,4},{1,7},{3,1},{5,3},{7,5},{8,14},{10,8},{12,... | collective-permute-start | bytes 1179656 | tf_op jit(solution)/shard_map/ppermute | solution.py:22
  71.8 0.8 collective-permute-start.12
  72.5 15.5 %copy-start.22 = (bf16[2,192,384]{2,1,0:T(8,128)(2,1)}, bf16[2,192,384]{2,1,0:T(8,128)(2,1)S(1)}, u32[]{:S(2)}) copy-start(bf16[2,192,384]{2,1,0:T(8,128)(2,1)S(1)} %collective-permute-done.12) | copy-start | bytes 884740
  89.5 1.8 copy-start.4
  92.2 12.1 %copy-start.5 = (bf16[512,384]{1,0:T(8,128)(2,1)S(1)}, bf16[512,384]{1,0:T(8,128)(2,1)}, u32[]{:S(2)}) copy-start(bf16[512,384]{1,0:T(8,128)(2,1)} %refs_0_.1) | copy-start | bytes 1179652
  92.2 12.1 %copy-start.20 = (f32[4,3072]{1,0:T(4,128)S(1)}, f32[4,3072]{1,0:T(4,128)}, u32[]{:S(2)}) copy-start(f32[4,3072]{1,0:T(4,128)} %mod_ref.2) | copy-start | bytes 147460
  92.3 2.8 %collective-permute-start.15 = (bf16[6,192,384]{2,1,0:T(8,128)(2,1)S(1)}, bf16[6,192,384]{2,1,0:T(8,128)(2,1)S(1)}, u32[]{:S(2)}, u32[]{:S(2)}) collective-permute-start(bf16[6,192,384]{2,1,0:T(8,128)(2,1)S(1)} %maximum_bitcast_fusion.refs_1_), channel_id=1, source_target_pairs={{0,8},{8,0},{1,9},{9,1},{2,10},{10,2},{3,11},{11,3},{4,12},{12,4},... | collective-permute-start | bytes 2654216 | tf_op jit(solution)/shard_map/ppermute | solution.py:22
  92.3 4.7 %collective-permute-start.16 = (bf16[6,192,384]{2,1,0:T(8,128)(2,1)S(1)}, bf16[6,192,384]{2,1,0:T(8,128)(2,1)}, u32[]{:S(2)}, u32[]{:S(2)}) collective-permute-start(bf16[6,192,384]{2,1,0:T(8,128)(2,1)S(1)} %collective-permute-done.5.refs_2_), channel_id=1, source_target_pairs={{0,8},{8,0},{1,9},{9,1},{2,10},{10,2},{3,11},{11,3},{4,12},{12,4},... | collective-permute-start | bytes 2654216 | tf_op jit(solution)/shard_map/ppermute | solution.py:22
  92.8 4.8 %collective-permute-start.17 = (bf16[6,192,384]{2,1,0:T(8,128)(2,1)}, bf16[6,192,384]{2,1,0:T(8,128)(2,1)}, u32[]{:S(2)}, u32[]{:S(2)}) collective-permute-start(bf16[6,192,384]{2,1,0:T(8,128)(2,1)} %collective-permute-done.6.refs_3_), channel_id=1, source_target_pairs={{0,8},{8,0},{1,9},{9,1},{2,10},{10,2},{3,11},{11,3},{4,12},{12,4},... | collective-permute-start | bytes 2654216 | tf_op jit(solution)/shard_map/ppermute | solution.py:22
  93.0 25.7 %collective-permute-start.13 = (bf16[6,192,384]{2,1,0:T(8,128)(2,1)S(1)}, bf16[6,192,384]{2,1,0:T(8,128)(2,1)}, u32[]{:S(2)}, u32[]{:S(2)}) collective-permute-start(bf16[6,192,384]{2,1,0:T(8,128)(2,1)S(1)} %collective-permute-done.5.refs_2_), channel_id=1, source_target_pairs={{0,16},{16,32},{32,48},{48,0},{1,17},{17,33},{33,49},{49,1},{2,18}... | collective-permute-start | bytes 2654216 | tf_op jit(solution)/shard_map/ppermute | solution.py:22
  93.0 23.6 %collective-permute-start.18 = (bf16[6,192,384]{2,1,0:T(8,128)(2,1)}, bf16[6,192,384]{2,1,0:T(8,128)(2,1)}, u32[]{:S(2)}, u32[]{:S(2)}) collective-permute-start(bf16[6,192,384]{2,1,0:T(8,128)(2,1)} %collective-permute-done.7.refs_5_), channel_id=1, source_target_pairs={{0,8},{8,0},{1,9},{9,1},{2,10},{10,2},{3,11},{11,3},{4,12},{12,4},... | collective-permute-start | bytes 2654216 | tf_op jit(solution)/shard_map/ppermute | solution.py:22
  95.1 5.2 %copy-start.6 = (bf16[6,192,384]{2,1,0:T(8,128)(2,1)}, bf16[6,192,384]{2,1,0:T(8,128)(2,1)S(1)}, u32[]{:S(2)}) copy-start(bf16[6,192,384]{2,1,0:T(8,128)(2,1)S(1)} %collective-permute-done.15.refs_9_) | copy-start | bytes 2654212
  95.1 21.6 %collective-permute-start.19 = (bf16[6,192,384]{2,1,0:T(8,128)(2,1)}, bf16[6,192,384]{2,1,0:T(8,128)(2,1)}, u32[]{:S(2)}, u32[]{:S(2)}) collective-permute-start(bf16[6,192,384]{2,1,0:T(8,128)(2,1)} %collective-permute-done.10.refs_6_), channel_id=1, source_target_pairs={{0,8},{8,0},{1,9},{9,1},{2,10},{10,2},{3,11},{11,3},{4,12},{12,4},... | collective-permute-start | bytes 2654216 | tf_op jit(solution)/shard_map/ppermute | solution.py:22
  97.1 19.6 %collective-permute-start.20 = (bf16[6,192,384]{2,1,0:T(8,128)(2,1)}, bf16[6,192,384]{2,1,0:T(8,128)(2,1)}, u32[]{:S(2)}, u32[]{:S(2)}) collective-permute-start(bf16[6,192,384]{2,1,0:T(8,128)(2,1)} %collective-permute-done.11.refs_7_), channel_id=1, source_target_pairs={{0,8},{8,0},{1,9},{9,1},{2,10},{10,2},{3,11},{11,3},{4,12},{12,4},... | collective-permute-start | bytes 2654216 | tf_op jit(solution)/shard_map/ppermute | solution.py:22
  97.6 26.7 %collective-permute-start.14 = (bf16[6,192,384]{2,1,0:T(8,128)(2,1)}, bf16[6,192,384]{2,1,0:T(8,128)(2,1)}, u32[]{:S(2)}, u32[]{:S(2)}) collective-permute-start(bf16[6,192,384]{2,1,0:T(8,128)(2,1)} %collective-permute-done.11.refs_7_), channel_id=1, source_target_pairs={{0,48},{16,0},{32,16},{48,32},{1,49},{17,1},{33,17},{49,33},{2,50}... | collective-permute-start | bytes 2654216 | tf_op jit(solution)/shard_map/ppermute | solution.py:22
  100.3 16.4 %all-to-all-start.2 = ((bf16[8,128,384]{2,1,0:T(8,128)(2,1)}), bf16[8,128,384]{2,1,0:T(8,128)(2,1)S(1)}, u32[]{:S(2)}, u32[]{:S(2)}) async-start(bf16[8,128,384]{2,1,0:T(8,128)(2,1)} %broadcast_in_dim.5), calls=%async_computation.2 | async-start | bytes 1572864 | tf_op jit(solution)/shard_map/all_to_all | solution.py:32
  109.3 15.6 %copy-start.31 = (s32[128]{0:T(128)S(1)}, s32[128]{0:T(128)}, u32[]{:S(2)}) copy-start(s32[128]{0:T(128)} %param.31) | copy-start | bytes 1540
  109.3 15.7 %copy-start.29 = (f32[128]{0:T(128)S(1)}, f32[128]{0:T(128)}, u32[]{:S(2)}) copy-start(f32[128]{0:T(128)} %param.26) | copy-start | bytes 1540
  109.3 15.7 %copy-start.30 = (f32[128]{0:T(128)S(1)}, f32[128]{0:T(128)}, u32[]{:S(2)}) copy-start(f32[128]{0:T(128)} %param.25) | copy-start | bytes 1540
  116.5 11.9 %copy-start.19 = (f32[4,3072]{1,0:T(4,128)S(1)}, f32[4,3072]{1,0:T(4,128)}, u32[]{:S(2)}) copy-start(f32[4,3072]{1,0:T(4,128)} %mod_ref.3) | copy-start | bytes 147460
  124.4 2.8 %collective-permute-start.21 = (bf16[6,192,384]{2,1,0:T(8,128)(2,1)}, bf16[6,192,384]{2,1,0:T(8,128)(2,1)}, u32[]{:S(2)}, u32[]{:S(2)}) collective-permute-start(bf16[6,192,384]{2,1,0:T(8,128)(2,1)} %collective-permute-done.13.refs_4_), channel_id=1, source_target_pairs={{0,8},{8,0},{1,9},{9,1},{2,10},{10,2},{3,11},{11,3},{4,12},{12,4},... | collective-permute-start | bytes 2654216 | tf_op jit(solution)/shard_map/ppermute | solution.py:22
  124.4 4.0 %collective-permute-start.22 = (bf16[6,192,384]{2,1,0:T(8,128)(2,1)}, bf16[6,192,384]{2,1,0:T(8,128)(2,1)}, u32[]{:S(2)}, u32[]{:S(2)}) collective-permute-start(bf16[6,192,384]{2,1,0:T(8,128)(2,1)} %collective-permute-done.14.refs_8_), channel_id=1, source_target_pairs={{0,8},{8,0},{1,9},{9,1},{2,10},{10,2},{3,11},{11,3},{4,12},{12,4},... | collective-permute-start | bytes 2654216 | tf_op jit(solution)/shard_map/ppermute | solution.py:22
  125.0 3.4 %copy-start.7 = (bf16[6,192,384]{2,1,0:T(8,128)(2,1)S(1)}, bf16[6,192,384]{2,1,0:T(8,128)(2,1)}, u32[]{:S(2)}) copy-start(bf16[6,192,384]{2,1,0:T(8,128)(2,1)} %copy-done.6) | copy-start | bytes 2654212
  140.2 5.0 %collective-permute-start.24 = (bf16[640,384]{1,0:T(8,128)(2,1)S(1)}, bf16[640,384]{1,0:T(8,128)(2,1)S(1)}, u32[]{:S(2)}, u32[]{:S(2)}) collective-permute-start(bf16[640,384]{1,0:T(8,128)(2,1)S(1)} %get-tuple-element.124.refs_0_), channel_id=1, source_target_pairs={{0,8},{8,0},{1,9},{9,1},{2,10},{10,2},{3,11},{11,3},{4,12},{12,4},... | collective-permute-start | bytes 1474568 | tf_op jit(solution)/shard_map/ppermute | solution.py:22
  140.5 17.9 %collective-permute-start.23 = (bf16[640,384]{1,0:T(8,128)(2,1)S(1)}, bf16[640,384]{1,0:T(8,128)(2,1)S(1)}, u32[]{:S(2)}, u32[]{:S(2)}) collective-permute-start(bf16[640,384]{1,0:T(8,128)(2,1)S(1)} %get-tuple-element.124.refs_0_), channel_id=1, source_target_pairs={{0,64},{64,0},{1,65},{65,1},{2,66},{66,2},{3,67},{67,3},{4,68},{68... | collective-permute-start | bytes 1474568 | tf_op jit(solution)/shard_map/ppermute | solution.py:22
  142.0 29.4 %collective-permute-start.26 = (bf16[2,640,384]{2,1,0:T(8,128)(2,1)S(1)}, bf16[2,640,384]{2,1,0:T(8,128)(2,1)S(1)}, u32[]{:S(2)}, u32[]{:S(2)}) collective-permute-start(bf16[2,640,384]{2,1,0:T(8,128)(2,1)S(1)} %get-tuple-element.125.refs_2_.refs_3_), channel_id=1, source_target_pairs={{0,16},{16,32},{32,48},{48,0},{1,17},{17,33},{33,49},{49,1},{2,18}... | collective-permute-start | bytes 2949128 | tf_op jit(solution)/shard_map/ppermute | solution.py:22
  142.1 29.4 %collective-permute-start.27 = (bf16[2,640,384]{2,1,0:T(8,128)(2,1)S(1)}, bf16[2,640,384]{2,1,0:T(8,128)(2,1)S(1)}, u32[]{:S(2)}, u32[]{:S(2)}) collective-permute-start(bf16[2,640,384]{2,1,0:T(8,128)(2,1)S(1)} %get-tuple-element.125.refs_2_.refs_3_), channel_id=1, source_target_pairs={{0,48},{16,0},{32,16},{48,32},{1,49},{17,1},{33,17},{49,33},{2,50}... | collective-permute-start | bytes 2949128 | tf_op jit(solution)/shard_map/ppermute | solution.py:22
  158.4 1.9 collective-permute-start.25
  171.5 14.0 %collective-permute-start.28 = (bf16[640,384]{1,0:T(8,128)(2,1)S(1)}, bf16[640,384]{1,0:T(8,128)(2,1)S(1)}, u32[]{:S(2)}, u32[]{:S(2)}) collective-permute-start(bf16[640,384]{1,0:T(8,128)(2,1)S(1)} %slice_bitcast_fusion.1), channel_id=1, source_target_pairs={{0,16},{16,32},{32,48},{48,0},{1,17},{17,33},{33,49},{49,1},{2,18}... | collective-permute-start | bytes 1474568 | tf_op jit(solution)/shard_map/ppermute | solution.py:22
  172.4 13.1 %collective-permute-start.29 = (bf16[640,384]{1,0:T(8,128)(2,1)S(1)}, bf16[640,384]{1,0:T(8,128)(2,1)S(1)}, u32[]{:S(2)}, u32[]{:S(2)}) collective-permute-start(bf16[640,384]{1,0:T(8,128)(2,1)S(1)} %slice_bitcast_fusion), channel_id=1, source_target_pairs={{0,48},{16,0},{32,16},{48,32},{1,49},{17,1},{33,17},{49,33},{2,50}... | collective-permute-start | bytes 1474568 | tf_op jit(solution)/shard_map/ppermute | solution.py:22
  190.4 3.2 %collective-permute-start.30 = (f32[640,384]{1,0:T(8,128)S(1)}, f32[640,384]{1,0:T(8,128)S(1)}, u32[]{:S(2)}, u32[]{:S(2)}) collective-permute-start(f32[640,384]{1,0:T(8,128)S(1)} %get-tuple-element.152), channel_id=1, source_target_pairs={{0,8},{8,0},{1,9},{9,1},{2,10},{10,2},{3,11},{11,3},{4,12},{12,4},... | collective-permute-start | bytes 2949128 | tf_op jit(solution)/shard_map/ppermute | solution.py:22
  190.5 3.0 %collective-permute-start.31 = (f32[640,128]{1,0:T(8,128)S(1)}, f32[640,128]{1,0:T(8,128)S(1)}, u32[]{:S(2)}, u32[]{:S(2)}) collective-permute-start(f32[640,128]{1,0:T(8,128)S(1)} %get-tuple-element.154), channel_id=1, source_target_pairs={{0,8},{8,0},{1,9},{9,1},{2,10},{10,2},{3,11},{11,3},{4,12},{12,4},... | collective-permute-start | bytes 983048 | tf_op jit(solution)/shard_map/ppermute | solution.py:22
  193.9 18.4 %collective-permute-start.32 = (bf16[640,512]{1,0:T(8,128)(2,1)S(1)}, bf16[640,512]{1,0:T(8,128)(2,1)S(1)}, u32[]{:S(2)}, u32[]{:S(2)}) collective-permute-start(bf16[640,512]{1,0:T(8,128)(2,1)S(1)} %pad_maximum_fusion), channel_id=1, source_target_pairs={{0,64},{64,0},{1,65},{65,1},{2,66},{66,2},{3,67},{67,3},{4,68},{68... | collective-permute-start | bytes 1966088 | tf_op jit(solution)/shard_map/ppermute | solution.py:22
  212.2 3.0 %collective-permute-start.33 = (f32[640,384]{1,0:T(8,128)S(1)}, f32[640,384]{1,0:T(8,128)S(1)}, u32[]{:S(2)}, u32[]{:S(2)}) collective-permute-start(f32[640,384]{1,0:T(8,128)S(1)} %get-tuple-element.169), channel_id=1, source_target_pairs={{0,8},{8,0},{1,9},{9,1},{2,10},{10,2},{3,11},{11,3},{4,12},{12,4},... | collective-permute-start | bytes 2949128 | tf_op jit(solution)/shard_map/ppermute | solution.py:22
  212.2 3.0 %collective-permute-start.34 = (f32[640,128]{1,0:T(8,128)S(1)}, f32[640,128]{1,0:T(8,128)S(1)}, u32[]{:S(2)}, u32[]{:S(2)}) collective-permute-start(f32[640,128]{1,0:T(8,128)S(1)} %get-tuple-element.172), channel_id=1, source_target_pairs={{0,8},{8,0},{1,9},{9,1},{2,10},{10,2},{3,11},{11,3},{4,12},{12,4},... | collective-permute-start | bytes 983048 | tf_op jit(solution)/shard_map/ppermute | solution.py:22
  215.8 13.3 %collective-permute-start.35 = (bf16[640,384]{1,0:T(8,128)(2,1)S(1)}, bf16[640,384]{1,0:T(8,128)(2,1)S(1)}, u32[]{:S(2)}, u32[]{:S(2)}) collective-permute-start(bf16[640,384]{1,0:T(8,128)(2,1)S(1)} %combine.1.own_ref), channel_id=1, source_target_pairs={{0,1},{1,0},{2,3},{3,2},{4,5},{5,4},{6,7},{7,6},{8,9},{9,8},{10,11... | collective-permute-start | bytes 1474568 | tf_op jit(solution)/shard_map/ppermute | solution.py:22
  229.2 2.3 copy-start.3
  235.4 29.2 %all-to-all-start.3 = ((bf16[4,640,384]{2,1,0:T(8,128)(2,1)}), bf16[4,640,384]{2,1,0:T(8,128)(2,1)}, u32[]{:S(2)}, u32[]{:S(2)}) async-start(bf16[4,640,384]{2,1,0:T(8,128)(2,1)} %out_projection.1), calls=%async_computation.3 | async-start | bytes 3932160 | tf_op jit(solution)/shard_map/all_to_all | solution.py:464
  239.9 26.7 %copy-start.21 = (bf16[512,384]{1,0:T(8,128)(2,1)S(1)}, bf16[512,384]{1,0:T(8,128)(2,1)}, u32[]{:S(2)}) copy-start(bf16[512,384]{1,0:T(8,128)(2,1)} %param.32) | copy-start | bytes 1179652
  240.1 27.4 %copy-start.27 = (bf16[128,384]{1,0:T(8,128)(2,1)S(1)}, bf16[128,384]{1,0:T(8,128)(2,1)}, u32[]{:S(2)}) copy-start(bf16[128,384]{1,0:T(8,128)(2,1)} %param.33) | copy-start | bytes 294916
  264.6 3.6 %copy-start.1 = (bf16[128,1280]{1,0:T(8,128)(2,1)S(1)}, bf16[128,1280]{1,0:T(8,128)(2,1)}, u32[]{:S(2)}) copy-start(bf16[128,1280]{1,0:T(8,128)(2,1)} %param.17) | copy-start | bytes 983044
  (9 other events, 9.0 us)
Sparse Core Ops, SparseCore 0:
  93.1 71.3 all-gather.2
